TPU v7x, 32 devices: a whole 2x2x4 slice. The times are simulated.
32 devices in a mesh: ctx: 4 (over z), fsdp: 8 (over y, x, core).
Axes of the slice: x: 2, y: 2, z: 4, core: 2. Of those that a mesh axis runs over, the one named last changes fastest.
Arguments:
- block_input: bfloat16 [2, 8, 512, 1792], P(None, 'fsdp', 'ctx'), may hold values from -6 to 6
- lengths: int32 [2, 8], P(None, 'fsdp'), may hold values from 128 to 512, as said below
- cotangent: bfloat16 [2, 8, 512, 1792], P(None, 'fsdp', 'ctx'), may hold values from -6 to 6
- gain_attn: bfloat16 [1792], P('fsdp'), may hold values from 0.099609375 to 1.8984375
- conv_taps: bfloat16 [3, 1792], P(None, 'fsdp'), may hold values from -3 to 3
- w_query: bfloat16 [1792, 256], P('fsdp'), may hold values from -0.25 to 0.25
- w_key: bfloat16 [1792, 256], P('fsdp'), may hold values from -0.25 to 0.25
- w_value: bfloat16 [1792, 1792], P('fsdp'), may hold values from -0.125 to 0.125
- w_out: bfloat16 [1792, 1792], P('fsdp'), may hold values from -1 to 1
- gain_ffn: bfloat16 [1792], P('fsdp'), may hold values from 0.099609375 to 1.8984375
- w_gate: bfloat16 [1792, 4864], P('fsdp'), may hold values from -0.125 to 0.125
- w_up: bfloat16 [1792, 4864], P('fsdp'), may hold values from -0.125 to 0.125
- w_down: bfloat16 [4864, 1792], P('fsdp'), may hold values from -0.078125 to 0.078125
Outputs:
- output: bfloat16 [2, 8, 512, 1792], P(None, 'fsdp', 'ctx')
- grad_input: bfloat16 [2, 8, 512, 1792], P(None, 'fsdp', 'ctx')
- grad_gain_attn: float32 [1792], P('fsdp')
- grad_conv_taps: float32 [3, 1792], P(None, 'fsdp')
- grad_w_query: float32 [1792, 256], P('fsdp')
- grad_w_key: float32 [1792, 256], P('fsdp')
- grad_w_value: float32 [1792, 1792], P('fsdp')
- grad_w_out: float32 [1792, 1792], P('fsdp')
- grad_gain_ffn: float32 [1792], P('fsdp')
- grad_w_gate: float32 [1792, 4864], P('fsdp')
- grad_w_up: float32 [1792, 4864], P('fsdp')
- grad_w_down: float32 [4864, 1792], P('fsdp')
Inputs may be any that keep to these rules, and one draw needn't show every extreme that they name: `lengths`: for each of the 8 sequence columns, one micro-batch, drawn from the seed, has all 512 slots used.
All inputs are finite; a program needn't handle non-finite values.
Results may differ from a plain program's by a relative error of at most 0.012.
The roundings to bfloat16 on the way count: a program that leaves them out, or rounds other values in their place, can miss the bound.
Values may be sent and summed in bfloat16 or wider, within the bound.
No kernel may reach another device: no remote copies, remote signals or barrier semaphores. Data moves between devices by JAX's collectives and lax.ppermute only.
A program may use at most 384 MiB of HBM per device.

v0:
```python
import math

import jax
import jax.numpy as jnp
from jax import lax
from jax.sharding import PartitionSpec as P

HEADS = 16
FEAT = 16


epsilon = 1e-05
highest = lax.Precision.HIGHEST


def passed_along(value, axis, steps):
    count = lax.axis_size(axis)
    leading, last = (max(0, -steps), min(count, count - steps))
    return lax.ppermute(value, axis, [(source, source + steps) for source in range(leading, last)])


def entering(part, axis, combine, identity, reverse):
    count = lax.axis_size(axis)
    place = lax.axis_index(axis)
    ahead = count - 1 - place if reverse else place
    gathered = jax.tree.map(lambda a: lax.all_gather(a, axis), part)
    state = jax.tree.map(lambda a, e: jnp.zeros_like(a) + jnp.asarray(e, a.dtype), part, identity)

    def one(hop, state):
        source = count - 1 - hop if reverse else hop
        return combine(
            state, jax.tree.map(lambda a: lax.dynamic_index_in_dim(a, source, 0, False), gathered)
        )

    return lax.fori_loop(0, ahead, one, state)


def feature(values):
    width = values.shape[-1]
    outer = (values[..., :, None] * values[..., None, :]).reshape(
        values.shape[:-1] + (width * width,)
    )
    return jnp.concatenate(
        [
            jnp.ones_like(values[..., :1]),
            values / math.sqrt(math.sqrt(width)),
            outer / math.sqrt(2.0 * width),
        ],
        -1,
    )


def matmul(left, right):
    return jnp.dot(left, right, preferred_element_type=jnp.float32)


def left_contract(left, right):
    return jnp.einsum("ta,tb->ab", left, right, preferred_element_type=jnp.float32)


def right_contract(left, right):
    return jnp.einsum("ta,ba->tb", left, right, preferred_element_type=jnp.float32)


def add_pairs(earlier, later):
    return (earlier[0] + later[0], earlier[1] + later[1])


def accumulate(prior, index, value):
    return value if prior is None else prior[index] + value


def gather_weights(shards):
    return (
        lax.all_gather(shards[0], "fsdp", axis=0, tiled=True),
        lax.all_gather(shards[1], "fsdp", axis=1, tiled=True),
        lax.all_gather(shards[2], "fsdp", axis=0, tiled=True),
        lax.all_gather(shards[3], "fsdp", axis=0, tiled=True),
        lax.all_gather(shards[4], "fsdp", axis=0, tiled=True),
        lax.all_gather(shards[5], "fsdp", axis=0, tiled=True),
        lax.all_gather(shards[6], "fsdp", axis=0, tiled=True),
        lax.all_gather(shards[7], "fsdp", axis=0, tiled=True),
        lax.all_gather(shards[8], "fsdp", axis=0, tiled=True),
        lax.all_gather(shards[9], "fsdp", axis=0, tiled=True),
    )


def reduce_grads(grads):
    return (
        lax.psum_scatter(grads[0], "fsdp", scatter_dimension=0, tiled=True),
        lax.psum_scatter(grads[1], "fsdp", scatter_dimension=1, tiled=True),
        lax.psum_scatter(grads[2], "fsdp", scatter_dimension=0, tiled=True),
        lax.psum_scatter(grads[3], "fsdp", scatter_dimension=0, tiled=True),
        lax.psum_scatter(grads[4], "fsdp", scatter_dimension=0, tiled=True),
        lax.psum_scatter(grads[5], "fsdp", scatter_dimension=0, tiled=True),
        lax.psum_scatter(grads[6], "fsdp", scatter_dimension=0, tiled=True),
        lax.psum_scatter(grads[7], "fsdp", scatter_dimension=0, tiled=True),
        lax.psum_scatter(grads[8], "fsdp", scatter_dimension=0, tiled=True),
        lax.psum_scatter(grads[9], "fsdp", scatter_dimension=0, tiled=True),
    )


def finish_grads(shares):
    return lax.psum(
        (
            shares[0],
            shares[1],
            shares[2],
            shares[3],
            shares[4],
            shares[5],
            shares[6],
            shares[7],
            shares[8],
            shares[9],
        ),
        "ctx",
    )


def micro_pass(rows_in, length, cotan, weights, prior):
    gain_attn, conv_taps, w_query, w_key, w_value, w_out, gain_ffn, w_gate, w_up, w_down = weights
    group, width = rows_in.shape
    feat = FEAT
    heads = HEADS
    head_size = width // heads
    positions = lax.axis_index("ctx") * group + lax.iota(jnp.int32, group)
    keep = (positions < length).astype(jnp.float32)[:, None]
    previous = passed_along(rows_in[group - 2 :], "ctx", 1)
    extended = jnp.concatenate([previous, rows_in], 0).astype(jnp.float32)
    gain_one = gain_attn.astype(jnp.float32)
    taps = conv_taps.astype(jnp.float32)
    scale_ext = lax.rsqrt(jnp.mean(extended * extended, -1, keepdims=True) + epsilon)
    normed_ext = extended * scale_ext * gain_one
    normed = normed_ext[2:]
    conv_out = taps[0] * normed + taps[1] * normed_ext[1:-1] + taps[2] * normed_ext[:-2]
    sig_one = jax.nn.sigmoid(normed)
    gate_act = normed * sig_one
    gated = (conv_out * gate_act).astype(jnp.bfloat16)
    queries = matmul(gated, w_query).astype(jnp.bfloat16)
    keys = matmul(gated, w_key).astype(jnp.bfloat16)
    values = matmul(gated, w_value).astype(jnp.bfloat16)
    query_f = queries.astype(jnp.float32).reshape(group, heads, feat)
    key_f = keys.astype(jnp.float32).reshape(group, heads, feat)
    value_f = values.astype(jnp.float32).reshape(group, heads, head_size)
    lower = jnp.tril(jnp.ones((group, group), jnp.float32))
    scores = jnp.einsum("thf,shf->hts", query_f, key_f, precision=highest) / math.sqrt(feat)
    weights_att = (1.0 + scores + 0.5 * scores * scores) * lower
    numer_local = jnp.einsum("hts,shd->thd", weights_att, value_f, precision=highest)
    denom_local = jnp.sum(weights_att, -1).T
    query_feat, pull_query = jax.vjp(feature, query_f)
    key_feat, pull_key = jax.vjp(feature, key_f)
    phi_count = query_feat.shape[-1]
    state_local = jnp.einsum("thp,thd->phd", key_feat, value_f, precision=highest).reshape(
        phi_count, width
    )
    normal_local = jnp.sum(key_feat, 0)
    state_in, normal_in = entering(
        (state_local, normal_local),
        "ctx",
        add_pairs,
        (jnp.zeros_like(state_local), jnp.zeros_like(normal_local)),
        False,
    )
    state_three = state_in.reshape(phi_count, heads, head_size)
    numerator = numer_local + jnp.einsum("thp,phd->thd", query_feat, state_three, precision=highest)
    denominator = denom_local + jnp.einsum("thp,hp->th", query_feat, normal_in, precision=highest)
    attended = numerator / denominator[..., None]
    mixed = attended.reshape(group, width).astype(jnp.bfloat16)
    branch = matmul(mixed, w_out)
    residual_in = extended[2:]
    middle = residual_in + keep * branch
    scale_two = lax.rsqrt(jnp.mean(middle * middle, -1, keepdims=True) + epsilon)
    gain_two = gain_ffn.astype(jnp.float32)
    normed_two = (middle * scale_two * gain_two).astype(jnp.bfloat16)
    gate_pre = matmul(normed_two, w_gate)
    up_pre = matmul(normed_two, w_up)
    sig_two = jax.nn.sigmoid(gate_pre)
    gate_silu = gate_pre * sig_two
    hidden = (gate_silu * up_pre).astype(jnp.bfloat16)
    result = (middle + keep * matmul(hidden, w_down)).astype(jnp.bfloat16)
    grad_out = (cotan.astype(jnp.float32) * keep).astype(jnp.bfloat16)
    grad_down = accumulate(prior, 9, left_contract(hidden, grad_out))
    grad_hidden = right_contract(grad_out, w_down)
    grad_gate_pre = (grad_hidden * up_pre * sig_two * (1.0 + gate_pre * (1.0 - sig_two))).astype(
        jnp.bfloat16
    )
    grad_up_pre = (grad_hidden * gate_silu).astype(jnp.bfloat16)
    grad_gate = accumulate(prior, 7, left_contract(normed_two, grad_gate_pre))
    grad_up = accumulate(prior, 8, left_contract(normed_two, grad_up_pre))
    grad_normed_two = right_contract(grad_gate_pre, w_gate) + right_contract(grad_up_pre, w_up)
    grad_gain_two = accumulate(prior, 6, jnp.sum(grad_normed_two * middle * scale_two, 0))
    scaled_two = grad_normed_two * gain_two
    cube_two = scale_two * scale_two * scale_two
    grad_middle = (
        grad_out.astype(jnp.float32)
        + scale_two * scaled_two
        - middle * cube_two * jnp.mean(scaled_two * middle, -1, keepdims=True)
    )
    grad_branch = (keep * grad_middle).astype(jnp.bfloat16)
    grad_wout = accumulate(prior, 5, left_contract(mixed, grad_branch))
    grad_mixed = right_contract(grad_branch, w_out).astype(jnp.bfloat16)
    grad_att = grad_mixed.astype(jnp.float32).reshape(group, heads, head_size)
    grad_numer = grad_att / denominator[..., None]
    grad_denom = -jnp.sum(grad_att * attended, -1) / denominator
    grad_weights = (
        jnp.einsum("thd,shd->hts", grad_numer, value_f, precision=highest)
        + grad_denom.T[:, :, None]
    ) * lower
    grad_value = jnp.einsum("hts,thd->shd", weights_att, grad_numer, precision=highest)
    grad_scores = grad_weights * (1.0 + scores) / math.sqrt(feat)
    grad_query = jnp.einsum("hts,shf->thf", grad_scores, key_f, precision=highest)
    grad_key = jnp.einsum("hts,thf->shf", grad_scores, query_f, precision=highest)
    grad_query_feat = (
        jnp.einsum("thd,phd->thp", grad_numer, state_three, precision=highest)
        + grad_denom[:, :, None] * normal_in[None]
    )
    grad_state_in = jnp.einsum("thp,thd->phd", query_feat, grad_numer, precision=highest).reshape(
        phi_count, width
    )
    grad_normal_in = jnp.einsum("thp,th->hp", query_feat, grad_denom, precision=highest)
    grad_state_out, grad_normal_out = entering(
        (grad_state_in, grad_normal_in),
        "ctx",
        add_pairs,
        (jnp.zeros_like(grad_state_in), jnp.zeros_like(grad_normal_in)),
        True,
    )
    state_back = grad_state_out.reshape(phi_count, heads, head_size)
    grad_key_feat = (
        jnp.einsum("phd,thd->thp", state_back, value_f, precision=highest) + grad_normal_out[None]
    )
    grad_value = grad_value + jnp.einsum("thp,phd->thd", key_feat, state_back, precision=highest)
    grad_query = grad_query + pull_query(grad_query_feat)[0]
    grad_key = grad_key + pull_key(grad_key_feat)[0]
    query_back = grad_query.reshape(group, heads * feat).astype(jnp.bfloat16)
    key_back = grad_key.reshape(group, heads * feat).astype(jnp.bfloat16)
    value_back = grad_value.reshape(group, width).astype(jnp.bfloat16)
    grad_wquery = accumulate(prior, 2, left_contract(gated, query_back))
    grad_wkey = accumulate(prior, 3, left_contract(gated, key_back))
    grad_wvalue = accumulate(prior, 4, left_contract(gated, value_back))
    grad_gated = (
        right_contract(query_back, w_query)
        + right_contract(key_back, w_key)
        + right_contract(value_back, w_value)
    )
    grad_conv = grad_gated * gate_act
    grad_normed = grad_gated * conv_out * sig_one * (1.0 + normed * (1.0 - sig_one))
    grad_taps = accumulate(
        prior,
        1,
        jnp.stack(
            [
                jnp.sum(grad_conv * normed, 0),
                jnp.sum(grad_conv * normed_ext[1:-1], 0),
                jnp.sum(grad_conv * normed_ext[:-2], 0),
            ]
        ),
    )
    grad_ext = (
        jnp.pad(taps[0] * grad_conv, ((2, 0), (0, 0)))
        + jnp.pad(taps[1] * grad_conv, ((1, 1), (0, 0)))
        + jnp.pad(taps[2] * grad_conv, ((0, 2), (0, 0)))
    )
    returned = passed_along(grad_ext[:2], "ctx", -1)
    grad_normed = grad_normed + grad_ext[2:] + jnp.pad(returned, ((group - 2, 0), (0, 0)))
    scale_own = scale_ext[2:]
    grad_gain_one = accumulate(prior, 0, jnp.sum(grad_normed * residual_in * scale_own, 0))
    scaled_one = grad_normed * gain_one
    cube_one = scale_own * scale_own * scale_own
    grad_rows = (
        grad_middle
        + scale_own * scaled_one
        - residual_in * cube_one * jnp.mean(scaled_one * residual_in, -1, keepdims=True)
    )
    grads = (
        grad_gain_one,
        grad_taps,
        grad_wquery,
        grad_wkey,
        grad_wvalue,
        grad_wout,
        grad_gain_two,
        grad_gate,
        grad_up,
        grad_down,
    )
    return (result, grad_rows.astype(jnp.bfloat16), grads)


def local(
    block_input,
    lengths,
    cotangent,
    gain_attn,
    conv_taps,
    w_query,
    w_key,
    w_value,
    w_out,
    gain_ffn,
    w_gate,
    w_up,
    w_down,
):
    shards = (gain_attn, conv_taps, w_query, w_key, w_value, w_out, gain_ffn, w_gate, w_up, w_down)
    results = []
    grad_list = []
    totals = None
    shares = None
    weights = gather_weights(shards)
    for batch_index in range(block_input.shape[0]):
        prior = totals
        result, grad_rows, grads = micro_pass(
            block_input[batch_index, 0],
            lengths[batch_index, 0],
            cotangent[batch_index, 0],
            weights,
            prior,
        )
        results.append(result)
        grad_list.append(grad_rows)
        totals = grads
    shares = reduce_grads(totals)
    summed = finish_grads(shares)
    output = jnp.stack(results)[:, None]
    grad_input = jnp.stack(grad_list)[:, None]
    return (
        output,
        grad_input,
        summed[0],
        summed[1],
        summed[2],
        summed[3],
        summed[4],
        summed[5],
        summed[6],
        summed[7],
        summed[8],
        summed[9],
    )


def solution(mesh):
    in_specs = (
        P(None, "fsdp", "ctx", None),
        P(None, "fsdp"),
        P(None, "fsdp", "ctx", None),
        P("fsdp"),
        P(None, "fsdp"),
        P("fsdp", None),
        P("fsdp", None),
        P("fsdp", None),
        P("fsdp", None),
        P("fsdp"),
        P("fsdp", None),
        P("fsdp", None),
        P("fsdp", None),
    )
    out_specs = (
        P(None, "fsdp", "ctx", None),
        P(None, "fsdp", "ctx", None),
        P("fsdp"),
        P(None, "fsdp"),
        P("fsdp", None),
        P("fsdp", None),
        P("fsdp", None),
        P("fsdp", None),
        P("fsdp"),
        P("fsdp", None),
        P("fsdp", None),
        P("fsdp", None),
    )
    return jax.shard_map(local, mesh=mesh, in_specs=in_specs, out_specs=out_specs, check_vma=False)
```

profile of v0, /device:TPU:0, one launch (start us, length us, event | category | flops | bytes accessed | tf_op | source)
XLA Modules:
  0.0 2660.9 jit_solution(7344938280633486474)
XLA Ops:
  40.8 14.1 all-reduce.15
  120.2 16.4 all-gather.1
  136.6 21.2 all-gather
  166.7 55.9 %all-gather.27.cloned.1.call-done = f32[4,273,1792]{2,1,0:T(8,128)} async-done(((f32[1,273,1792]{2,1,0:T(8,128)}), f32[4,273,1792]{2,1,0:T(8,128)}) %all-gather.27.cloned.1.call-update) | async-done | bytes 7827472 | tf_op jit(solution)/shard_map/all_gather | solution.py:26
  225.6 140.5 %all-gather.17.cloned.1.call-done = f32[4,273,1792]{2,1,0:T(8,128)} async-done(((f32[1,273,1792]{2,1,0:T(8,128)}), f32[4,273,1792]{2,1,0:T(8,128)}) %all-gather.17.cloned.1.call-update) | async-done | bytes 7827472 | tf_op jit(solution)/shard_map/all_gather | solution.py:26
  382.3 29.9 %all-gather.19.cloned.1.call-done = bf16[1792,1792]{1,0:T(8,128)(2,1)} async-done(((bf16[224,1792]{1,0:T(8,128)(2,1)}), bf16[1792,1792]{1,0:T(8,128)(2,1)}) %all-gather.19.cloned.1.call-update) | async-done | bytes 6422544 | tf_op jit(solution)/shard_map/all_gather | solution.py:80
  425.7 80.9 %all-gather.21.cloned.1.call-done = bf16[1792,4864]{1,0:T(8,128)(2,1)} async-done(((bf16[224,4864]{1,0:T(8,128)(2,1)}), bf16[1792,4864]{1,0:T(8,128)(2,1)}) %all-gather.21.cloned.1.call-update) | async-done | bytes 17432592 | tf_op jit(solution)/shard_map/all_gather | solution.py:82
  516.5 84.5 %all-gather.23.cloned.1.call-done = bf16[1792,4864]{1,0:T(8,128)(2,1)} async-done(((bf16[224,4864]{1,0:T(8,128)(2,1)}), bf16[1792,4864]{1,0:T(8,128)(2,1)}) %all-gather.23.cloned.1.call-update) | async-done | bytes 17432592 | tf_op jit(solution)/shard_map/all_gather | solution.py:83
  610.9 84.7 %all-gather.25.cloned.1.call-done = bf16[4864,1792]{1,0:T(8,128)(2,1)} async-done(((bf16[608,1792]{1,0:T(8,128)(2,1)}), bf16[4864,1792]{1,0:T(8,128)(2,1)}) %all-gather.25.cloned.1.call-update) | async-done | bytes 17432592 | tf_op jit(solution)/shard_map/all_gather | solution.py:84
  838.7 16.6 all-gather.3
  855.3 18.0 all-gather.2
  894.0 64.1 %all-gather.31.cloned.1.call-done = f32[4,273,1792]{2,1,0:T(8,128)} async-done(((f32[1,273,1792]{2,1,0:T(8,128)}), f32[4,273,1792]{2,1,0:T(8,128)}) %all-gather.31.cloned.1.call-update) | async-done | bytes 7827472 | tf_op jit(solution)/shard_map/all_gather | solution.py:26
  969.7 132.1 %all-gather.29.cloned.1.call-done = f32[4,273,1792]{2,1,0:T(8,128)} async-done(((f32[1,273,1792]{2,1,0:T(8,128)}), f32[4,273,1792]{2,1,0:T(8,128)}) %all-gather.29.cloned.1.call-update) | async-done | bytes 7827472 | tf_op jit(solution)/shard_map/all_gather | solution.py:26
  1180.3 28.6 %convolution_add_fusion.1 = f32[1792,4864]{1,0:T(8,128)} fusion(f32[1792,4864]{1,0:T(8,128)} %fusion.139, bf16[128,1792]{1,0:T(8,128)(2,1)S(1)} %copy-done.41, bf16[128,4864]{1,0:T(8,128)(2,1)S(1)} %copy-done.54), kind=kOutput, calls=%fused_computation.9 | convolution fusion | flops 2240086016 | bytes 71434240 | tf_op jit(solution)/shard_map/ta,tb->ab/dot_general | solution.py:58
  1210.3 14.5 fusion.140
  1224.8 26.5 convolution_add_fusion
  1252.9 14.7 fusion.108
  1267.6 26.3 convolution_add_fusion.2
  1312.0 69.5 %reduce-scatter.15.cloned.1.call-done = f32[224,1792]{1,0:T(8,128)} async-done(((f32[1792,1792]{1,0:T(8,128)}), f32[224,1792]{1,0:T(8,128)}) %reduce-scatter.15.cloned.1.call-update) | async-done | bytes 1605648 | tf_op jit(solution)/shard_map/reduce_scatter | solution.py:94
  1381.5 215.3 %reduce-scatter.19.cloned.1.call-done = f32[224,4864]{1,0:T(8,128)} async-done(((f32[1792,4864]{1,0:T(8,128)}), f32[224,4864]{1,0:T(8,128)}) %reduce-scatter.19.cloned.1.call-update) | async-done | bytes 4358160 | tf_op jit(solution)/shard_map/reduce_scatter | solution.py:97
  1596.8 215.7 %reduce-scatter.21.cloned.1.call-done = f32[224,4864]{1,0:T(8,128)} async-done(((f32[1792,4864]{1,0:T(8,128)}), f32[224,4864]{1,0:T(8,128)}) %reduce-scatter.21.cloned.1.call-update) | async-done | bytes 4358160 | tf_op jit(solution)/shard_map/reduce_scatter | solution.py:98
  1812.5 215.3 %reduce-scatter.23.cloned.1.call-done = f32[608,1792]{1,0:T(8,128)} async-done(((f32[4864,1792]{1,0:T(8,128)}), f32[608,1792]{1,0:T(8,128)}) %reduce-scatter.23.cloned.1.call-update) | async-done | bytes 4358160 | tf_op jit(solution)/shard_map/reduce_scatter | solution.py:99
  2059.5 22.4 all-reduce.12
  2100.8 537.6 %all-reduce.18.cloned.1.call-done = (f32[224,256]{1,0:T(8,128)}, f32[224,256]{1,0:T(8,128)}, f32[224,1792]{1,0:T(8,128)}, f32[224,1792]{1,0:T(8,128)}, f32[224,4...) async-done(((f32[224,256]{1,0:T(8,128)}, f32[224,256]{1,0:T(8,128)}, f32[224,1792]{1,0:T(8,128)}, f32[224,1792]{1,0:T(8,128)}, f32[224,4864]{1,0:T(8,128)}, ...) | async-done | bytes 16744464 | tf_op jit(solution)/shard_map/psum | solution.py:104
  (606 shorter events, 514.1 us)
Async XLA Ops:
  7.2 55.4 %all-gather.15.cloned.1.call-start = ((), (), s32[]{:S(2)}) async-start(), calls=%async_computation.8 | async-start | bytes 7225344 | tf_op jit(solution)/shard_map/all_gather | solution.py:79
  8.0 214.6 %all-gather.27.cloned.1.call-start = ((), (), s32[]{:S(2)}) async-start(), calls=%async_computation.14 | async-start | bytes 10035200 | tf_op jit(solution)/shard_map/all_gather | solution.py:26
  8.8 46.2 %collective-permute-start = (bf16[2,1792]{1,0:T(2,128)(2,1)S(1)}, bf16[2,1792]{1,0:T(2,128)(2,1)S(1)}, u32[]{:S(2)}, u32[]{:S(2)}) collective-permute-start(bf16[2,1792]{1,0:T(2,128)(2,1)S(1)} %get-tuple-element.411), channel_id=1, source_target_pairs={{0,8},{8,16},{16,24},{1,9},{9,17},{17,25},{2,10},{10,18},{18,26},{... | collective-permute-start | bytes 21512 | tf_op jit(solution)/shard_map/ppermute | solution.py:19
  13.7 41.5 %collective-permute-start.1 = (bf16[2,1792]{1,0:T(2,128)(2,1)S(1)}, bf16[2,1792]{1,0:T(2,128)(2,1)S(1)}, u32[]{:S(2)}, u32[]{:S(2)}) collective-permute-start(bf16[2,1792]{1,0:T(2,128)(2,1)S(1)} %get-tuple-element.412), channel_id=1, source_target_pairs={{0,8},{8,16},{16,24},{1,9},{9,17},{17,25},{2,10},{10,18},{18,26},{... | collective-permute-start | bytes 21512 | tf_op jit(solution)/shard_map/ppermute | solution.py:19
  75.7 290.5 %all-gather.17.cloned.1.call-start = ((), (), s32[]{:S(2)}) async-start(), calls=%async_computation.9 | async-start | bytes 10035200 | tf_op jit(solution)/shard_map/all_gather | solution.py:26
  93.4 318.9 %all-gather.19.cloned.1.call-start = ((), (), s32[]{:S(2)}) async-start(), calls=%async_computation.10 | async-start | bytes 7225344 | tf_op jit(solution)/shard_map/all_gather | solution.py:80
  94.0 412.7 %all-gather.21.cloned.1.call-start = ((), (), s32[]{:S(2)}) async-start(), calls=%async_computation.11 | async-start | bytes 19611648 | tf_op jit(solution)/shard_map/all_gather | solution.py:82
  94.6 506.5 %all-gather.23.cloned.1.call-start = ((), (), s32[]{:S(2)}) async-start(), calls=%async_computation.12 | async-start | bytes 19611648 | tf_op jit(solution)/shard_map/all_gather | solution.py:83
  95.1 600.4 %all-gather.25.cloned.1.call-start = ((), (), s32[]{:S(2)}) async-start(), calls=%async_computation.13 | async-start | bytes 19611648 | tf_op jit(solution)/shard_map/all_gather | solution.py:84
  95.9 862.2 %all-gather.31.cloned.1.call-start = ((), (), s32[]{:S(2)}) async-start(), calls=%async_computation.16 | async-start | bytes 10035200 | tf_op jit(solution)/shard_map/all_gather | solution.py:26
  416.8 372.3 %copy-start.6 = (f32[128,1792]{1,0:T(8,128)}, f32[128,1792]{1,0:T(8,128)S(1)}, u32[]{:S(2)}) copy-start(f32[128,1792]{1,0:T(8,128)S(1)} %get-tuple-element.442) | copy-start | bytes 2752516
  425.5 363.6 %copy-start.8 = (f32[128,1792]{1,0:T(8,128)}, f32[128,1792]{1,0:T(8,128)S(1)}, u32[]{:S(2)}) copy-start(f32[128,1792]{1,0:T(8,128)S(1)} %get-tuple-element.444) | copy-start | bytes 2752516
  811.2 290.6 %all-gather.29.cloned.1.call-start = ((), (), s32[]{:S(2)}) async-start(), calls=%async_computation.15 | async-start | bytes 10035200 | tf_op jit(solution)/shard_map/all_gather | solution.py:26
  830.5 481.4 %reduce-scatter.11.cloned.1.call-start = ((), (), s32[]{:S(2)}) async-start(), calls=%async_computation.17 | async-start | bytes 2064384 | tf_op jit(solution)/shard_map/reduce_scatter | solution.py:92
  894.0 418.0 %reduce-scatter.13.cloned.1.call-start = ((), (), s32[]{:S(2)}) async-start(), calls=%async_computation.18 | async-start | bytes 2064384 | tf_op jit(solution)/shard_map/reduce_scatter | solution.py:93
  1128.2 183.8 %reduce-scatter.17.cloned.1.call-start = ((), (), s32[]{:S(2)}) async-start(), calls=%async_computation.20 | async-start | bytes 14450688 | tf_op jit(solution)/shard_map/reduce_scatter | solution.py:95
  1136.7 244.8 %reduce-scatter.15.cloned.1.call-start = ((), (), s32[]{:S(2)}) async-start(), calls=%async_computation.19 | async-start | bytes 14450688 | tf_op jit(solution)/shard_map/reduce_scatter | solution.py:94
  1165.2 431.6 %reduce-scatter.19.cloned.1.call-start = ((), (), s32[]{:S(2)}) async-start(), calls=%async_computation.21 | async-start | bytes 39223296 | tf_op jit(solution)/shard_map/reduce_scatter | solution.py:97
  1209.0 603.5 %reduce-scatter.21.cloned.1.call-start = ((), (), s32[]{:S(2)}) async-start(), calls=%async_computation.22 | async-start | bytes 39223296 | tf_op jit(solution)/shard_map/reduce_scatter | solution.py:98
  1251.3 776.4 %reduce-scatter.23.cloned.1.call-start = ((), (), s32[]{:S(2)}) async-start(), calls=%async_computation.23 | async-start | bytes 39223296 | tf_op jit(solution)/shard_map/reduce_scatter | solution.py:99
  1293.9 792.1 %reduce-scatter.25.cloned.1.call-start = ((), (), s32[]{:S(2)}) async-start(), calls=%async_computation.24 | async-start | bytes 1032192
  1311.9 1326.5 %all-reduce.18.cloned.1.call-start = ((), (), s32[]{:S(2)}) async-start(), calls=%async_computation.25 | async-start | bytes 33488896 | tf_op jit(solution)/shard_map/psum | solution.py:104
  2049.1 5.6 collective-permute-start.2
  2050.5 6.2 collective-permute-start.3
  (171 other events, 1953.1 us)
Sparse Core Ops, SparseCore 0:
  9.9 52.5 all-gather.14
  75.8 146.7 all-gather.26
  224.1 141.9 all-gather.16
  367.9 44.2 all-gather.18
  414.0 92.6 all-gather.20
  508.4 92.6 all-gather.22
  602.9 92.6 all-gather.24
  811.3 146.8 all-gather.30
  959.7 141.9 all-gather.28
  1105.5 37.8 reduce-scatter.10
  1146.8 39.6 reduce-scatter.12
  1189.9 93.7 reduce-scatter.16
  1287.7 93.7 reduce-scatter.14
  1385.0 211.7 reduce-scatter.18
  1600.7 211.7 reduce-scatter.20
  1816.0 211.7 reduce-scatter.22
  2031.1 35.4 reduce-scatter.24
  2070.4 567.9 all-reduce.17
where the time goes:
time: 2670 us; the launch traced here: 2660 us
  waiting for transfers between devices  1940 us (73%)
  matrix products  404 us (15%)
  blocking collectives  154 us (6%)
  local copies, waits for them, and re-layouts  81 us (3%)
  other arithmetic  53.8 us (2%)
    psum x1, waiting for transfers between devices, finish_grads(): lax.psum((shares[0], shares[1], shares[2], shares[3], shares[4], shares[5...  538 us
    all_gather x4, waiting for transfers between devices, entering(): gathered = jax.tree.map(lambda a: lax.all_gather(a, axis), part)  393 us
    reduce_scatter x1, waiting for transfers between devices, reduce_grads(): lax.psum_scatter(grads[8], 'fsdp', scatter_dimension=0, tiled=True)  216 us
    reduce_scatter x1, waiting for transfers between devices, reduce_grads(): lax.psum_scatter(grads[9], 'fsdp', scatter_dimension=0, tiled=True)  215 us
    reduce_scatter x1, waiting for transfers between devices, reduce_grads(): lax.psum_scatter(grads[7], 'fsdp', scatter_dimension=0, tiled=True)  215 us
    dot_general x14, matrix products, left_contract(): jnp.einsum('ta,tb->ab', left, right, preferred_element_type=jnp.float32)  145 us
    dot_general x14, matrix products, right_contract(): jnp.einsum('ta,ba->tb', left, right, preferred_element_type=jnp.float32)  103 us
    all_gather x1, waiting for transfers between devices, gather_weights(): lax.all_gather(shards[9], 'fsdp', axis=0, tiled=True)  84.7 us
  transfers between devices with their start and end apart: 22, of which 16 were waited for; matrix products, arithmetic and copies ran while one was open for 14% of the time, Pallas kernels for 0%

commit v1 on v0

v1 whole, which is shorter than its diff:
```python
import functools
import math

import jax
import jax.numpy as jnp
from jax import lax
from jax.experimental import pallas as pl
from jax.experimental.pallas import tpu as pltpu
from jax.sharding import PartitionSpec as P

HEADS = 16
FEAT = 16
PAIR = 2
FREE = pl.CostEstimate(flops=0, bytes_accessed=0, transcendentals=0)

epsilon = 1e-05
bf16 = jnp.bfloat16
f32 = jnp.float32


def dot(left, right, over):
    return lax.dot_general(left, right, (over, ((), ())), preferred_element_type=f32)


def matmul(left, right):
    return dot(left, right, ((1,), (0,)))


def left_contract(left, right):
    return dot(left, right, ((0,), (0,)))


def right_contract(left, right):
    return dot(left, right, ((1,), (1,)))


def along(value, steps):
    count = lax.axis_size("ctx")
    first, last = (max(0, -steps), min(count, count - steps))
    return lax.ppermute(value, "ctx", [(i, i + steps) for i in range(first, last)])


def rotate(value, steps):
    count = lax.axis_size("ctx")
    return lax.ppermute(value, "ctx", [(i, (i + steps) % count) for i in range(count)])


def across(value, mask):
    count = lax.axis_size("fsdp")
    return lax.ppermute(value, "fsdp", [(i, i ^ mask) for i in range(count)])


def diagonal(value):
    count = lax.axis_size("fsdp")
    return lax.ppermute(value, "fsdp", [(i, i ^ (2 if i & 1 else 4)) for i in range(count)])


def interleaved(own, other):
    return [part for pair in zip(own, other) for part in pair]


def swap(pieces):
    return [across(piece, 1) for piece in pieces]


def chip_exchange(pieces):
    return [across(p, PAIR * k) if k else p for k, p in enumerate(pieces)]


def total(pieces):
    return sum(p.astype(f32) for p in pieces[1:]) + pieces[0].astype(f32)


def join(*values):
    return list(lax.optimization_barrier(values))


def pick(stack, index):
    return lax.dynamic_index_in_dim(stack, index, 0, False)


def placed(pieces, indices):
    buffer = jnp.zeros((len(pieces),) + pieces[0].shape, pieces[0].dtype)
    for piece, index in zip(pieces, indices):
        buffer = lax.dynamic_update_index_in_dim(buffer, piece, index, 0)
    return buffer


def kernel_call(kernel, ids, arrays, outs, scratch=(), anywhere=()):
    whole = pl.BlockSpec(memory_space=pltpu.VMEM)
    specs = [pl.BlockSpec(memory_space=pltpu.SMEM)]
    anyplace = pl.BlockSpec(memory_space=pl.ANY)
    specs += [anyplace if i in anywhere else whole for i in range(len(arrays))]
    return pl.pallas_call(
        kernel,
        out_shape=list(outs),
        in_specs=specs,
        out_specs=[whole] * len(outs),
        scratch_shapes=list(scratch),
        compiler_params=pltpu.CompilerParams(vmem_limit_bytes=48 * 1024 * 1024),
        cost_estimate=FREE,
    )(ids, *arrays)


def fetch_rows(pieces, whole, sems, mine):
    size = pieces[0].shape[0]
    copies = []
    for m, piece in enumerate(pieces):
        start = pl.multiple_of((mine ^ m) * size, 16)
        copies.append(pltpu.make_async_copy(piece, whole.at[pl.ds(start, size)], sems.at[m]))
    for copy in copies:
        copy.start()
    return copies


def tiles(size, step):
    return [slice(at, min(at + step, size)) for at in range(0, size, step)]


def route(value, index, refs):
    for at, ref in enumerate(refs):

        @pl.when(index == at)
        def _(ref=ref):
            ref[...] = value


def ring_step(group, place, count):
    return lax.rem(group + count - place, count)


def project_kernel(count, shards, heads, ids, gated, *rest):
    pieces, outs = rest[:shards], rest[shards : shards + count]
    weight, projected, sems = rest[shards + count :]
    place, mine = ids[0], ids[1]
    for copy in fetch_rows(pieces, weight, sems, mine):
        copy.wait()
    width = weight.shape[1]
    for tile in tiles(width, 256):
        projected[:, tile] = matmul(gated[...], weight[:, tile]).astype(bf16)
    features = heads * FEAT
    all_features = features * count
    part = (width - 2 * all_features) // count
    for group in range(count):
        start = 2 * all_features + part * group
        value = jnp.concatenate(
            [
                projected[:, features * group : features * (group + 1)],
                projected[:, all_features + features * group : all_features + features * (group + 1)],
                projected[:, start : start + part],
            ],
            -1,
        )
        route(value, ring_step(group, place, count), outs)


def project_back_kernel(count, shards, heads, ids, *rest):
    ins, pieces = rest[:count], rest[count : count + shards]
    natural, grad = rest[count + shards : count + shards + 2]
    weight, grouped, sems = rest[count + shards + 2 :]
    place, mine = ids[0], ids[1]
    copies = fetch_rows(pieces, weight, sems, mine)
    features = heads * FEAT
    part = ins[0].shape[1] - 2 * features
    for step in range(count):
        grouped[lax.rem(place + step, count)] = ins[step][...]
    parts = [grouped[g, :, :features] for g in range(count)]
    parts += [grouped[g, :, features : 2 * features] for g in range(count)]
    parts += [grouped[g, :, 2 * features :] for g in range(count)]
    natural[...] = jnp.concatenate(parts, -1)
    for copy in copies:
        copy.wait()
    for tile in tiles(weight.shape[0], 256):
        grad[:, tile] = right_contract(natural[...], weight[tile])


def merge_kernel(count, ids, *rest):
    ins = rest[:count]
    weight, inputs, keep, gain, mixed, middle, normed, grouped, branch = rest[count:]
    place = ids[0]
    for step in range(count):
        grouped[lax.rem(place + step, count)] = ins[step][...]
    mixed[...] = jnp.concatenate([grouped[g] for g in range(count)], -1)
    for tile in tiles(weight.shape[1], 256):
        branch[:, tile] = matmul(mixed[...], weight[:, tile])

    @pl.loop(0, inputs.shape[0] // 16)
    def _(i):
        rows = pl.ds(pl.multiple_of(i * 16, 16), 16)
        value = inputs[rows].astype(f32) + keep[rows] * branch[rows]
        middle[rows] = value
        scale = lax.rsqrt(jnp.mean(value * value, -1, keepdims=True) + epsilon)
        normed[rows] = (value * scale * gain[...]).astype(bf16)


def norm_back_kernel(count, chips, ids, *rest):
    backs = rest[:chips]
    middle, grad_out, keep, gain, weight = rest[chips : chips + 5]
    grad_middle, grad_branch, grad_gain = rest[chips + 5 : chips + 8]
    outs = rest[chips + 8 :]
    place = ids[0]
    grad_gain[...] = jnp.zeros_like(grad_gain)

    @pl.loop(0, middle.shape[0] // 16)
    def _(i):
        rows = pl.ds(pl.multiple_of(i * 16, 16), 16)
        back = backs[0][rows].astype(f32)
        for ref in backs[1:]:
            back = back + ref[rows].astype(f32)
        value = middle[rows]
        scale = lax.rsqrt(jnp.mean(value * value, -1, keepdims=True) + epsilon)
        grad_gain[...] += jnp.sum(back * value * scale, 0, keepdims=True)
        scaled = back * gain[...]
        cube = scale * scale * scale
        grad = (
            grad_out[rows].astype(f32)
            + scale * scaled
            - value * (cube * jnp.mean(scaled * value, -1, keepdims=True))
        )
        grad_middle[rows] = grad
        grad_branch[rows] = (keep[rows] * grad).astype(bf16)

    part = weight.shape[0] // count
    for group in range(count):
        value = right_contract(grad_branch[...], weight[group * part : (group + 1) * part])
        route(value.astype(bf16), ring_step(group, place, count), outs)


def arrange_kernel(shards, ids, *rest):
    pieces, own_down, other_down = rest[:shards], rest[shards], rest[shards + 1]
    gate, up, down, sems = rest[shards + 2 :]
    mine = ids[1]
    size = pieces[0].shape[1]
    copies = []
    for m, piece in enumerate(pieces):
        rows = pl.ds(pl.multiple_of((mine ^ m) * size, 16), size)
        for half, out in enumerate((gate, up)):
            copies.append(pltpu.make_async_copy(piece.at[half], out.at[rows], sems.at[2 * m + half]))
    size = own_down.shape[0]
    core = lax.rem(mine, PAIR)
    for at, piece in enumerate((own_down, other_down)):
        rows = pl.ds(pl.multiple_of((core ^ at) * size, 16), size)
        copies.append(pltpu.make_async_copy(piece, down.at[rows], sems.at[2 * shards + at]))
    for copy in copies:
        copy.start()
    for copy in copies:
        copy.wait()


def pack_kernel(chips, ids, gate, up, out):
    chip = lax.div(ids[1], PAIR)
    part = gate.shape[1] // chips
    for q in range(chips):
        for half, ref in enumerate((gate, up)):
            out[q ^ chip, half] = ref[:, q * part : (q + 1) * part]


def ffn_kernel(chunks, ids, *rest):
    normed = jnp.concatenate([ref[...] for ref in rest[:chunks]], 0)
    grad_out = jnp.concatenate([ref[...] for ref in rest[chunks : 2 * chunks]], 0)
    gate_w, up_w, down_w = rest[2 * chunks : 2 * chunks + 3]
    outs = rest[2 * chunks + 3 : -2]
    gate_all, up_all = rest[-2:]
    size = normed.shape[0] // chunks

    def put(which, tile, value):
        for k in range(chunks):
            outs[4 * k + which][:, tile] = value[k * size : (k + 1) * size].astype(bf16)

    for tile in tiles(gate_w.shape[1], 256):
        gate_pre = matmul(normed, gate_w[:, tile])
        up_pre = matmul(normed, up_w[:, tile])
        grad_hidden = right_contract(grad_out, down_w[tile])
        sig = jax.nn.sigmoid(gate_pre)
        gate_silu = gate_pre * sig
        gate_back = grad_hidden * up_pre * sig * (1.0 + gate_pre * (1.0 - sig))
        gate_back, up_back = gate_back.astype(bf16), (grad_hidden * gate_silu).astype(bf16)
        gate_all[:, tile], up_all[:, tile] = gate_back, up_back
        put(0, tile, gate_silu * up_pre)
        put(1, tile, gate_back)
        put(2, tile, up_back)
    for tile in tiles(gate_w.shape[0], 256):
        value = right_contract(gate_all[...], gate_w[tile])
        put(3, tile, value + right_contract(up_all[...], up_w[tile]))


def down_kernel(chips, ids, *rest):
    hidden, weight, outs = rest[:chips], rest[chips], rest[chips + 1 :]
    for tile in tiles(weight.shape[1], 256):
        for source, out in zip(hidden, outs):
            out[:, tile] = matmul(source[...], weight[:, tile]).astype(bf16)


def finish_kernel(chips, ids, whole, gate, up):
    chip = lax.div(ids[1], PAIR)
    part = whole.shape[-1]
    for q in range(chips):
        for half, out in enumerate((gate, up)):
            out[:, q * part : (q + 1) * part] = whole[q ^ chip, half].astype(f32)


def weight_grad_kernel(blocks, groups, parts, ids, *rest):
    chunks = (len(rest) - 3) // (groups + 1)
    lefts, rights = rest[:chunks], rest[chunks:-3]
    keeps, sends, turned = rest[-3:]
    mine = lax.rem(ids[1], blocks)
    tokens, rows = lefts[0].shape
    size = rows // blocks
    step = size // parts

    @pl.when((pl.program_id(0) == 0) & (pl.program_id(1) == 0) & (pl.program_id(2) == 0))
    def _():
        for k, left in enumerate(lefts):
            for tile in tiles(rows, 128):
                turned[tile, k * tokens : (k + 1) * tokens] = left[:, tile].T

    for g in range(groups):

        @pl.when(pl.program_id(0) == g)
        def _(g=g):
            right = [part[...] for part in rights[g * chunks : (g + 1) * chunks]]
            right = jnp.concatenate(right, 0)
            for at, out in enumerate((keeps, sends)):
                block = mine ^ (PAIR * pl.program_id(1) + at)
                start = pl.multiple_of(block * size + pl.program_id(2) * step, 16)
                out[0, 0] = matmul(turned[pl.ds(start, step)], right).astype(bf16)


def weight_grad(ids, lefts, rights, blocks, parts=1):
    groups, chunks = len(rights), len(lefts)
    tokens, rows = lefts[0].shape
    columns = rights[0][0].shape[1]
    size = rows // blocks
    out = jax.ShapeDtypeStruct((blocks // PAIR, groups, size, columns), bf16)
    arrays = list(lefts) + [part for right in rights for part in right]
    block = pl.BlockSpec((1, 1, size // parts, columns), lambda g, k, j: (k, g, j, 0))
    return pl.pallas_call(
        functools.partial(weight_grad_kernel, blocks, groups, parts),
        out_shape=[out, out],
        grid=(groups, blocks // PAIR, parts),
        in_specs=[pl.BlockSpec(memory_space=pltpu.SMEM)]
        + [pl.BlockSpec(memory_space=pltpu.VMEM)] * len(arrays),
        out_specs=[block] * 2,
        scratch_shapes=[pltpu.VMEM((rows, chunks * tokens), bf16)],
        compiler_params=pltpu.CompilerParams(vmem_limit_bytes=48 * 1024 * 1024),
        cost_estimate=FREE,
    )(ids, *arrays)


def pack_call(ids, w_gate, w_up, chips):
    rows, columns = w_gate.shape
    out = jax.ShapeDtypeStruct((chips, 2, rows, columns // chips), bf16)
    return kernel_call(functools.partial(pack_kernel, chips), ids, [w_gate, w_up], [out])


def arrange(ids, pieces, own_down, other_down, width):
    shards = len(pieces)
    hidden_width = pieces[0].shape[-1]
    shape_of = jax.ShapeDtypeStruct
    anywhere = pl.BlockSpec(memory_space=pl.ANY)
    return pl.pallas_call(
        functools.partial(arrange_kernel, shards),
        out_shape=[shape_of((width, hidden_width), bf16)] * 2
        + [shape_of((PAIR * own_down.shape[0], width), bf16)],
        in_specs=[pl.BlockSpec(memory_space=pltpu.SMEM)] + [anywhere] * (shards + 2),
        out_specs=[pl.BlockSpec(memory_space=pltpu.VMEM)] * 3,
        scratch_shapes=[pltpu.SemaphoreType.DMA((2 * shards + 2,))],
        compiler_params=pltpu.CompilerParams(vmem_limit_bytes=48 * 1024 * 1024),
        cost_estimate=FREE,
    )(ids, *pieces, own_down, other_down)


def causal(place, count, group, block):
    row_block = lax.rem(place + (count - block), count)
    rows = row_block * group + lax.broadcasted_iota(jnp.int32, (group, count * group), 0)
    column = lax.broadcasted_iota(jnp.int32, (group, count * group), 1)
    ordinal, inner = column // group, column % group
    columns = lax.rem(place + (count - ordinal), count) * group + inner
    return rows >= columns


def head_parts(refs, head, heads, head_size):
    features = heads * FEAT
    queries = [r[0][:, head * FEAT : (head + 1) * FEAT] * 0.25 for r in refs]
    keys = [r[0][:, features + head * FEAT : features + (head + 1) * FEAT] for r in refs]
    start = 2 * features + head * head_size
    values = [r[0][:, start : start + head_size] for r in refs]
    return queries, jnp.concatenate(keys, 0), jnp.concatenate(values, 0)


def attend_kernel(count, heads, head_size, place_ref, *refs):
    ins, outs = refs[:count], refs[count:]
    group = ins[0].shape[1]
    place = place_ref[0]
    masks = [causal(place, count, group, block) for block in range(count)]
    mixed = [[] for _ in range(count)]
    for head in range(heads):
        queries, keys, values = head_parts(ins, head, heads, head_size)
        for block in range(count):
            scores = right_contract(queries[block], keys)
            weights = jnp.where(masks[block], 1.0 + scores + 0.5 * scores * scores, 0.0)
            denominator = jnp.sum(weights, -1, keepdims=True)
            numerator = matmul(weights.astype(bf16), values)
            mixed[block].append((numerator / denominator).astype(bf16))
    for block in range(count):
        outs[block][0] = jnp.concatenate(mixed[block], -1)


def attend_back_kernel(count, heads, head_size, place_ref, *refs):
    ins, grads, outs = refs[:count], refs[count : 2 * count], refs[2 * count :]
    group = ins[0].shape[1]
    place = place_ref[0]
    masks = [causal(place, count, group, block) for block in range(count)]
    dqs = [[] for _ in range(count)]
    dks, dvs = [], []
    for head in range(heads):
        queries, keys, values = head_parts(ins, head, heads, head_size)
        key_back = value_back = 0.0
        for block in range(count):
            upstream = grads[block][0][:, head * head_size : (head + 1) * head_size]
            scores = right_contract(queries[block], keys)
            weights = jnp.where(masks[block], 1.0 + scores + 0.5 * scores * scores, 0.0)
            inverse = 1.0 / jnp.sum(weights, -1, keepdims=True)
            weights = weights * inverse
            inner = right_contract(upstream, values)
            shift = jnp.sum(weights * inner, -1, keepdims=True)
            score_back = (inner - shift) * inverse * (1.0 + scores)
            score_back = jnp.where(masks[block], score_back, 0.0).astype(bf16)
            dqs[block].append((0.25 * matmul(score_back, keys)).astype(bf16))
            key_back = key_back + left_contract(queries[block], score_back)
            value_back = value_back + left_contract(upstream, weights.astype(bf16))
        dks.append(key_back.T.astype(bf16))
        dvs.append(value_back.T.astype(bf16))
    for block in range(count):
        rows = slice(block * group, (block + 1) * group)
        parts = dqs[block] + [k[rows] for k in dks] + [v[rows] for v in dvs]
        outs[block][0] = jnp.concatenate(parts, -1)


def block_call(kernel, ids, arrays, out_width):
    count = lax.axis_size("ctx")
    batch, group, _ = arrays[0].shape
    spec = lambda a: pl.BlockSpec((1, group, a.shape[2]), lambda b: (b, 0, 0))
    out = jax.ShapeDtypeStruct((batch, group, out_width), bf16)
    return pl.pallas_call(
        kernel,
        out_shape=[out] * count,
        grid=(batch,),
        in_specs=[pl.BlockSpec(memory_space=pltpu.SMEM)] + [spec(a) for a in arrays],
        out_specs=[spec(out)] * count,
        compiler_params=pltpu.CompilerParams(vmem_limit_bytes=48 * 1024 * 1024),
        cost_estimate=FREE,
    )(ids, *arrays)


def local(
    block_input,
    lengths,
    cotangent,
    gain_attn,
    conv_taps,
    w_query,
    w_key,
    w_value,
    w_out,
    gain_ffn,
    w_gate,
    w_up,
    w_down,
):
    count = lax.axis_size("ctx")
    shards = lax.axis_size("fsdp")
    chips = shards // PAIR
    place = lax.axis_index("ctx")
    mine = lax.axis_index("fsdp")
    core, chip = mine % PAIR, mine // PAIR
    ids = jnp.stack([place, mine]).astype(jnp.int32)
    batch, _, group, width = block_input.shape
    rows = batch * group
    own_rows = w_query.shape[0]
    heads = HEADS // count
    head_size = width // HEADS
    mixed_width = heads * head_size
    qkv_width = 2 * heads * FEAT + mixed_width
    hidden_width = w_gate.shape[1] // chips
    part_rows = own_rows // count
    vmem = lambda shape, kind: pltpu.VMEM(shape, kind)
    shape_of = jax.ShapeDtypeStruct
    rotated = lambda pieces: [rotate(p, d) if d else p for d, p in enumerate(pieces)]
    returned = lambda pieces: [rotate(p, -d) if d else p for d, p in enumerate(pieces)]

    small = jnp.concatenate([gain_attn[None], gain_ffn[None], conv_taps], 0)
    small = jnp.pad(small, ((0, 3), (0, 0)))[None]
    mask = 1
    while mask < shards:
        small = jnp.concatenate([small, across(small, mask)], 0)
        mask *= 2
    small = placed([small[m] for m in range(shards)], [mine ^ m for m in range(shards)])
    small = jnp.transpose(small, (1, 0, 2)).reshape(8, width).astype(f32)
    gain_one, gain_two, taps = small[0], small[1], small[2:5]
    inputs = block_input[:, 0]
    previous = along(inputs[:, group - 2 :], 1)

    qkv_shard = jnp.concatenate([w_query, w_key, w_value], -1)
    total_width = qkv_shard.shape[1]
    if chips == 4:
        one, two = across(qkv_shard, 2), across(qkv_shard, 4)
        (packed,) = pack_call(ids, w_gate, w_up, chips)
        one, two, packed = join(one, two, packed)
        three = diagonal(jnp.where(core == 0, one, two))
        others = swap([qkv_shard, one, two])
        three, *others = join(three, *others)
        qkv_own, qkv_other = [qkv_shard, one, two, three], others + swap([three])
    else:
        (packed,) = pack_call(ids, w_gate, w_up, chips)
        qkv_own = join(*[across(qkv_shard, PAIR * k) if k else qkv_shard for k in range(chips)])
        qkv_other = swap(qkv_own)

    extended = jnp.concatenate([previous, inputs], 1).astype(f32)
    scale_ext = lax.rsqrt(jnp.mean(extended * extended, -1, keepdims=True) + epsilon)
    normed_ext = extended * scale_ext * gain_one
    normed = normed_ext[:, 2:]
    conv_out = taps[0] * normed + taps[1] * normed_ext[:, 1:-1] + taps[2] * normed_ext[:, :-2]
    sig_one = jax.nn.sigmoid(normed)
    gate_act = normed * sig_one
    gated = (conv_out * gate_act).astype(bf16).reshape(rows, width)
    positions = place * group + lax.iota(jnp.int32, group)
    keep = (positions[None] < lengths).astype(f32).reshape(rows, 1)
    grad_out = (cotangent[:, 0].astype(f32).reshape(rows, width) * keep).astype(bf16)

    gated, w_out, w_down, packed, grad_out, *qkv_other = join(
        gated, w_out, w_down, packed, grad_out, *qkv_other
    )
    qkv_pieces = interleaved(qkv_own, qkv_other)
    w_out_full = lax.all_gather(w_out, "fsdp", axis=0, tiled=True)
    columns = [[i + PAIR * k for k in range(chips)] for i in range(PAIR)]
    grad_all = lax.all_gather(grad_out, "fsdp", axis_index_groups=columns)

    projected = kernel_call(
        functools.partial(project_kernel, count, shards, heads),
        ids,
        [gated] + qkv_pieces,
        [shape_of((rows, qkv_width), bf16)] * count,
        scratch=[
            vmem((width, total_width), bf16),
            vmem((rows, total_width), bf16),
            pltpu.SemaphoreType.DMA((shards,)),
        ],
        anywhere=range(1, shards + 1),
    )
    packed, *projected = join(packed, *projected)
    early = max(1, chips - 1)
    gate_up = [across(packed[k], PAIR * k) if k else packed[0] for k in range(early)]
    qkv = rotated(projected)
    qkv = join(*qkv)
    qkv = [a.reshape(batch, group, qkv_width) for a in qkv]
    mixed = block_call(
        functools.partial(attend_kernel, count, heads, head_size), ids, qkv, mixed_width
    )
    *mixed, packed = join(*mixed, packed)
    gate_up += [across(packed[k], PAIR * k) for k in range(early, chips)]
    mixed = returned(mixed)
    both = join(w_down, *gate_up, *mixed)
    own_down, gate_up, mixed = both[0], both[1 : 1 + chips], both[1 + chips :]
    siblings = swap([*gate_up, own_down])
    mixed, middle, normed_two = kernel_call(
        functools.partial(merge_kernel, count),
        ids,
        [a.reshape(rows, mixed_width) for a in mixed]
        + [w_out_full, inputs.reshape(rows, width), keep, gain_two[None]],
        [shape_of((rows, width), kind) for kind in (bf16, f32, bf16)],
        scratch=[vmem((count, rows, mixed_width), bf16), vmem((rows, width), f32)],
    )
    normed_two, other_down, *siblings = join(normed_two, siblings[-1], *siblings[:-1])

    def feed(at, tokens):
        out = [shape_of((rows, hidden_width), bf16)] * 3 + [shape_of((rows, width), bf16)]
        grads = [pick(grad_all, chip ^ k) for k in at]
        outs = kernel_call(
            functools.partial(ffn_kernel, len(at)),
            ids,
            [*tokens, *grads, gate_w, up_w, down_w],
            out * len(at),
            scratch=[vmem((rows * len(at), hidden_width), bf16)] * 2,
        )
        return [[*outs[4 * k : 4 * k + 4], grads[k]] for k in range(len(at))]

    if chips == 4:
        one, two = across(normed_two, 2), across(normed_two, 4)
        gate_w, up_w, down_w = arrange(
            ids, interleaved(gate_up, siblings), w_down, other_down, width
        )
        one, two, gate_w, up_w = join(one, two, gate_w, up_w)
        three = diagonal(jnp.where(core == 0, one, two))
        normed_all = [normed_two, one, two, three]
        last = feed([3], [three])
        last[0][3], one, two = join(last[0][3], one, two)
        received = [across(last[0][3], 6)]
        fed = feed([1, 2], [one, two])
        both = join(normed_two, *received, fed[0][3], fed[1][3])
        normed_own, received, (fed[0][3], fed[1][3]) = both[0], both[1:2], both[2:]
        received += [across(fed[0][3], 2), across(fed[1][3], 4)]
        fed = feed([0], [normed_own]) + fed + last
    else:
        gate_w, up_w, down_w = arrange(
            ids, interleaved(gate_up, siblings), w_down, other_down, width
        )
        normed_all = [across(normed_two, PAIR * k) if k else normed_two for k in range(chips)]
        fed = [feed([k], [normed_all[k]])[0] for k in range(chips)]
        received = [across(fed[k][3], PAIR * k) for k in range(1, chips)]
    hidden_all, gate_back, up_back, backs, grad_all = map(list, zip(*fed))
    down_keeps, down_sends = weight_grad(ids, hidden_all, [grad_all], PAIR, 2)
    both = join(down_sends, gate_back[0], *received)
    down_sends, gate_back[0], received = both[0], both[1], both[2:]

    down_other = across(down_sends[0, 0], 1)
    norm_back = kernel_call(
        functools.partial(norm_back_kernel, count, chips),
        ids,
        [backs[0], *received, middle, grad_out, keep, gain_two[None], w_out_full],
        [shape_of((rows, width), f32), shape_of((rows, width), bf16), shape_of((1, width), f32)]
        + [shape_of((rows, mixed_width), bf16)] * count,
    )
    down_own = (down_keeps[0, 0].astype(f32) + down_other).astype(bf16)
    both = join(down_own, gate_back[0], *norm_back)
    down_own, gate_back[0], norm_back = both[0], both[1], both[2:]
    grad_middle, grad_branch, grad_gain_two = norm_back[:3]

    down_part = lax.psum_scatter(down_own, "ctx", scatter_dimension=0, tiled=True)
    grad_parts = rotated(norm_back[3:])
    keeps, sends = weight_grad(ids, normed_all, [gate_back, up_back], shards)
    out_keeps, out_sends = weight_grad(ids, [mixed], [[grad_branch]], shards)
    downs = kernel_call(
        functools.partial(down_kernel, chips),
        ids,
        hidden_all + [down_w],
        [shape_of((rows, width), bf16)] * chips,
    )
    both = join(sends, out_sends, *grad_parts, *downs)
    sends, out_sends, grad_parts, downs = both[0], both[1], both[2 : 2 + count], both[2 + count :]
    other, out_other = across(sends, 1), across(out_sends[:, 0], 1)
    grad_parts = [a.reshape(batch, group, mixed_width) for a in grad_parts]
    grad_qkv = block_call(
        functools.partial(attend_back_kernel, count, heads, head_size),
        ids,
        qkv + grad_parts,
        qkv_width,
    )
    gate_up_own = [(keeps[k].astype(f32) + other[k]).astype(bf16) for k in range(chips)]
    both = join(down_part, out_other, *grad_qkv, *gate_up_own)
    down_part, out_other, grad_qkv = both[0], both[1], both[2 : 2 + count]
    gate_up_rows = chip_exchange(both[2 + count :])
    grad_qkv = returned(grad_qkv)
    down_whole = lax.all_gather(down_part, "ctx", axis=0, tiled=True)
    both = join(out_other, *grad_qkv, *gate_up_rows[:early])
    out_other, grad_qkv, gate_up_rows[:early] = both[0], both[1 : 1 + count], both[1 + count :]
    grad_qkv, grad_gated = kernel_call(
        functools.partial(project_back_kernel, count, shards, heads),
        ids,
        [a.reshape(rows, qkv_width) for a in grad_qkv] + qkv_pieces,
        [shape_of((rows, total_width), bf16), shape_of((rows, width), f32)],
        scratch=[
            vmem((width, total_width), bf16),
            vmem((count, rows, qkv_width), bf16),
            pltpu.SemaphoreType.DMA((shards,)),
        ],
        anywhere=range(count, count + shards),
    )
    qkv_keeps, qkv_sends = weight_grad(ids, [gated], [[grad_qkv]], shards)
    gate_up_sent = jnp.stack(gate_up_rows).reshape(-1, hidden_width)
    qkv_sends, grad_gated, gate_up_sent = join(qkv_sends, grad_gated, gate_up_sent)

    gate_up_part = lax.psum_scatter(gate_up_sent, "ctx", scatter_dimension=0, tiled=True)
    qkv_other = across(qkv_sends[:, 0], 1)
    out_own = [(out_keeps[k, 0].astype(f32) + out_other[k]).astype(bf16) for k in range(chips)]
    out_rows = chip_exchange(out_own)

    grad_gated = grad_gated.reshape(batch, group, width)
    grad_conv = grad_gated * gate_act
    grad_normed = grad_gated * conv_out * sig_one * (1.0 + normed * (1.0 - sig_one))
    grad_taps = [
        jnp.sum(grad_conv * normed, (0, 1)),
        jnp.sum(grad_conv * normed_ext[:, 1:-1], (0, 1)),
        jnp.sum(grad_conv * normed_ext[:, :-2], (0, 1)),
    ]
    padded = lambda a, before, after: jnp.pad(a, ((0, 0), (before, after), (0, 0)))
    grad_ext = (
        padded(taps[0] * grad_conv, 2, 0)
        + padded(taps[1] * grad_conv, 1, 1)
        + padded(taps[2] * grad_conv, 0, 2)
    )
    later_rows = along(grad_ext[:, :2], -1)
    qkv_own = [(qkv_keeps[k, 0].astype(f32) + qkv_other[k]).astype(bf16) for k in range(chips)]
    grad_normed = grad_normed + grad_ext[:, 2:] + padded(later_rows, group - 2, 0)
    residual = inputs.astype(f32)
    scale_own = scale_ext[:, 2:]
    grad_gain_one = jnp.sum(grad_normed * residual * scale_own, (0, 1))
    scaled_one = grad_normed * gain_one
    cube_one = scale_own * scale_own * scale_own
    grad_rows = (
        grad_middle.reshape(batch, group, width)
        + scale_own * scaled_one
        - residual * cube_one * jnp.mean(scaled_one * residual, -1, keepdims=True)
    ).astype(bf16)
    zero = jnp.zeros_like(grad_gain_one)
    small = jnp.stack([grad_gain_one, grad_gain_two[0]] + grad_taps + [zero, zero, zero])
    small = small + across(small, 1)
    small, grad_rows, *qkv_own = join(small, grad_rows, *qkv_own)
    small = total([small] + [across(small, PAIR * k) for k in range(1, chips)])
    small = lax.dynamic_slice_in_dim(small, mine * own_rows, own_rows, 1).T
    qkv_rows = chip_exchange(qkv_own)

    both = join(gate_up_part, small, *qkv_rows, *out_rows)
    gate_up_part, small, qkv_rows, out_rows = both[0], both[1], both[2 : 2 + chips], both[2 + chips :]
    gate_up_whole = lax.all_gather(gate_up_part, "ctx", axis=0, tiled=True)
    small = jnp.pad(small, ((0, 0), (0, 120)))
    summed = jnp.concatenate([total(qkv_rows), total(out_rows), small], -1).astype(bf16)
    parts = summed.reshape(count, part_rows, summed.shape[1])
    ordered = [(place + step) % count for step in range(count)]
    parts = join(*rotated([pick(parts, at) for at in ordered]))
    part = total(parts).astype(bf16)
    parts = returned([part] * count)
    whole = placed(parts, ordered).reshape(own_rows, summed.shape[1]).astype(f32)
    result = (middle + keep * total(chip_exchange(downs))).astype(bf16)
    gate_up_whole = gate_up_whole.reshape(chips, 2, own_rows, hidden_width)
    grad_w_gate, grad_w_up = kernel_call(
        functools.partial(finish_kernel, chips),
        ids,
        [gate_up_whole],
        [shape_of(w_gate.shape, f32)] * 2,
    )
    small = whole[:, total_width + width :].T
    features = HEADS * FEAT
    return (
        result.reshape(batch, 1, group, width),
        grad_rows[:, None],
        small[0],
        small[2:5],
        whole[:, :features],
        whole[:, features : 2 * features],
        whole[:, 2 * features : total_width],
        whole[:, total_width : total_width + width],
        small[1],
        grad_w_gate,
        grad_w_up,
        down_whole.astype(f32),
    )


def solution(mesh):
    in_specs = (
        P(None, "fsdp", "ctx", None),
        P(None, "fsdp"),
        P(None, "fsdp", "ctx", None),
        P("fsdp"),
        P(None, "fsdp"),
        P("fsdp", None),
        P("fsdp", None),
        P("fsdp", None),
        P("fsdp", None),
        P("fsdp"),
        P("fsdp", None),
        P("fsdp", None),
        P("fsdp", None),
    )
    out_specs = (
        P(None, "fsdp", "ctx", None),
        P(None, "fsdp", "ctx", None),
        P("fsdp"),
        P(None, "fsdp"),
        P("fsdp", None),
        P("fsdp", None),
        P("fsdp", None),
        P("fsdp", None),
        P("fsdp"),
        P("fsdp", None),
        P("fsdp", None),
        P("fsdp", None),
    )
    return jax.shard_map(local, mesh=mesh, in_specs=in_specs, out_specs=out_specs, check_vma=False)
```

time: 2670 us -> 768 us (0.29)
  waiting for transfers between devices: 1940 us -> 336 us
  matrix products: 404 us -> 0 us
  Pallas kernels: 0 us -> 164 us
  blocking collectives: 154 us -> 0 us
  starting transfers between devices: 12.9 us -> 126 us
    reduce_scatter x7 -> x2, waiting for transfers between devices: 716 us -> 16.3 us  [the longest x1 16.3 us: local(): lax.psum_scatter(down_own, 'ctx', scatter_dimension=0, tiled=True)]
    all_gather x9 -> x4, waiting for transfers between devices: 675 us -> 16.8 us  [the longest x1 16.6 us: local(): grad_all = lax.all_gather(grad_out, 'fsdp', axis_index_groups=columns)]
    psum x1 -> x0, waiting for transfers between devices: 538 us -> none  [finish_grads(): lax.psum((shares[0], shares[1], shares[2], shares[3], shares[4], shares[5...]
    dot_general x70 -> x0, matrix products: 404 us -> none  [the longest x14 145 us: left_contract(): jnp.einsum('ta,tb->ab', left, right, preferred_element_type=jnp.float32)]
    ppermute x4 -> x64, waiting for transfers between devices: 4.26 us -> 302 us  [the longest x42 153 us: across(): return lax.ppermute(value, 'fsdp', [(i, i ^ mask) for i in range(count)])]
    pallas_call x0 -> x17, Pallas kernels: none -> 164 us  [the longest x10 95 us: kernel_call(): pl.pallas_call(kernel, out_shape=list(outs), in_specs=specs, out_specs=[w...]
    ppermute x4 -> x64, starting transfers between devices: 11.2 us -> 125 us  [the longest x18 81.1 us: rotate(): lax.ppermute(value, 'ctx', [(i, (i + steps) % count) for i in range(count)])]
    all_gather x7 -> x0, blocking collectives: 104 us -> none  [the longest x4 72.2 us: entering(): gathered = jax.tree.map(lambda a: lax.all_gather(a, axis), part)]
  transfers between devices with their start and end apart: 22 -> 70, of which waited for: 16 -> 31; matrix products, arithmetic and copies ran while one was open for 14% -> 9% of each run, Pallas kernels for 0% -> 19%
where the time goes in v1:
time: 768 us; the launch traced here: 757 us
  waiting for transfers between devices  336 us (44%)
  Pallas kernels  164 us (21%)
  starting transfers between devices  126 us (16%)
  local copies, waits for them, and re-layouts  62.8 us (8%)
  other arithmetic  53.2 us (7%)
  between operations  15.6 us (2%)
    ppermute x42, waiting for transfers between devices, across(): return lax.ppermute(value, 'fsdp', [(i, i ^ mask) for i in range(count)])  153 us
    ppermute x18, waiting for transfers between devices, rotate(): lax.ppermute(value, 'ctx', [(i, (i + steps) % count) for i in range(count)])  147 us
    pallas_call x10, Pallas kernels, kernel_call(): pl.pallas_call(kernel, out_shape=list(outs), in_specs=specs, out_specs=[w...  95 us
    ppermute x18, starting transfers between devices, rotate(): lax.ppermute(value, 'ctx', [(i, (i + steps) % count) for i in range(count)])  81.1 us
    unnamed x204, local copies, waits for them, and re-layouts  43.9 us
    ppermute x42, starting transfers between devices, across(): return lax.ppermute(value, 'fsdp', [(i, i ^ mask) for i in range(count)])  36.1 us
    pallas_call x4, Pallas kernels, weight_grad(): pl.pallas_call(functools.partial(weight_grad_kernel, blocks, groups, part...  33.4 us
    pallas_call x2, Pallas kernels, block_call(): pl.pallas_call(kernel, out_shape=[out] * count, grid=(batch,), in_specs=[...  25 us
  transfers between devices with their start and end apart: 70, of which 31 were waited for; matrix products, arithmetic and copies ran while one was open for 9% of the time, Pallas kernels for 19%

profile of v1, /device:TPU:0, one launch (start us, length us, event | category | flops | bytes accessed | tf_op | source)
XLA Modules:
  0.0 757.1 jit_solution(16579416604148317720)
XLA Ops:
  42.6 11.9 %collective-permute-done.2 = bf16[4,8,224]{2,1,0:T(8,128)(2,1)S(1)} collective-permute-done((bf16[4,8,224]{2,1,0:T(8,128)(2,1)S(1)}, bf16[4,8,224]{2,1,0:T(8,128)(2,1)S(1)}, u32[]{:S(2)}, u32[]{:S(2)}) %collective-permute-start.2) | collective-permute-done | bytes 14368 | tf_op jit(solution)/shard_map/ppermute | solution.py:50
  80.8 13.7 %collective-permute-done.14 = bf16[256,576]{1,0:T(8,128)(2,1)} collective-permute-done((bf16[256,576]{1,0:T(8,128)(2,1)}, bf16[256,576]{1,0:T(8,128)(2,1)}, u32[]{:S(2)}, u32[]{:S(2)}) %collective-permute-start.14) | collective-permute-done | bytes 294944 | tf_op jit(solution)/shard_map/ppermute | solution.py:45
  105.5 8.5 %collective-permute-start.17 = (bf16[2,128,448]{2,1,0:T(8,128)(2,1)S(1)}, bf16[2,128,448]{2,1,0:T(8,128)(2,1)S(1)}, u32[]{:S(2)}, u32[]{:S(2)}) collective-permute-start(bf16[2,128,448]{2,1,0:T(8,128)(2,1)S(1)} %get-tuple-element.223), channel_id=1, source_target_pairs={{0,24},{8,0},{16,8},{24,16},{1,25},{9,1},{17,9},{25,17},{2,26},{10... | collective-permute-start | bytes 688136 | tf_op jit(solution)/shard_map/ppermute | solution.py:45
  121.5 12.6 %collective-permute-start.19 = (bf16[2,128,448]{2,1,0:T(8,128)(2,1)S(1)}, bf16[2,128,448]{2,1,0:T(8,128)(2,1)S(1)}, u32[]{:S(2)}, u32[]{:S(2)}) collective-permute-start(bf16[2,128,448]{2,1,0:T(8,128)(2,1)S(1)} %get-tuple-element.225), channel_id=1, source_target_pairs={{0,8},{8,16},{16,24},{24,0},{1,9},{9,17},{17,25},{25,1},{2,10},{10... | collective-permute-start | bytes 688136 | tf_op jit(solution)/shard_map/ppermute | solution.py:45
  165.1 10.6 %shard_map.224 = (bf16[1792,1216]{1,0:T(8,128)(2,1)}, bf16[1792,1216]{1,0:T(8,128)(2,1)}, bf16[1216,1792]{1,0:T(8,128)(2,1)}) custom-call(s32[2]{0:T(128)S(1)} %pad_add_fusion.2.ids.place_ref, bf16[2,224,1216]{2,1,0:T(8,128)(2,1)} %get-tuple-element.234.rest_0_, bf16[2,224,1216]{2,1,0:T(8,128)(2,1)} %collective-permute-done.21.rest_1_, ...), custom_call_target="tpu_custom_call" | custom-call | tf_op jit(solution)/shard_map/pallas_call | solution.py:361
  175.7 21.6 %collective-permute-done.25.rest_0_.rest_1_ = bf16[256,1792]{1,0:T(8,128)(2,1)S(1)} collective-permute-done((bf16[256,1792]{1,0:T(8,128)(2,1)S(1)}, bf16[256,1792]{1,0:T(8,128)(2,1)S(1)}, u32[]{:S(2)}, u32[]{:S(2)}) %collective-permute-start.25) | collective-permute-done | bytes 917536 | tf_op jit(solution)/shard_map/ppermute | solution.py:50
  200.9 16.6 %all-gather.12.cloned.1.call-done = bf16[1024,1792]{1,0:T(8,128)(2,1)} async-done(((bf16[256,1792]{1,0:T(8,128)(2,1)}), bf16[1024,1792]{1,0:T(8,128)(2,1)}) %all-gather.12.cloned.1.call-update) | async-done | bytes 3670032 | tf_op jit(solution)/shard_map/all_gather | solution.py:537
  222.5 12.0 %shard_map.225 = (bf16[256,1216]{1,0:T(8,128)(2,1)S(1)}, bf16[256,1216]{1,0:T(8,128)(2,1)S(1)}, bf16[256,1216]{1,0:T(8,128)(2,1)S(1)}, bf16[256,1792]{1,0:T(8,128)(2,1)S(1)}) custom-call(s32[2]{0:T(128)S(1)} %pad_add_fusion.2.ids.place_ref, bf16[256,1792]{1,0:T(8,128)(2,1)} %collective-permute-done.27.rest_0_.rest_3_, ...), custom_call_target="tpu_custom_call" | custom-call | tf_op jit(solution)/shard_map/pallas_call | solution.py:94
  236.8 20.4 %shard_map.226 = (bf16[256,1216]{1,0:T(8,128)(2,1)S(1)}, bf16[256,1216]{1,0:T(8,128)(2,1)S(1)}, bf16[256,1216]{1,0:T(8,128)(2,1)S(1)}, bf16[256,1792]{1,0:T(8,12...) custom-call(s32[2]{0:T(128)S(1)} %pad_add_fusion.2.ids.place_ref, ...), custom_call_target="tpu_custom_call" | custom-call | tf_op jit(solution)/shard_map/pallas_call | solution.py:94
  262.6 11.9 %shard_map.227 = (bf16[256,1216]{1,0:T(8,128)(2,1)S(1)}, bf16[256,1216]{1,0:T(8,128)(2,1)S(1)}, bf16[256,1216]{1,0:T(8,128)(2,1)S(1)}, bf16[256,1792]{1,0:T(8,128)(2,1)S(1)}) custom-call(s32[2]{0:T(128)S(1)} %pad_add_fusion.2.ids.place_ref, bf16[256,1792]{1,0:T(8,128)(2,1)S(1)} %copy-done.11, bf16[256,1792]{1,0:T(8,128)(2,1)S(1)} %get-tuple-element.460.rest_1_.rest_4_, ...), custom_call_target="tpu_custom_call" | custom-call | tf_op jit(solution)/shard_map/pallas_call | solution.py:94
  274.5 8.5 %shard_map.228 = (bf16[1,1,608,1792]{3,2,1,0:T(8,128)(2,1)}, bf16[1,1,608,1792]{3,2,1,0:T(8,128)(2,1)}) custom-call(s32[2]{0:T(128)S(1)} %pad_add_fusion.2.ids.place_ref, bf16[256,1216]{1,0:T(8,128)(2,1)S(1)} %get-tuple-element.259.rest_0_, bf16[256,1216]{1,0:T(8,128)(2,1)S(1)} %get-tuple-element.260.rest_1_, ...), custom_call_target="tpu_custom_call" | custom-call | tf_op jit(solution)/shard_map/pallas_call | solution.py:337
  283.3 10.4 %shard_map.229 = (f32[256,1792]{1,0:T(8,128)}, bf16[256,1792]{1,0:T(8,128)(2,1)S(1)}, f32[1,1792]{1,0:T(1,128)S(1)}, bf16[256,448]{1,0:T(8,128)(2,1)S(1)}, bf16[...) custom-call(s32[2]{0:T(128)S(1)} %pad_add_fusion.2.ids.place_ref, ...), custom_call_target="tpu_custom_call" | custom-call | tf_op jit(solution)/shard_map/pallas_call | solution.py:94
  325.2 15.1 %shard_map.230 = (bf16[4,2,224,1216]{3,2,1,0:T(8,128)(2,1)}, bf16[4,2,224,1216]{3,2,1,0:T(8,128)(2,1)}) custom-call(s32[2]{0:T(128)S(1)} %pad_add_fusion.2.ids.place_ref, bf16[256,1792]{1,0:T(8,128)(2,1)S(1)} %copy-done.12, bf16[256,1792]{1,0:T(8,128)(2,1)} %copy-done.79, bf16[256,1792]{1,0:T(8,128)(2,1)} %copy-done.80, ...), custom_call_target="tpu_custom_call" | custom-call | tf_op jit(solution)/shard_map/pallas_call | solution.py:337
  344.1 17.0 %shard_map.233 = (bf16[2,128,576]{2,1,0:T(8,128)(2,1)S(1)}, bf16[2,128,576]{2,1,0:T(8,128)(2,1)S(1)}, bf16[2,128,576]{2,1,0:T(8,128)(2,1)S(1)}, bf16[2,128,576]{2,1,0:T(8,128)(2,1)S(1)}) custom-call(s32[2]{0:T(128)S(1)} %pad_add_fusion.2.ids.place_ref, bf16[2,128,576]{2,1,0:T(8,128)(2,1)S(1)} %bitcast.175, bf16[2,128,576]{2,1,0:T(8,128)(2,1)S(1)} %bitcast.177, ...), custom_call_target="tpu_custom_call" | custom-call | tf_op jit(solution)/shard_map/pallas_call | solution.py:445
  367.5 16.3 %reduce-scatter.3.cloned.1.call-done = bf16[152,1792]{1,0:T(8,128)(2,1)} async-done(((bf16[608,1792]{1,0:T(8,128)(2,1)}), bf16[152,1792]{1,0:T(8,128)(2,1)}) %reduce-scatter.3.cloned.1.call-update) | async-done | bytes 544784 | tf_op jit(solution)/shard_map/reduce_scatter | solution.py:629
  397.6 15.3 %collective-permute-start.42 = (bf16[2,128,576]{2,1,0:T(8,128)(2,1)}, bf16[2,128,576]{2,1,0:T(8,128)(2,1)S(1)}, u32[]{:S(2)}, u32[]{:S(2)}) collective-permute-start(bf16[2,128,576]{2,1,0:T(8,128)(2,1)} %copy-done.70), channel_id=1, source_target_pairs={{0,8},{8,16},{16,24},{24,0},{1,9},{9,17},{17,25},{25,1},{2,10},{10... | collective-permute-start | bytes 884744 | tf_op jit(solution)/shard_map/ppermute | solution.py:45
  417.8 19.1 %collective-permute-done.44 = bf16[2,224,1216]{2,1,0:T(8,128)(2,1)S(1)} collective-permute-done((bf16[2,224,1216]{2,1,0:T(8,128)(2,1)}, bf16[2,224,1216]{2,1,0:T(8,128)(2,1)S(1)}, u32[]{:S(2)}, u32[]{:S(2)}) %collective-permute-start.44) | collective-permute-done | bytes 1089568 | tf_op jit(solution)/shard_map/ppermute | solution.py:50
  490.4 43.0 %collective-permute-done.49 = f32[8,1792]{1,0:T(8,128)S(1)} collective-permute-done((f32[8,1792]{1,0:T(8,128)S(1)}, f32[8,1792]{1,0:T(8,128)S(1)}, u32[]{:S(2)}, u32[]{:S(2)}) %collective-permute-start.49) | collective-permute-done | bytes 57376 | tf_op jit(solution)/shard_map/ppermute | solution.py:50
  540.8 31.7 %collective-permute-done.56 = bf16[224,1792]{1,0:T(8,128)(2,1)} collective-permute-done((bf16[224,1792]{1,0:T(8,128)(2,1)}, bf16[224,1792]{1,0:T(8,128)(2,1)}, u32[]{:S(2)}, u32[]{:S(2)}) %collective-permute-start.56) | collective-permute-done | bytes 802848 | tf_op jit(solution)/shard_map/ppermute | solution.py:50
  585.4 13.9 %collective-permute-done.58 = bf16[56,4224]{1,0:T(8,128)(2,1)} collective-permute-done((bf16[56,4224]{1,0:T(8,128)(2,1)}, bf16[56,4224]{1,0:T(8,128)(2,1)}, u32[]{:S(2)}, u32[]{:S(2)}) %collective-permute-start.58) | collective-permute-done | bytes 473120 | tf_op jit(solution)/shard_map/ppermute | solution.py:45
  601.6 17.0 %collective-permute-done.59 = bf16[56,4224]{1,0:T(8,128)(2,1)} collective-permute-done((bf16[56,4224]{1,0:T(8,128)(2,1)}, bf16[56,4224]{1,0:T(8,128)(2,1)}, u32[]{:S(2)}, u32[]{:S(2)}) %collective-permute-start.59) | collective-permute-done | bytes 473120 | tf_op jit(solution)/shard_map/ppermute | solution.py:45
  621.5 24.4 %collective-permute-start.61 = (bf16[56,4224]{1,0:T(8,128)(2,1)}, bf16[56,4224]{1,0:T(8,128)(2,1)S(1)}, u32[]{:S(2)}, u32[]{:S(2)}) collective-permute-start(bf16[56,4224]{1,0:T(8,128)(2,1)} %get-tuple-element.436), channel_id=1, source_target_pairs={{0,24},{8,0},{16,8},{24,16},{1,25},{9,1},{17,9},{25,17},{2,26},{10... | collective-permute-start | bytes 1419272 | tf_op jit(solution)/shard_map/ppermute | solution.py:45
  654.6 21.7 %collective-permute-done.61 = bf16[56,4224]{1,0:T(8,128)(2,1)S(1)} collective-permute-done((bf16[56,4224]{1,0:T(8,128)(2,1)}, bf16[56,4224]{1,0:T(8,128)(2,1)S(1)}, u32[]{:S(2)}, u32[]{:S(2)}) %collective-permute-start.61) | collective-permute-done | bytes 473120 | tf_op jit(solution)/shard_map/ppermute | solution.py:45
  676.4 56.8 %collective-permute-done.62 = bf16[56,4224]{1,0:T(8,128)(2,1)S(1)} collective-permute-done((bf16[56,4224]{1,0:T(8,128)(2,1)}, bf16[56,4224]{1,0:T(8,128)(2,1)S(1)}, u32[]{:S(2)}, u32[]{:S(2)}) %collective-permute-start.62) | collective-permute-done | bytes 473120 | tf_op jit(solution)/shard_map/ppermute | solution.py:45
  (430 shorter events, 291.3 us)
Async XLA Ops:
  7.2 141.3 %all-gather.6.cloned.1.call-start = ((), (), s32[]{:S(2)}) async-start(), calls=%async_computation.2 | async-start | bytes 7225344 | tf_op jit(solution)/shard_map/all_gather | solution.py:535
  59.1 158.4 %all-gather.12.cloned.1.call-start = ((), (), s32[]{:S(2)}) async-start(), calls=%async_computation.7 | async-start | bytes 4587520 | tf_op jit(solution)/shard_map/all_gather | solution.py:537
  77.4 61.4 %collective-permute-start.11 = (bf16[2,224,1216]{2,1,0:T(8,128)(2,1)}, bf16[2,224,1216]{2,1,0:T(8,128)(2,1)}, u32[]{:S(2)}, u32[]{:S(2)}) collective-permute-start(bf16[2,224,1216]{2,1,0:T(8,128)(2,1)} %get-tuple-element.454), channel_id=1, source_target_pairs={{0,2},{1,3},{2,0},{3,1},{4,6},{5,7},{6,4},{7,5},{8,10},{9,11},{10,... | collective-permute-start | bytes 3268616 | tf_op jit(solution)/shard_map/ppermute | solution.py:50
  78.0 67.6 %collective-permute-start.12 = (bf16[2,224,1216]{2,1,0:T(8,128)(2,1)}, bf16[2,224,1216]{2,1,0:T(8,128)(2,1)}, u32[]{:S(2)}, u32[]{:S(2)}) collective-permute-start(bf16[2,224,1216]{2,1,0:T(8,128)(2,1)} %get-tuple-element.453), channel_id=1, source_target_pairs={{0,4},{1,5},{2,6},{3,7},{4,0},{5,1},{6,2},{7,3},{8,12},{9,13},{10,... | collective-permute-start | bytes 3268616 | tf_op jit(solution)/shard_map/ppermute | solution.py:50
  79.5 304.3 %reduce-scatter.3.cloned.1.call-start = ((), (), s32[]{:S(2)}) async-start(), calls=%async_computation.3 | async-start | bytes 2723840 | tf_op jit(solution)/shard_map/reduce_scatter | solution.py:629
  104.0 43.2 %collective-permute-start.16 = (bf16[2,224,1216]{2,1,0:T(8,128)(2,1)S(1)}, bf16[2,224,1216]{2,1,0:T(8,128)(2,1)}, u32[]{:S(2)}, u32[]{:S(2)}) collective-permute-start(bf16[2,224,1216]{2,1,0:T(8,128)(2,1)S(1)} %slice_bitcast_fusion), channel_id=1, source_target_pairs={{0,6},{1,7},{2,4},{3,5},{4,2},{5,3},{6,0},{7,1},{8,14},{9,15},{10,... | collective-permute-start | bytes 3268616 | tf_op jit(solution)/shard_map/ppermute | solution.py:50
  299.4 41.0 %collective-permute-start.32 = (bf16[256,448]{1,0:T(8,128)(2,1)}, bf16[256,448]{1,0:T(8,128)(2,1)S(1)}, u32[]{:S(2)}, u32[]{:S(2)}) collective-permute-start(bf16[256,448]{1,0:T(8,128)(2,1)} %copy-done.75), channel_id=1, source_target_pairs={{0,8},{8,16},{16,24},{24,0},{1,9},{9,17},{17,25},{25,1},{2,10},{10... | collective-permute-start | bytes 688136 | tf_op jit(solution)/shard_map/ppermute | solution.py:45
  300.8 40.3 %collective-permute-start.33 = (bf16[256,448]{1,0:T(8,128)(2,1)}, bf16[256,448]{1,0:T(8,128)(2,1)}, u32[]{:S(2)}, u32[]{:S(2)}) collective-permute-start(bf16[256,448]{1,0:T(8,128)(2,1)} %copy-done.74), channel_id=1, source_target_pairs={{0,16},{8,24},{16,0},{24,8},{1,17},{9,25},{17,1},{25,9},{2,18},{10... | collective-permute-start | bytes 688136 | tf_op jit(solution)/shard_map/ppermute | solution.py:45
  341.1 231.4 %reduce-scatter.5.cloned.1.call-start = ((), (), s32[]{:S(2)}) async-start(), calls=%async_computation.4 | async-start | bytes 5734400 | tf_op jit(solution)/shard_map/reduce_scatter | solution.py:673
  385.6 51.3 %collective-permute-start.44 = (bf16[2,224,1216]{2,1,0:T(8,128)(2,1)}, bf16[2,224,1216]{2,1,0:T(8,128)(2,1)S(1)}, u32[]{:S(2)}, u32[]{:S(2)}) collective-permute-start(bf16[2,224,1216]{2,1,0:T(8,128)(2,1)} %get-tuple-element.325), channel_id=1, source_target_pairs={{0,4},{1,5},{2,6},{3,7},{4,0},{5,1},{6,2},{7,3},{8,12},{9,13},{10,... | collective-permute-start | bytes 3268616 | tf_op jit(solution)/shard_map/ppermute | solution.py:50
  387.1 66.5 %collective-permute-start.45 = (bf16[2,224,1216]{2,1,0:T(8,128)(2,1)}, bf16[2,224,1216]{2,1,0:T(8,128)(2,1)S(1)}, u32[]{:S(2)}, u32[]{:S(2)}) collective-permute-start(bf16[2,224,1216]{2,1,0:T(8,128)(2,1)} %get-tuple-element.336), channel_id=1, source_target_pairs={{0,6},{1,7},{2,4},{3,5},{4,2},{5,3},{6,0},{7,1},{8,14},{9,15},{10,... | collective-permute-start | bytes 3268616 | tf_op jit(solution)/shard_map/ppermute | solution.py:50
  456.1 192.6 %all-gather.10.cloned.1.call-start = ((), (), s32[]{:S(2)}) async-start(), calls=%async_computation.6 | async-start | bytes 2723840 | tf_op jit(solution)/shard_map/all_gather | solution.py:654
  481.2 91.4 %collective-permute-start.52 = (bf16[224,2304]{1,0:T(8,128)(2,1)}, bf16[224,2304]{1,0:T(8,128)(2,1)S(1)}, u32[]{:S(2)}, u32[]{:S(2)}) collective-permute-start(bf16[224,2304]{1,0:T(8,128)(2,1)} %get-tuple-element.346), channel_id=1, source_target_pairs={{0,2},{1,3},{2,0},{3,1},{4,6},{5,7},{6,4},{7,5},{8,10},{9,11},{10,... | collective-permute-start | bytes 3096584 | tf_op jit(solution)/shard_map/ppermute | solution.py:50
  481.7 90.9 %collective-permute-start.53 = (bf16[224,2304]{1,0:T(8,128)(2,1)}, bf16[224,2304]{1,0:T(8,128)(2,1)}, u32[]{:S(2)}, u32[]{:S(2)}) collective-permute-start(bf16[224,2304]{1,0:T(8,128)(2,1)} %get-tuple-element.347), channel_id=1, source_target_pairs={{0,4},{1,5},{2,6},{3,7},{4,0},{5,1},{6,2},{7,3},{8,12},{9,13},{10,... | collective-permute-start | bytes 3096584 | tf_op jit(solution)/shard_map/ppermute | solution.py:50
  483.7 88.8 %collective-permute-start.54 = (bf16[224,2304]{1,0:T(8,128)(2,1)}, bf16[224,2304]{1,0:T(8,128)(2,1)}, u32[]{:S(2)}, u32[]{:S(2)}) collective-permute-start(bf16[224,2304]{1,0:T(8,128)(2,1)} %get-tuple-element.348), channel_id=1, source_target_pairs={{0,6},{1,7},{2,4},{3,5},{4,2},{5,3},{6,0},{7,1},{8,14},{9,15},{10,... | collective-permute-start | bytes 3096584 | tf_op jit(solution)/shard_map/ppermute | solution.py:50
  484.7 48.8 %collective-permute-start.49 = (f32[8,1792]{1,0:T(8,128)S(1)}, f32[8,1792]{1,0:T(8,128)S(1)}, u32[]{:S(2)}, u32[]{:S(2)}) collective-permute-start(f32[8,1792]{1,0:T(8,128)S(1)} %add.282), channel_id=1, source_target_pairs={{0,2},{1,3},{2,0},{3,1},{4,6},{5,7},{6,4},{7,5},{8,10},{9,11},{10,... | collective-permute-start | bytes 172040 | tf_op jit(solution)/shard_map/ppermute | solution.py:50
  488.8 46.6 %collective-permute-start.50 = (f32[8,1792]{1,0:T(8,128)S(1)}, f32[8,1792]{1,0:T(8,128)S(1)}, u32[]{:S(2)}, u32[]{:S(2)}) collective-permute-start(f32[8,1792]{1,0:T(8,128)S(1)} %add.282), channel_id=1, source_target_pairs={{0,4},{1,5},{2,6},{3,7},{4,0},{5,1},{6,2},{7,3},{8,12},{9,13},{10,... | collective-permute-start | bytes 172040 | tf_op jit(solution)/shard_map/ppermute | solution.py:50
  540.6 202.3 %all-gather.8.cloned.1.call-start = ((), (), s32[]{:S(2)}) async-start(), calls=%async_computation.5 | async-start | bytes 5734400 | tf_op jit(solution)/shard_map/all_gather | solution.py:715
  583.2 62.6 %collective-permute-start.35 = (bf16[256,1792]{1,0:T(8,128)(2,1)S(1)}, bf16[256,1792]{1,0:T(8,128)(2,1)S(1)}, u32[]{:S(2)}, u32[]{:S(2)}) collective-permute-start(bf16[256,1792]{1,0:T(8,128)(2,1)S(1)} %copy-done.69), channel_id=1, source_target_pairs={{0,2},{1,3},{2,0},{3,1},{4,6},{5,7},{6,4},{7,5},{8,10},{9,11},{10,... | collective-permute-start | bytes 2752520 | tf_op jit(solution)/shard_map/ppermute | solution.py:50
  584.1 61.7 %collective-permute-start.36 = (bf16[256,1792]{1,0:T(8,128)(2,1)S(1)}, bf16[256,1792]{1,0:T(8,128)(2,1)}, u32[]{:S(2)}, u32[]{:S(2)}) collective-permute-start(bf16[256,1792]{1,0:T(8,128)(2,1)S(1)} %copy-done.67), channel_id=1, source_target_pairs={{0,4},{1,5},{2,6},{3,7},{4,0},{5,1},{6,2},{7,3},{8,12},{9,13},{10,... | collective-permute-start | bytes 2752520 | tf_op jit(solution)/shard_map/ppermute | solution.py:50
  599.3 46.6 %collective-permute-start.37 = (bf16[256,1792]{1,0:T(8,128)(2,1)}, bf16[256,1792]{1,0:T(8,128)(2,1)S(1)}, u32[]{:S(2)}, u32[]{:S(2)}) collective-permute-start(bf16[256,1792]{1,0:T(8,128)(2,1)} %get-tuple-element.304), channel_id=1, source_target_pairs={{0,6},{1,7},{2,4},{3,5},{4,2},{5,3},{6,0},{7,1},{8,14},{9,15},{10,... | collective-permute-start | bytes 2752520 | tf_op jit(solution)/shard_map/ppermute | solution.py:50
  621.5 54.8 %collective-permute-start.61 = (bf16[56,4224]{1,0:T(8,128)(2,1)}, bf16[56,4224]{1,0:T(8,128)(2,1)S(1)}, u32[]{:S(2)}, u32[]{:S(2)}) collective-permute-start(bf16[56,4224]{1,0:T(8,128)(2,1)} %get-tuple-element.436), channel_id=1, source_target_pairs={{0,24},{8,0},{16,8},{24,16},{1,25},{9,1},{17,9},{25,17},{2,26},{10... | collective-permute-start | bytes 1419272 | tf_op jit(solution)/shard_map/ppermute | solution.py:45
  652.8 80.3 %collective-permute-start.62 = (bf16[56,4224]{1,0:T(8,128)(2,1)}, bf16[56,4224]{1,0:T(8,128)(2,1)S(1)}, u32[]{:S(2)}, u32[]{:S(2)}) collective-permute-start(bf16[56,4224]{1,0:T(8,128)(2,1)} %get-tuple-element.436), channel_id=1, source_target_pairs={{0,16},{8,24},{16,0},{24,8},{1,17},{9,25},{17,1},{25,9},{2,18},{10... | collective-permute-start | bytes 1419272 | tf_op jit(solution)/shard_map/ppermute | solution.py:45
  653.7 79.5 %collective-permute-start.63 = (bf16[56,4224]{1,0:T(8,128)(2,1)}, bf16[56,4224]{1,0:T(8,128)(2,1)S(1)}, u32[]{:S(2)}, u32[]{:S(2)}) collective-permute-start(bf16[56,4224]{1,0:T(8,128)(2,1)} %get-tuple-element.436), channel_id=1, source_target_pairs={{0,8},{8,16},{16,24},{24,0},{1,9},{9,17},{17,25},{25,1},{2,10},{10... | collective-permute-start | bytes 1419272 | tf_op jit(solution)/shard_map/ppermute | solution.py:45
  (146 other events, 1751.7 us)
Sparse Core Ops, SparseCore 0:
  59.2 64.9 all-gather.5
  126.6 90.7 all-gather.11
  341.3 42.5 reduce-scatter.2
  456.2 82.4 reduce-scatter.4
  540.8 70.8 all-gather.9
  613.1 129.7 all-gather.7

commit v2 on v1

--- a/solution.py
+++ b/solution.py
@@ -86,7 +86,7 @@
     return buffer
 
 
-def kernel_call(kernel, ids, arrays, outs, scratch=(), anywhere=()):
+def kernel_call(kernel, ids, arrays, outs, scratch=(), anywhere=(), vmem=32):
     whole = pl.BlockSpec(memory_space=pltpu.VMEM)
     specs = [pl.BlockSpec(memory_space=pltpu.SMEM)]
     anyplace = pl.BlockSpec(memory_space=pl.ANY)
@@ -97,7 +97,7 @@
         in_specs=specs,
         out_specs=[whole] * len(outs),
         scratch_shapes=list(scratch),
-        compiler_params=pltpu.CompilerParams(vmem_limit_bytes=48 * 1024 * 1024),
+        compiler_params=pltpu.CompilerParams(vmem_limit_bytes=vmem * 1024 * 1024),
         cost_estimate=FREE,
     )(ids, *arrays)
 
@@ -255,33 +255,49 @@
             out[q ^ chip, half] = ref[:, q * part : (q + 1) * part]
 
 
-def ffn_kernel(chunks, ids, *rest):
-    normed = jnp.concatenate([ref[...] for ref in rest[:chunks]], 0)
-    grad_out = jnp.concatenate([ref[...] for ref in rest[chunks : 2 * chunks]], 0)
-    gate_w, up_w, down_w = rest[2 * chunks : 2 * chunks + 3]
-    outs = rest[2 * chunks + 3 : -2]
+def feed_kernel(chunks, ids, *rest):
+    tokens = jnp.concatenate([ref[...] for ref in rest[:chunks]], 0)
+    gate_w, up_w = rest[chunks : chunks + 2]
+    hidden, to_gate, to_up = (rest[chunks + 2 + i * chunks :][:chunks] for i in range(3))
+    size = tokens.shape[0] // chunks
+
+    def put(refs, tile, value):
+        for k, ref in enumerate(refs):
+            ref[:, tile] = value[k * size : (k + 1) * size].astype(bf16)
+
+    for tile in tiles(gate_w.shape[1], 256):
+        gate_pre = matmul(tokens, gate_w[:, tile])
+        up_pre = matmul(tokens, up_w[:, tile])
+        sig = jax.nn.sigmoid(gate_pre)
+        gate_silu = gate_pre * sig
+        put(hidden, tile, gate_silu * up_pre)
+        put(to_gate, tile, up_pre * sig * (1.0 + gate_pre * (1.0 - sig)))
+        put(to_up, tile, gate_silu)
+
+
+def feed_back_kernel(chunks, ids, *rest):
+    grad_out = jnp.concatenate([ref[...] for ref in rest[:chunks]], 0)
+    to_gate = jnp.concatenate([ref[...] for ref in rest[chunks : 2 * chunks]], 0)
+    to_up = jnp.concatenate([ref[...] for ref in rest[2 * chunks : 3 * chunks]], 0)
+    gate_w, up_w, down_w = rest[3 * chunks : 3 * chunks + 3]
+    outs = rest[3 * chunks + 3 : -2]
     gate_all, up_all = rest[-2:]
-    size = normed.shape[0] // chunks
+    size = grad_out.shape[0] // chunks
 
     def put(which, tile, value):
         for k in range(chunks):
-            outs[4 * k + which][:, tile] = value[k * size : (k + 1) * size].astype(bf16)
+            outs[3 * k + which][:, tile] = value[k * size : (k + 1) * size].astype(bf16)
 
     for tile in tiles(gate_w.shape[1], 256):
-        gate_pre = matmul(normed, gate_w[:, tile])
-        up_pre = matmul(normed, up_w[:, tile])
         grad_hidden = right_contract(grad_out, down_w[tile])
-        sig = jax.nn.sigmoid(gate_pre)
-        gate_silu = gate_pre * sig
-        gate_back = grad_hidden * up_pre * sig * (1.0 + gate_pre * (1.0 - sig))
-        gate_back, up_back = gate_back.astype(bf16), (grad_hidden * gate_silu).astype(bf16)
+        gate_back = (grad_hidden * to_gate[:, tile].astype(f32)).astype(bf16)
+        up_back = (grad_hidden * to_up[:, tile].astype(f32)).astype(bf16)
         gate_all[:, tile], up_all[:, tile] = gate_back, up_back
-        put(0, tile, gate_silu * up_pre)
-        put(1, tile, gate_back)
-        put(2, tile, up_back)
+        put(0, tile, gate_back)
+        put(1, tile, up_back)
     for tile in tiles(gate_w.shape[0], 256):
         value = right_contract(gate_all[...], gate_w[tile])
-        put(3, tile, value + right_contract(up_all[...], up_w[tile]))
+        put(2, tile, value + right_contract(up_all[...], up_w[tile]))
 
 
 def down_kernel(chips, ids, *rest):
@@ -342,7 +358,7 @@
         + [pl.BlockSpec(memory_space=pltpu.VMEM)] * len(arrays),
         out_specs=[block] * 2,
         scratch_shapes=[pltpu.VMEM((rows, chunks * tokens), bf16)],
-        compiler_params=pltpu.CompilerParams(vmem_limit_bytes=48 * 1024 * 1024),
+        compiler_params=pltpu.CompilerParams(vmem_limit_bytes=32 * 1024 * 1024),
         cost_estimate=FREE,
     )(ids, *arrays)
 
@@ -365,7 +381,7 @@
         in_specs=[pl.BlockSpec(memory_space=pltpu.SMEM)] + [anywhere] * (shards + 2),
         out_specs=[pl.BlockSpec(memory_space=pltpu.VMEM)] * 3,
         scratch_shapes=[pltpu.SemaphoreType.DMA((2 * shards + 2,))],
-        compiler_params=pltpu.CompilerParams(vmem_limit_bytes=48 * 1024 * 1024),
+        compiler_params=pltpu.CompilerParams(vmem_limit_bytes=24 * 1024 * 1024),
         cost_estimate=FREE,
     )(ids, *pieces, own_down, other_down)
 
@@ -448,7 +464,7 @@
         grid=(batch,),
         in_specs=[pl.BlockSpec(memory_space=pltpu.SMEM)] + [spec(a) for a in arrays],
         out_specs=[spec(out)] * count,
-        compiler_params=pltpu.CompilerParams(vmem_limit_bytes=48 * 1024 * 1024),
+        compiler_params=pltpu.CompilerParams(vmem_limit_bytes=24 * 1024 * 1024),
         cost_estimate=FREE,
     )(ids, *arrays)
 
@@ -573,47 +589,65 @@
     )
     normed_two, other_down, *siblings = join(normed_two, siblings[-1], *siblings[:-1])
 
-    def feed(at, tokens):
-        out = [shape_of((rows, hidden_width), bf16)] * 3 + [shape_of((rows, width), bf16)]
-        grads = [pick(grad_all, chip ^ k) for k in at]
-        outs = kernel_call(
-            functools.partial(ffn_kernel, len(at)),
-            ids,
-            [*tokens, *grads, gate_w, up_w, down_w],
-            out * len(at),
-            scratch=[vmem((rows * len(at), hidden_width), bf16)] * 2,
-        )
-        return [[*outs[4 * k : 4 * k + 4], grads[k]] for k in range(len(at))]
-
+    gate_w, up_w, down_w = arrange(
+        ids, interleaved(gate_up, siblings), w_down, other_down, width
+    )
     if chips == 4:
         one, two = across(normed_two, 2), across(normed_two, 4)
-        gate_w, up_w, down_w = arrange(
-            ids, interleaved(gate_up, siblings), w_down, other_down, width
+        one, two, gate_w, up_w = join(one, two, gate_w, up_w)
+        normed_all = [normed_two, one, two, diagonal(jnp.where(core == 0, one, two))]
+    else:
+        normed_all = [across(normed_two, PAIR * k) if k else normed_two for k in range(chips)]
+    unit = shape_of((rows, hidden_width), bf16)
+    fed = kernel_call(
+        functools.partial(feed_kernel, chips),
+        ids,
+        [*normed_all, gate_w, up_w],
+        [unit] * 3 * chips,
+        vmem=32,
+    )
+    hidden_all, to_gate, to_up = fed[:chips], fed[chips : 2 * chips], fed[2 * chips :]
+    grad_all = [pick(grad_all, chip ^ k) for k in range(chips)]
+
+    def feed_back(at):
+        outs = kernel_call(
+            functools.partial(feed_back_kernel, len(at)),
+            ids,
+            [source[k] for source in (grad_all, to_gate, to_up) for k in at]
+            + [gate_w, up_w, down_w],
+            [unit, unit, shape_of((rows, width), bf16)] * len(at),
+            scratch=[vmem((rows * len(at), hidden_width), bf16)] * 2,
+            vmem=32,
         )
-        one, two, gate_w, up_w = join(one, two, gate_w, up_w)
-        three = diagonal(jnp.where(core == 0, one, two))
-        normed_all = [normed_two, one, two, three]
-        last = feed([3], [three])
-        last[0][3], one, two = join(last[0][3], one, two)
-        received = [across(last[0][3], 6)]
-        fed = feed([1, 2], [one, two])
-        both = join(normed_two, *received, fed[0][3], fed[1][3])
-        normed_own, received, (fed[0][3], fed[1][3]) = both[0], both[1:2], both[2:]
-        received += [across(fed[0][3], 2), across(fed[1][3], 4)]
-        fed = feed([0], [normed_own]) + fed + last
+        return [list(outs[3 * i : 3 * i + 3]) for i in range(len(at))]
+
+    down_keeps, down_sends = weight_grad(ids, hidden_all, [grad_all], PAIR, 2)
+    both = join(down_sends, *grad_all)
+    down_sends, grad_all = both[0], both[1:]
+    down_other = across(down_sends[0, 0], 1)
+    if chips == 4:
+        last = feed_back([3])
+        down_own = (down_keeps[0, 0].astype(f32) + down_other).astype(bf16)
+        both = join(down_own, last[0][2], *grad_all)
+        down_own, last[0][2], grad_all = both[0], both[1], both[2:]
+        down_part = lax.psum_scatter(down_own, "ctx", scatter_dimension=0, tiled=True)
+        received = [across(last[0][2], 6)]
+        middles = feed_back([1, 2])
+        both = join(*received, middles[0][2], middles[1][2], *grad_all)
+        received, middles[0][2], middles[1][2], grad_all = both[:1], both[1], both[2], both[3:]
+        received += [across(middles[0][2], 2), across(middles[1][2], 4)]
+        fed = feed_back([0]) + middles + last
     else:
-        gate_w, up_w, down_w = arrange(
-            ids, interleaved(gate_up, siblings), w_down, other_down, width
-        )
-        normed_all = [across(normed_two, PAIR * k) if k else normed_two for k in range(chips)]
-        fed = [feed([k], [normed_all[k]])[0] for k in range(chips)]
-        received = [across(fed[k][3], PAIR * k) for k in range(1, chips)]
-    hidden_all, gate_back, up_back, backs, grad_all = map(list, zip(*fed))
-    down_keeps, down_sends = weight_grad(ids, hidden_all, [grad_all], PAIR, 2)
-    both = join(down_sends, gate_back[0], *received)
-    down_sends, gate_back[0], received = both[0], both[1], both[2:]
-
-    down_other = across(down_sends[0, 0], 1)
+        fed = [feed_back([k])[0] for k in range(chips)]
+        received = [across(fed[k][2], PAIR * k) for k in range(1, chips)]
+        down_own = (down_keeps[0, 0].astype(f32) + down_other).astype(bf16)
+        down_part = lax.psum_scatter(down_own, "ctx", scatter_dimension=0, tiled=True)
+    gate_back, up_back, backs = map(list, zip(*fed))
+    keeps, sends = weight_grad(ids, normed_all, [gate_back, up_back], shards)
+    down_part, sends, *received = join(down_part, sends, *received)
+
+    other = across(sends, 1)
+    down_parts = [down_part, rotate(down_part, -1)]
     norm_back = kernel_call(
         functools.partial(norm_back_kernel, count, chips),
         ids,
@@ -621,24 +655,20 @@
         [shape_of((rows, width), f32), shape_of((rows, width), bf16), shape_of((1, width), f32)]
         + [shape_of((rows, mixed_width), bf16)] * count,
     )
-    down_own = (down_keeps[0, 0].astype(f32) + down_other).astype(bf16)
-    both = join(down_own, gate_back[0], *norm_back)
-    down_own, gate_back[0], norm_back = both[0], both[1], both[2:]
+    both = join(other, *down_parts, *norm_back)
+    other, down_parts, norm_back = both[0], both[1:3], both[3:]
     grad_middle, grad_branch, grad_gain_two = norm_back[:3]
 
-    down_part = lax.psum_scatter(down_own, "ctx", scatter_dimension=0, tiled=True)
     grad_parts = rotated(norm_back[3:])
-    keeps, sends = weight_grad(ids, normed_all, [gate_back, up_back], shards)
+    gate_up_own = [(keeps[k].astype(f32) + other[k]).astype(bf16) for k in range(chips)]
     out_keeps, out_sends = weight_grad(ids, [mixed], [[grad_branch]], shards)
-    downs = kernel_call(
-        functools.partial(down_kernel, chips),
-        ids,
-        hidden_all + [down_w],
-        [shape_of((rows, width), bf16)] * chips,
-    )
-    both = join(sends, out_sends, *grad_parts, *downs)
-    sends, out_sends, grad_parts, downs = both[0], both[1], both[2 : 2 + count], both[2 + count :]
-    other, out_other = across(sends, 1), across(out_sends[:, 0], 1)
+    out_other = across(out_sends[:, 0], 1)
+    out_own = [(out_keeps[k, 0].astype(f32) + out_other[k]).astype(bf16) for k in range(chips)]
+    both = join(down_part, *gate_up_own, *out_own, *grad_parts)
+    down_part, gate_up_own, both = both[0], both[1 : 1 + chips], both[1 + chips :]
+    out_own, grad_parts = both[:chips], both[chips:]
+    down_parts += [rotate(down_part, -step) for step in range(2, count - 1)]
+    gate_up_rows = chip_exchange(gate_up_own)[:early]
     grad_parts = [a.reshape(batch, group, mixed_width) for a in grad_parts]
     grad_qkv = block_call(
         functools.partial(attend_back_kernel, count, heads, head_size),
@@ -646,14 +676,18 @@
         qkv + grad_parts,
         qkv_width,
     )
-    gate_up_own = [(keeps[k].astype(f32) + other[k]).astype(bf16) for k in range(chips)]
-    both = join(down_part, out_other, *grad_qkv, *gate_up_own)
-    down_part, out_other, grad_qkv = both[0], both[1], both[2 : 2 + count]
-    gate_up_rows = chip_exchange(both[2 + count :])
+    both = join(down_part, gate_up_own[-1], *gate_up_rows, *grad_qkv, *down_parts)
+    down_part, gate_up_own[-1], gate_up_rows, both = *both[:2], both[2 : 2 + early], both[2 + early :]
+    grad_qkv, down_parts = both[:count], both[count:]
+    gate_up_rows += chip_exchange(gate_up_own)[early:]
     grad_qkv = returned(grad_qkv)
-    down_whole = lax.all_gather(down_part, "ctx", axis=0, tiled=True)
-    both = join(out_other, *grad_qkv, *gate_up_rows[:early])
-    out_other, grad_qkv, gate_up_rows[:early] = both[0], both[1 : 1 + count], both[1 + count :]
+    gate_up_sent = jnp.stack(gate_up_rows).reshape(-1, hidden_width)
+    both = join(gate_up_sent, down_part, *out_own, *grad_qkv)
+    gate_up_sent, down_part, out_own, grad_qkv = *both[:2], both[2 : 2 + chips], both[2 + chips :]
+
+    gate_up_part = lax.psum_scatter(gate_up_sent, "ctx", scatter_dimension=0, tiled=True)
+    down_parts += [rotate(down_part, -step) for step in range(max(2, count - 1), count)]
+    out_rows = chip_exchange(out_own)[:early]
     grad_qkv, grad_gated = kernel_call(
         functools.partial(project_back_kernel, count, shards, heads),
         ids,
@@ -667,14 +701,11 @@
         anywhere=range(count, count + shards),
     )
     qkv_keeps, qkv_sends = weight_grad(ids, [gated], [[grad_qkv]], shards)
-    gate_up_sent = jnp.stack(gate_up_rows).reshape(-1, hidden_width)
-    qkv_sends, grad_gated, gate_up_sent = join(qkv_sends, grad_gated, gate_up_sent)
-
-    gate_up_part = lax.psum_scatter(gate_up_sent, "ctx", scatter_dimension=0, tiled=True)
+    both = join(qkv_sends, grad_gated, out_own[-1], down_w, *out_rows)
+    qkv_sends, grad_gated, out_own[-1], down_w, out_rows = *both[:4], both[4:]
+    out_rows += chip_exchange(out_own)[early:]
+    ordered = [(place + step) % count for step in range(count)]
     qkv_other = across(qkv_sends[:, 0], 1)
-    out_own = [(out_keeps[k, 0].astype(f32) + out_other[k]).astype(bf16) for k in range(chips)]
-    out_rows = chip_exchange(out_own)
-
     grad_gated = grad_gated.reshape(batch, group, width)
     grad_conv = grad_gated * gate_act
     grad_normed = grad_gated * conv_out * sig_one * (1.0 + normed * (1.0 - sig_one))
@@ -691,6 +722,8 @@
     )
     later_rows = along(grad_ext[:, :2], -1)
     qkv_own = [(qkv_keeps[k, 0].astype(f32) + qkv_other[k]).astype(bf16) for k in range(chips)]
+    both = join(later_rows, down_w, *qkv_own, *out_rows)
+    later_rows, down_w, qkv_own, out_rows = *both[:2], both[2 : 2 + chips], both[2 + chips :]
     grad_normed = grad_normed + grad_ext[:, 2:] + padded(later_rows, group - 2, 0)
     residual = inputs.astype(f32)
     scale_own = scale_ext[:, 2:]
@@ -704,23 +737,34 @@
     ).astype(bf16)
     zero = jnp.zeros_like(grad_gain_one)
     small = jnp.stack([grad_gain_one, grad_gain_two[0]] + grad_taps + [zero, zero, zero])
+    qkv_rows = chip_exchange(qkv_own)
     small = small + across(small, 1)
-    small, grad_rows, *qkv_own = join(small, grad_rows, *qkv_own)
+    out_sum = total(out_rows).astype(bf16).reshape(count, part_rows, width)
+    out_parts = rotated([pick(out_sum, at) for at in ordered])
+
+    both = join(gate_up_part, small, *down_parts, *qkv_rows, *out_parts)
+    gate_up_part, small, both = both[0], both[1], both[2:]
+    down_parts, qkv_rows, out_parts = both[:count], both[count:][:chips], both[count + chips :]
+    gate_up_whole = lax.all_gather(gate_up_part, "ctx", axis=0, tiled=True)
     small = total([small] + [across(small, PAIR * k) for k in range(1, chips)])
-    small = lax.dynamic_slice_in_dim(small, mine * own_rows, own_rows, 1).T
-    qkv_rows = chip_exchange(qkv_own)
-
-    both = join(gate_up_part, small, *qkv_rows, *out_rows)
-    gate_up_part, small, qkv_rows, out_rows = both[0], both[1], both[2 : 2 + chips], both[2 + chips :]
-    gate_up_whole = lax.all_gather(gate_up_part, "ctx", axis=0, tiled=True)
-    small = jnp.pad(small, ((0, 0), (0, 120)))
-    summed = jnp.concatenate([total(qkv_rows), total(out_rows), small], -1).astype(bf16)
-    parts = summed.reshape(count, part_rows, summed.shape[1])
-    ordered = [(place + step) % count for step in range(count)]
-    parts = join(*rotated([pick(parts, at) for at in ordered]))
-    part = total(parts).astype(bf16)
+    small = lax.dynamic_slice_in_dim(small, mine * own_rows, own_rows, 1)
+    parts = total(qkv_rows).astype(bf16).reshape(count, part_rows, total_width)
+    parts = rotated([pick(parts, at) for at in ordered])
+    out_parts = returned([total(out_parts).astype(bf16)] * count)
+    down_whole = placed(down_parts, ordered).reshape(w_down.shape)
+    both = join(small, total(parts).astype(bf16), down_w, *hidden_all, *out_parts)
+    small, part, down_w, both = *both[:3], both[3:]
+    hidden_all, out_parts = both[:chips], both[chips:]
+    small = total(rotated([small] * count))
     parts = returned([part] * count)
-    whole = placed(parts, ordered).reshape(own_rows, summed.shape[1]).astype(f32)
+    whole = placed(parts, ordered).reshape(own_rows, total_width).astype(f32)
+    grad_wout = placed(out_parts, ordered).reshape(own_rows, width).astype(f32)
+    downs = kernel_call(
+        functools.partial(down_kernel, chips),
+        ids,
+        [*hidden_all, down_w],
+        [shape_of((rows, width), bf16)] * chips,
+    )
     result = (middle + keep * total(chip_exchange(downs))).astype(bf16)
     gate_up_whole = gate_up_whole.reshape(chips, 2, own_rows, hidden_width)
     grad_w_gate, grad_w_up = kernel_call(
@@ -729,7 +773,6 @@
         [gate_up_whole],
         [shape_of(w_gate.shape, f32)] * 2,
     )
-    small = whole[:, total_width + width :].T
     features = HEADS * FEAT
     return (
         result.reshape(batch, 1, group, width),
@@ -738,8 +781,8 @@
         small[2:5],
         whole[:, :features],
         whole[:, features : 2 * features],
-        whole[:, 2 * features : total_width],
-        whole[:, total_width : total_width + width],
+        whole[:, 2 * features :],
+        grad_wout,
         small[1],
         grad_w_gate,
         grad_w_up,

time: 768 us -> 707 us (0.921)
  waiting for transfers between devices: 336 us -> 276 us
  local copies, waits for them, and re-layouts: 62.8 us -> 103 us
  Pallas kernels: 164 us -> 137 us
  other arithmetic: 53.2 us -> 40.9 us
    ppermute x42, waiting for transfers between devices: 153 us -> 84.8 us  [across(): return lax.ppermute(value, 'fsdp', [(i, i ^ mask) for i in range(count)])]
    unnamed x204 -> x250, local copies, waits for them, and re-layouts: 43.9 us -> 87.4 us
    pallas_call x10 -> x11, Pallas kernels: 95 us -> 65.6 us  [kernel_call(): pl.pallas_call(kernel, out_shape=list(outs), in_specs=specs, out_specs=[w...]
    reduce_scatter x1, waiting for transfers between devices: 16.3 us -> 0.01 us  [local(): lax.psum_scatter(down_own, 'ctx', scatter_dimension=0, tiled=True)]
    ppermute x18 -> x30, waiting for transfers between devices: 147 us -> 159 us  [rotate(): lax.ppermute(value, 'ctx', [(i, (i + steps) % count) for i in range(count)])]
    reduce_scatter x1, waiting for transfers between devices: 0.02 us -> 8.36 us  [local(): lax.psum_scatter(gate_up_sent, 'ctx', scatter_dimension=0, tiled=True)]
    pallas_call x4, Pallas kernels: 33.4 us -> 41.2 us  [weight_grad(): pl.pallas_call(functools.partial(weight_grad_kernel, blocks, groups, part...]
    ppermute x18 -> x30, starting transfers between devices: 81.1 us -> 86.8 us  [rotate(): lax.ppermute(value, 'ctx', [(i, (i + steps) % count) for i in range(count)])]
  transfers between devices with their start and end apart: 70 -> 81, of which waited for: 31 -> 32; matrix products, arithmetic and copies ran while one was open for 9% -> 8% of each run, Pallas kernels for 19% -> 14%
where the time goes in v2:
time: 707 us; the launch traced here: 703 us
  waiting for transfers between devices  276 us (39%)
  Pallas kernels  137 us (19%)
  starting transfers between devices  130 us (18%)
  local copies, waits for them, and re-layouts  103 us (15%)
  other arithmetic  40.9 us (6%)
  between operations  15.5 us (2%)
    ppermute x30, waiting for transfers between devices, rotate(): lax.ppermute(value, 'ctx', [(i, (i + steps) % count) for i in range(count)])  159 us
    unnamed x250, local copies, waits for them, and re-layouts  87.4 us
    ppermute x30, starting transfers between devices, rotate(): lax.ppermute(value, 'ctx', [(i, (i + steps) % count) for i in range(count)])  86.8 us
    ppermute x42, waiting for transfers between devices, across(): return lax.ppermute(value, 'fsdp', [(i, i ^ mask) for i in range(count)])  84.8 us
    pallas_call x11, Pallas kernels, kernel_call(): pl.pallas_call(kernel, out_shape=list(outs), in_specs=specs, out_specs=[w...  65.6 us
    pallas_call x4, Pallas kernels, weight_grad(): pl.pallas_call(functools.partial(weight_grad_kernel, blocks, groups, part...  41.2 us
    ppermute x42, starting transfers between devices, across(): return lax.ppermute(value, 'fsdp', [(i, i ^ mask) for i in range(count)])  36.6 us
    pallas_call x2, Pallas kernels, block_call(): pl.pallas_call(kernel, out_shape=[out] * count, grid=(batch,), in_specs=[...  24.9 us
  transfers between devices with their start and end apart: 81, of which 32 were waited for; matrix products, arithmetic and copies ran while one was open for 8% of the time, Pallas kernels for 14%

profile of v2, /device:TPU:0, one launch (start us, length us, event | category | flops | bytes accessed | tf_op | source)
XLA Modules:
  0.0 703.3 jit_solution(1337122663173037476)
XLA Ops:
  31.1 7.6 %collective-permute-done.1 = bf16[2,8,224]{2,1,0:T(8,128)(2,1)S(1)} collective-permute-done((bf16[2,8,224]{2,1,0:T(8,128)(2,1)S(1)}, bf16[2,8,224]{2,1,0:T(8,128)(2,1)S(1)}, u32[]{:S(2)}, u32[]{:S(2)}) %collective-permute-start.1) | collective-permute-done | bytes 7200 | tf_op jit(solution)/shard_map/ppermute | solution.py:50
  44.2 12.3 %collective-permute-done.2 = bf16[4,8,224]{2,1,0:T(8,128)(2,1)S(1)} collective-permute-done((bf16[4,8,224]{2,1,0:T(8,128)(2,1)S(1)}, bf16[4,8,224]{2,1,0:T(8,128)(2,1)S(1)}, u32[]{:S(2)}, u32[]{:S(2)}) %collective-permute-start.2) | collective-permute-done | bytes 14368 | tf_op jit(solution)/shard_map/ppermute | solution.py:50
  83.5 13.7 %collective-permute-done.14 = bf16[256,576]{1,0:T(8,128)(2,1)} collective-permute-done((bf16[256,576]{1,0:T(8,128)(2,1)}, bf16[256,576]{1,0:T(8,128)(2,1)}, u32[]{:S(2)}, u32[]{:S(2)}) %collective-permute-start.14) | collective-permute-done | bytes 294944 | tf_op jit(solution)/shard_map/ppermute | solution.py:45
  97.2 8.1 %shard_map.222 = (bf16[2,128,448]{2,1,0:T(8,128)(2,1)S(1)}, bf16[2,128,448]{2,1,0:T(8,128)(2,1)S(1)}, bf16[2,128,448]{2,1,0:T(8,128)(2,1)S(1)}, bf16[2,128,448]{2,1,0:T(8,128)(2,1)S(1)}) custom-call(s32[2]{0:T(128)S(1)} %pad_add_fusion.2.ids.place_ref, bf16[2,128,576]{2,1,0:T(8,128)(2,1)S(1)} %bitcast.215, bf16[2,128,576]{2,1,0:T(8,128)(2,1)} %bitcast.13.refs_1_, ...), custom_call_target="tpu_custom_call" | custom-call | tf_op jit(solution)/shard_map/pallas_call | solution.py:461
  108.5 8.5 %collective-permute-start.17 = (bf16[2,128,448]{2,1,0:T(8,128)(2,1)S(1)}, bf16[2,128,448]{2,1,0:T(8,128)(2,1)S(1)}, u32[]{:S(2)}, u32[]{:S(2)}) collective-permute-start(bf16[2,128,448]{2,1,0:T(8,128)(2,1)S(1)} %get-tuple-element.265), channel_id=1, source_target_pairs={{0,24},{8,0},{16,8},{24,16},{1,25},{9,1},{17,9},{25,17},{2,26},{10... | collective-permute-start | bytes 688136 | tf_op jit(solution)/shard_map/ppermute | solution.py:45
  124.5 12.9 %collective-permute-start.19 = (bf16[2,128,448]{2,1,0:T(8,128)(2,1)S(1)}, bf16[2,128,448]{2,1,0:T(8,128)(2,1)S(1)}, u32[]{:S(2)}, u32[]{:S(2)}) collective-permute-start(bf16[2,128,448]{2,1,0:T(8,128)(2,1)S(1)} %get-tuple-element.267), channel_id=1, source_target_pairs={{0,8},{8,16},{16,24},{24,0},{1,9},{9,17},{17,25},{25,1},{2,10},{10... | collective-permute-start | bytes 688136 | tf_op jit(solution)/shard_map/ppermute | solution.py:45
  180.0 19.4 %collective-permute-done.25.rest_1_ = bf16[256,1792]{1,0:T(8,128)(2,1)S(1)} collective-permute-done((bf16[256,1792]{1,0:T(8,128)(2,1)S(1)}, bf16[256,1792]{1,0:T(8,128)(2,1)S(1)}, u32[]{:S(2)}, u32[]{:S(2)}) %collective-permute-start.25) | collective-permute-done | bytes 917536 | tf_op jit(solution)/shard_map/ppermute | solution.py:50
  202.9 15.8 %all-gather.9.cloned.1.call-done = bf16[1024,1792]{1,0:T(8,128)(2,1)} async-done(((bf16[256,1792]{1,0:T(8,128)(2,1)}), bf16[1024,1792]{1,0:T(8,128)(2,1)}) %all-gather.9.cloned.1.call-update) | async-done | bytes 3670032 | tf_op jit(solution)/shard_map/all_gather | solution.py:553
  226.6 11.0 %shard_map.225 = (bf16[256,1216]{1,0:T(8,128)(2,1)S(1)}, bf16[256,1216]{1,0:T(8,128)(2,1)S(1)}, bf16[256,1216]{1,0:T(8,128)(2,1)S(1)}, bf16[256,1216]{1,0:T(8,12...) custom-call(s32[2]{0:T(128)S(1)} %pad_add_fusion.2.ids.place_ref, ...), custom_call_target="tpu_custom_call" | custom-call | tf_op jit(solution)/shard_map/pallas_call | solution.py:94
  239.5 19.6 %shard_map.226 = (bf16[1,1,608,1792]{3,2,1,0:T(8,128)(2,1)S(1)}, bf16[1,1,608,1792]{3,2,1,0:T(8,128)(2,1)S(1)}) custom-call(s32[2]{0:T(128)S(1)} %pad_add_fusion.2.ids.place_ref, bf16[256,1216]{1,0:T(8,128)(2,1)S(1)} %get-tuple-element.429.rest_0_, bf16[256,1216]{1,0:T(8,128)(2,1)S(1)} %get-tuple-element.430.rest_1_, ...), custom_call_target="tpu_custom_call" | custom-call | tf_op jit(solution)/shard_map/pallas_call | solution.py:353
  286.0 9.6 %shard_map.228 = (bf16[256,1216]{1,0:T(8,128)(2,1)S(1)}, bf16[256,1216]{1,0:T(8,128)(2,1)S(1)}, bf16[256,1792]{1,0:T(8,128)(2,1)}, bf16[256,1216]{1,0:T(8,128)(2...) custom-call(s32[2]{0:T(128)S(1)} %pad_add_fusion.2.ids.place_ref, ...), custom_call_target="tpu_custom_call" | custom-call | tf_op jit(solution)/shard_map/pallas_call | solution.py:94
  303.7 13.4 %shard_map.230 = (bf16[4,2,224,1216]{3,2,1,0:T(8,128)(2,1)S(1)}, bf16[4,2,224,1216]{3,2,1,0:T(8,128)(2,1)S(1)}) custom-call(s32[2]{0:T(128)S(1)} %pad_add_fusion.2.ids.place_ref, bf16[256,1792]{1,0:T(8,128)(2,1)S(1)} %copy-done.44, bf16[256,1792]{1,0:T(8,128)(2,1)S(1)} %copy-done.18, bf16[256,1792]{1,0:T(8,128)(2,1)S(1)} %copy-done.21, ...), custom_call_target="tpu_custom_call" | custom-call | tf_op jit(solution)/shard_map/pallas_call | solution.py:353
  358.5 10.2 %collective-permute-done.36 = bf16[256,448]{1,0:T(8,128)(2,1)S(1)} collective-permute-done((bf16[256,448]{1,0:T(8,128)(2,1)S(1)}, bf16[256,448]{1,0:T(8,128)(2,1)S(1)}, u32[]{:S(2)}, u32[]{:S(2)}) %collective-permute-start.36) | collective-permute-done | bytes 229408 | tf_op jit(solution)/shard_map/ppermute | solution.py:45
  375.1 16.7 %shard_map.233 = (bf16[2,128,576]{2,1,0:T(8,128)(2,1)S(1)}, bf16[2,128,576]{2,1,0:T(8,128)(2,1)S(1)}, bf16[2,128,576]{2,1,0:T(8,128)(2,1)S(1)}, bf16[2,128,576]{2,1,0:T(8,128)(2,1)S(1)}) custom-call(s32[2]{0:T(128)S(1)} %pad_add_fusion.2.ids.place_ref, bf16[2,128,576]{2,1,0:T(8,128)(2,1)S(1)} %bitcast.216, bf16[2,128,576]{2,1,0:T(8,128)(2,1)} %bitcast.13.refs_1_, ...), custom_call_target="tpu_custom_call" | custom-call | tf_op jit(solution)/shard_map/pallas_call | solution.py:461
  404.8 20.5 %collective-permute-done.41 = bf16[2,224,1216]{2,1,0:T(8,128)(2,1)S(1)} collective-permute-done((bf16[2,224,1216]{2,1,0:T(8,128)(2,1)S(1)}, bf16[2,224,1216]{2,1,0:T(8,128)(2,1)S(1)}, u32[]{:S(2)}, u32[]{:S(2)}) %collective-permute-start.41) | collective-permute-done | bytes 1089568 | tf_op jit(solution)/shard_map/ppermute | solution.py:50
  471.0 9.5 %collective-permute-done.49 = bf16[224,1792]{1,0:T(8,128)(2,1)S(1)} collective-permute-done((bf16[224,1792]{1,0:T(8,128)(2,1)S(1)}, bf16[224,1792]{1,0:T(8,128)(2,1)S(1)}, u32[]{:S(2)}, u32[]{:S(2)}) %collective-permute-start.49) | collective-permute-done | bytes 802848 | tf_op jit(solution)/shard_map/ppermute | solution.py:50
  494.3 9.6 %collective-permute-done.55 = bf16[56,1792]{1,0:T(8,128)(2,1)S(1)} collective-permute-done((bf16[56,1792]{1,0:T(8,128)(2,1)S(1)}, bf16[56,1792]{1,0:T(8,128)(2,1)S(1)}, u32[]{:S(2)}, u32[]{:S(2)}) %collective-permute-start.55) | collective-permute-done | bytes 200736 | tf_op jit(solution)/shard_map/ppermute | solution.py:45
  510.1 9.1 %collective-permute-done.56 = bf16[56,1792]{1,0:T(8,128)(2,1)S(1)} collective-permute-done((bf16[56,1792]{1,0:T(8,128)(2,1)S(1)}, bf16[56,1792]{1,0:T(8,128)(2,1)S(1)}, u32[]{:S(2)}, u32[]{:S(2)}) %collective-permute-start.56) | collective-permute-done | bytes 200736 | tf_op jit(solution)/shard_map/ppermute | solution.py:45
  519.2 8.4 %collective-permute-done.57 = bf16[56,1792]{1,0:T(8,128)(2,1)S(1)} collective-permute-done((bf16[56,1792]{1,0:T(8,128)(2,1)S(1)}, bf16[56,1792]{1,0:T(8,128)(2,1)S(1)}, u32[]{:S(2)}, u32[]{:S(2)}) %collective-permute-start.57) | collective-permute-done | bytes 200736 | tf_op jit(solution)/shard_map/ppermute | solution.py:45
  532.1 8.4 %reduce-scatter.5.cloned.1.call-done = bf16[448,1216]{1,0:T(8,128)(2,1)} async-done(((bf16[1792,1216]{1,0:T(8,128)(2,1)}), bf16[448,1216]{1,0:T(8,128)(2,1)}) %reduce-scatter.5.cloned.1.call-update) | async-done | bytes 1089552 | tf_op jit(solution)/shard_map/reduce_scatter | solution.py:688
  562.9 15.0 %collective-permute-start.66 = (bf16[56,1792]{1,0:T(8,128)(2,1)S(1)}, bf16[56,1792]{1,0:T(8,128)(2,1)S(1)}, u32[]{:S(2)}, u32[]{:S(2)}) collective-permute-start(bf16[56,1792]{1,0:T(8,128)(2,1)S(1)} %add_convert_fusion.7), channel_id=1, source_target_pairs={{0,8},{8,16},{16,24},{24,0},{1,9},{9,17},{17,25},{25,1},{2,10},{10... | collective-permute-start | bytes 602120 | tf_op jit(solution)/shard_map/ppermute | solution.py:45
  577.9 28.3 %collective-permute-done.62 = bf16[56,2304]{1,0:T(8,128)(2,1)S(1)} collective-permute-done((bf16[56,2304]{1,0:T(8,128)(2,1)S(1)}, bf16[56,2304]{1,0:T(8,128)(2,1)S(1)}, u32[]{:S(2)}, u32[]{:S(2)}) %collective-permute-start.62) | collective-permute-done | bytes 258080 | tf_op jit(solution)/shard_map/ppermute | solution.py:45
  606.3 31.3 %collective-permute-done.65 = bf16[56,1792]{1,0:T(8,128)(2,1)S(1)} collective-permute-done((bf16[56,1792]{1,0:T(8,128)(2,1)S(1)}, bf16[56,1792]{1,0:T(8,128)(2,1)S(1)}, u32[]{:S(2)}, u32[]{:S(2)}) %collective-permute-start.65) | collective-permute-done | bytes 200736 | tf_op jit(solution)/shard_map/ppermute | solution.py:45
  657.5 24.8 %collective-permute-done.74 = bf16[56,2304]{1,0:T(8,128)(2,1)S(1)} collective-permute-done((bf16[56,2304]{1,0:T(8,128)(2,1)S(1)}, bf16[56,2304]{1,0:T(8,128)(2,1)S(1)}, u32[]{:S(2)}, u32[]{:S(2)}) %collective-permute-start.74) | collective-permute-done | bytes 258080 | tf_op jit(solution)/shard_map/ppermute | solution.py:45
  (511 shorter events, 343.9 us)
Async XLA Ops:
  7.2 144.0 %all-gather.5.cloned.1.call-start = ((), (), s32[]{:S(2)}) async-start(), calls=%async_computation.2 | async-start | bytes 7225344 | tf_op jit(solution)/shard_map/all_gather | solution.py:551
  17.0 40.2 %collective-permute-start.7 = (bf16[224,2304]{1,0:T(8,128)(2,1)}, bf16[224,2304]{1,0:T(8,128)(2,1)}, u32[]{:S(2)}, u32[]{:S(2)}) collective-permute-start(bf16[224,2304]{1,0:T(8,128)(2,1)} %constant_dynamic-update-slice_fusion.rest_0_.rest_4_), channel_id=1, source_target_pairs={{0,1},{1,0},{2,3},{3,2},{4,5},{5,4},{6,7},{7,6},{8,9},{9,8},{10,11... | collective-permute-start | bytes 3096584 | tf_op jit(solution)/shard_map/ppermute | solution.py:50
  61.2 157.5 %all-gather.9.cloned.1.call-start = ((), (), s32[]{:S(2)}) async-start(), calls=%async_computation.6 | async-start | bytes 4587520 | tf_op jit(solution)/shard_map/all_gather | solution.py:553
  80.0 62.0 %collective-permute-start.11 = (bf16[2,224,1216]{2,1,0:T(8,128)(2,1)}, bf16[2,224,1216]{2,1,0:T(8,128)(2,1)}, u32[]{:S(2)}, u32[]{:S(2)}) collective-permute-start(bf16[2,224,1216]{2,1,0:T(8,128)(2,1)} %get-tuple-element.498), channel_id=1, source_target_pairs={{0,2},{1,3},{2,0},{3,1},{4,6},{5,7},{6,4},{7,5},{8,10},{9,11},{10,... | collective-permute-start | bytes 3268616 | tf_op jit(solution)/shard_map/ppermute | solution.py:50
  80.8 67.7 %collective-permute-start.12 = (bf16[2,224,1216]{2,1,0:T(8,128)(2,1)}, bf16[2,224,1216]{2,1,0:T(8,128)(2,1)}, u32[]{:S(2)}, u32[]{:S(2)}) collective-permute-start(bf16[2,224,1216]{2,1,0:T(8,128)(2,1)} %get-tuple-element.497), channel_id=1, source_target_pairs={{0,4},{1,5},{2,6},{3,7},{4,0},{5,1},{6,2},{7,3},{8,12},{9,13},{10,... | collective-permute-start | bytes 3268616 | tf_op jit(solution)/shard_map/ppermute | solution.py:50
  82.3 241.0 %reduce-scatter.3.cloned.1.call-start = ((), (), s32[]{:S(2)}) async-start(), calls=%async_computation.3 | async-start | bytes 2723840 | tf_op jit(solution)/shard_map/reduce_scatter | solution.py:633
  106.8 43.1 %collective-permute-start.16 = (bf16[2,224,1216]{2,1,0:T(8,128)(2,1)S(1)}, bf16[2,224,1216]{2,1,0:T(8,128)(2,1)}, u32[]{:S(2)}, u32[]{:S(2)}) collective-permute-start(bf16[2,224,1216]{2,1,0:T(8,128)(2,1)S(1)} %slice_bitcast_fusion), channel_id=1, source_target_pairs={{0,6},{1,7},{2,4},{3,5},{4,2},{5,3},{6,0},{7,1},{8,14},{9,15},{10,... | collective-permute-start | bytes 3268616 | tf_op jit(solution)/shard_map/ppermute | solution.py:50
  165.7 33.7 %collective-permute-start.25 = (bf16[256,1792]{1,0:T(8,128)(2,1)S(1)}, bf16[256,1792]{1,0:T(8,128)(2,1)S(1)}, u32[]{:S(2)}, u32[]{:S(2)}) collective-permute-start(bf16[256,1792]{1,0:T(8,128)(2,1)S(1)} %get-tuple-element.280.rest_0_), channel_id=1, source_target_pairs={{0,2},{1,3},{2,0},{3,1},{4,6},{5,7},{6,4},{7,5},{8,10},{9,11},{10,... | collective-permute-start | bytes 2752520 | tf_op jit(solution)/shard_map/ppermute | solution.py:50
  166.5 34.0 %collective-permute-start.26 = (bf16[256,1792]{1,0:T(8,128)(2,1)S(1)}, bf16[256,1792]{1,0:T(8,128)(2,1)S(1)}, u32[]{:S(2)}, u32[]{:S(2)}) collective-permute-start(bf16[256,1792]{1,0:T(8,128)(2,1)S(1)} %get-tuple-element.280.rest_0_), channel_id=1, source_target_pairs={{0,4},{1,5},{2,6},{3,7},{4,0},{5,1},{6,2},{7,3},{8,12},{9,13},{10,... | collective-permute-start | bytes 2752520 | tf_op jit(solution)/shard_map/ppermute | solution.py:50
  270.8 269.6 %reduce-scatter.5.cloned.1.call-start = ((), (), s32[]{:S(2)}) async-start(), calls=%async_computation.4 | async-start | bytes 5734400 | tf_op jit(solution)/shard_map/reduce_scatter | solution.py:688
  432.9 256.6 %all-gather.7.cloned.1.call-start = ((), (), s32[]{:S(2)}) async-start(), calls=%async_computation.5 | async-start | bytes 5734400 | tf_op jit(solution)/shard_map/all_gather | solution.py:748
  453.3 36.0 %collective-permute-start.51 = (bf16[152,1792]{1,0:T(8,128)(2,1)}, bf16[152,1792]{1,0:T(8,128)(2,1)}, u32[]{:S(2)}, u32[]{:S(2)}) collective-permute-start(bf16[152,1792]{1,0:T(8,128)(2,1)} %reduce-scatter.3.cloned.1.call-done), channel_id=1, source_target_pairs={{0,8},{8,16},{16,24},{24,0},{1,9},{9,17},{17,25},{25,1},{2,10},{10... | collective-permute-start | bytes 1634312 | tf_op jit(solution)/shard_map/ppermute | solution.py:45
  483.3 44.3 %collective-permute-start.52 = (bf16[224,2304]{1,0:T(8,128)(2,1)}, bf16[224,2304]{1,0:T(8,128)(2,1)}, u32[]{:S(2)}, u32[]{:S(2)}) collective-permute-start(bf16[224,2304]{1,0:T(8,128)(2,1)} %get-tuple-element.412), channel_id=1, source_target_pairs={{0,2},{1,3},{2,0},{3,1},{4,6},{5,7},{6,4},{7,5},{8,10},{9,11},{10,... | collective-permute-start | bytes 3096584 | tf_op jit(solution)/shard_map/ppermute | solution.py:50
  484.7 47.3 %collective-permute-start.53 = (bf16[224,2304]{1,0:T(8,128)(2,1)}, bf16[224,2304]{1,0:T(8,128)(2,1)}, u32[]{:S(2)}, u32[]{:S(2)}) collective-permute-start(bf16[224,2304]{1,0:T(8,128)(2,1)} %get-tuple-element.413), channel_id=1, source_target_pairs={{0,4},{1,5},{2,6},{3,7},{4,0},{5,1},{6,2},{7,3},{8,12},{9,13},{10,... | collective-permute-start | bytes 3096584 | tf_op jit(solution)/shard_map/ppermute | solution.py:50
  485.9 46.2 %collective-permute-start.54 = (bf16[224,2304]{1,0:T(8,128)(2,1)}, bf16[224,2304]{1,0:T(8,128)(2,1)}, u32[]{:S(2)}, u32[]{:S(2)}) collective-permute-start(bf16[224,2304]{1,0:T(8,128)(2,1)} %get-tuple-element.414), channel_id=1, source_target_pairs={{0,6},{1,7},{2,4},{3,5},{4,2},{5,3},{6,0},{7,1},{8,14},{9,15},{10,... | collective-permute-start | bytes 3096584 | tf_op jit(solution)/shard_map/ppermute | solution.py:50
  548.3 57.9 %collective-permute-start.62 = (bf16[56,2304]{1,0:T(8,128)(2,1)S(1)}, bf16[56,2304]{1,0:T(8,128)(2,1)S(1)}, u32[]{:S(2)}, u32[]{:S(2)}) collective-permute-start(bf16[56,2304]{1,0:T(8,128)(2,1)S(1)} %get-tuple-element.511), channel_id=1, source_target_pairs={{0,16},{8,24},{16,0},{24,8},{1,17},{9,25},{17,1},{25,9},{2,18},{10... | collective-permute-start | bytes 774152 | tf_op jit(solution)/shard_map/ppermute | solution.py:45
  558.8 47.4 %collective-permute-start.61 = (bf16[56,2304]{1,0:T(8,128)(2,1)S(1)}, bf16[56,2304]{1,0:T(8,128)(2,1)S(1)}, u32[]{:S(2)}, u32[]{:S(2)}) collective-permute-start(bf16[56,2304]{1,0:T(8,128)(2,1)S(1)} %get-tuple-element.509), channel_id=1, source_target_pairs={{0,8},{8,16},{16,24},{24,0},{1,9},{9,17},{17,25},{25,1},{2,10},{10... | collective-permute-start | bytes 774152 | tf_op jit(solution)/shard_map/ppermute | solution.py:45
  558.9 47.4 %collective-permute-start.64 = (bf16[56,1792]{1,0:T(8,128)(2,1)S(1)}, bf16[56,1792]{1,0:T(8,128)(2,1)S(1)}, u32[]{:S(2)}, u32[]{:S(2)}) collective-permute-start(bf16[56,1792]{1,0:T(8,128)(2,1)S(1)} %add_convert_fusion.7), channel_id=1, source_target_pairs={{0,24},{8,0},{16,8},{24,16},{1,25},{9,1},{17,9},{25,17},{2,26},{10... | collective-permute-start | bytes 602120 | tf_op jit(solution)/shard_map/ppermute | solution.py:45
  562.8 74.9 %collective-permute-start.65 = (bf16[56,1792]{1,0:T(8,128)(2,1)S(1)}, bf16[56,1792]{1,0:T(8,128)(2,1)S(1)}, u32[]{:S(2)}, u32[]{:S(2)}) collective-permute-start(bf16[56,1792]{1,0:T(8,128)(2,1)S(1)} %add_convert_fusion.7), channel_id=1, source_target_pairs={{0,16},{8,24},{16,0},{24,8},{1,17},{9,25},{17,1},{25,9},{2,18},{10... | collective-permute-start | bytes 602120 | tf_op jit(solution)/shard_map/ppermute | solution.py:45
  562.9 74.8 %collective-permute-start.66 = (bf16[56,1792]{1,0:T(8,128)(2,1)S(1)}, bf16[56,1792]{1,0:T(8,128)(2,1)S(1)}, u32[]{:S(2)}, u32[]{:S(2)}) collective-permute-start(bf16[56,1792]{1,0:T(8,128)(2,1)S(1)} %add_convert_fusion.7), channel_id=1, source_target_pairs={{0,8},{8,16},{16,24},{24,0},{1,9},{9,17},{17,25},{25,1},{2,10},{10... | collective-permute-start | bytes 602120 | tf_op jit(solution)/shard_map/ppermute | solution.py:45
  642.2 40.0 %collective-permute-start.74 = (bf16[56,2304]{1,0:T(8,128)(2,1)S(1)}, bf16[56,2304]{1,0:T(8,128)(2,1)S(1)}, u32[]{:S(2)}, u32[]{:S(2)}) collective-permute-start(bf16[56,2304]{1,0:T(8,128)(2,1)S(1)} %fusion.25), channel_id=1, source_target_pairs={{0,16},{8,24},{16,0},{24,8},{1,17},{9,25},{17,1},{25,9},{2,18},{10... | collective-permute-start | bytes 774152 | tf_op jit(solution)/shard_map/ppermute | solution.py:45
  651.6 30.7 %collective-permute-start.75 = (bf16[56,2304]{1,0:T(8,128)(2,1)S(1)}, bf16[56,2304]{1,0:T(8,128)(2,1)S(1)}, u32[]{:S(2)}, u32[]{:S(2)}) collective-permute-start(bf16[56,2304]{1,0:T(8,128)(2,1)S(1)} %fusion.25), channel_id=1, source_target_pairs={{0,8},{8,16},{16,24},{24,0},{1,9},{9,17},{17,25},{25,1},{2,10},{10... | collective-permute-start | bytes 774152 | tf_op jit(solution)/shard_map/ppermute | solution.py:45
  652.8 31.8 %collective-permute-start.69 = (bf16[256,1792]{1,0:T(8,128)(2,1)S(1)}, bf16[256,1792]{1,0:T(8,128)(2,1)S(1)}, u32[]{:S(2)}, u32[]{:S(2)}) collective-permute-start(bf16[256,1792]{1,0:T(8,128)(2,1)S(1)} %get-tuple-element.436), channel_id=1, source_target_pairs={{0,6},{1,7},{2,4},{3,5},{4,2},{5,3},{6,0},{7,1},{8,14},{9,15},{10,... | collective-permute-start | bytes 2752520 | tf_op jit(solution)/shard_map/ppermute | solution.py:50
  655.2 29.9 %collective-permute-start.68 = (bf16[256,1792]{1,0:T(8,128)(2,1)S(1)}, bf16[256,1792]{1,0:T(8,128)(2,1)S(1)}, u32[]{:S(2)}, u32[]{:S(2)}) collective-permute-start(bf16[256,1792]{1,0:T(8,128)(2,1)S(1)} %get-tuple-element.435), channel_id=1, source_target_pairs={{0,4},{1,5},{2,6},{3,7},{4,0},{5,1},{6,2},{7,3},{8,12},{9,13},{10,... | collective-permute-start | bytes 2752520 | tf_op jit(solution)/shard_map/ppermute | solution.py:50
  (181 other events, 2052.6 us)
Sparse Core Ops, SparseCore 0:
  61.3 64.8 all-gather.4
  128.1 90.6 all-gather.8
  270.9 45.5 reduce-scatter.2
  433.0 107.3 reduce-scatter.4
  553.8 135.6 all-gather.6

commit v3 on v2

--- a/solution.py
+++ b/solution.py
@@ -549,8 +549,10 @@
     )
     qkv_pieces = interleaved(qkv_own, qkv_other)
     w_out_full = lax.all_gather(w_out, "fsdp", axis=0, tiled=True)
-    columns = [[i + PAIR * k for k in range(chips)] for i in range(PAIR)]
-    grad_all = lax.all_gather(grad_out, "fsdp", axis_index_groups=columns)
+    if chips == 4:
+        grad_all = [grad_out, across(grad_out, 2), across(grad_out, 4)]
+    else:
+        grad_all = [across(grad_out, PAIR * k) if k else grad_out for k in range(chips)]
 
     projected = kernel_call(
         functools.partial(project_kernel, count, shards, heads),
@@ -568,17 +570,20 @@
     early = max(1, chips - 1)
     gate_up = [across(packed[k], PAIR * k) if k else packed[0] for k in range(early)]
     qkv = rotated(projected)
-    qkv = join(*qkv)
+    both = join(*qkv, *grad_all)
+    qkv, grad_all = both[:count], both[count:]
     qkv = [a.reshape(batch, group, qkv_width) for a in qkv]
     mixed = block_call(
         functools.partial(attend_kernel, count, heads, head_size), ids, qkv, mixed_width
     )
     *mixed, packed = join(*mixed, packed)
+    mixed = returned(mixed)
+    relayed = jnp.where(core == 0, grad_all[1], grad_all[2]) if chips == 4 else grad_all.pop()
+    both = join(w_down, packed, relayed, *gate_up[:early], *mixed)
+    own_down, packed, relayed, gate_up, mixed = *both[:3], both[3 : 3 + early], both[3 + early :]
+    grad_all.append(diagonal(relayed) if chips == 4 else relayed)
+    siblings = swap([own_down, *gate_up])
     gate_up += [across(packed[k], PAIR * k) for k in range(early, chips)]
-    mixed = returned(mixed)
-    both = join(w_down, *gate_up, *mixed)
-    own_down, gate_up, mixed = both[0], both[1 : 1 + chips], both[1 + chips :]
-    siblings = swap([*gate_up, own_down])
     mixed, middle, normed_two = kernel_call(
         functools.partial(merge_kernel, count),
         ids,
@@ -587,7 +592,10 @@
         [shape_of((rows, width), kind) for kind in (bf16, f32, bf16)],
         scratch=[vmem((count, rows, mixed_width), bf16), vmem((rows, width), f32)],
     )
-    normed_two, other_down, *siblings = join(normed_two, siblings[-1], *siblings[:-1])
+    both = join(normed_two, grad_all[-1], *siblings, *gate_up[early:])
+    normed_two, grad_all[-1], other_down, both = *both[:3], both[3:]
+    siblings, gate_up[early:] = both[:early], both[early:]
+    siblings += swap(gate_up[early:])
 
     gate_w, up_w, down_w = arrange(
         ids, interleaved(gate_up, siblings), w_down, other_down, width
@@ -607,7 +615,6 @@
         vmem=32,
     )
     hidden_all, to_gate, to_up = fed[:chips], fed[chips : 2 * chips], fed[2 * chips :]
-    grad_all = [pick(grad_all, chip ^ k) for k in range(chips)]
 
     def feed_back(at):
         outs = kernel_call(
@@ -661,12 +668,8 @@
 
     grad_parts = rotated(norm_back[3:])
     gate_up_own = [(keeps[k].astype(f32) + other[k]).astype(bf16) for k in range(chips)]
-    out_keeps, out_sends = weight_grad(ids, [mixed], [[grad_branch]], shards)
-    out_other = across(out_sends[:, 0], 1)
-    out_own = [(out_keeps[k, 0].astype(f32) + out_other[k]).astype(bf16) for k in range(chips)]
-    both = join(down_part, *gate_up_own, *out_own, *grad_parts)
-    down_part, gate_up_own, both = both[0], both[1 : 1 + chips], both[1 + chips :]
-    out_own, grad_parts = both[:chips], both[chips:]
+    both = join(down_part, grad_branch, *gate_up_own, *grad_parts)
+    down_part, grad_branch, gate_up_own, grad_parts = *both[:2], both[2 : 2 + chips], both[2 + chips :]
     down_parts += [rotate(down_part, -step) for step in range(2, count - 1)]
     gate_up_rows = chip_exchange(gate_up_own)[:early]
     grad_parts = [a.reshape(batch, group, mixed_width) for a in grad_parts]
@@ -676,9 +679,12 @@
         qkv + grad_parts,
         qkv_width,
     )
-    both = join(down_part, gate_up_own[-1], *gate_up_rows, *grad_qkv, *down_parts)
-    down_part, gate_up_own[-1], gate_up_rows, both = *both[:2], both[2 : 2 + early], both[2 + early :]
-    grad_qkv, down_parts = both[:count], both[count:]
+    out_keeps, out_sends = weight_grad(ids, [mixed], [[grad_branch]], shards)
+    both = join(down_part, gate_up_own[-1], out_sends, *gate_up_rows, *grad_qkv, *down_parts)
+    down_part, gate_up_own[-1], out_sends, both = *both[:3], both[3:]
+    gate_up_rows, grad_qkv, down_parts = both[:early], both[early:][:count], both[early + count :]
+    out_other = across(out_sends[:, 0], 1)
+    out_own = [(out_keeps[k, 0].astype(f32) + out_other[k]).astype(bf16) for k in range(chips)]
     gate_up_rows += chip_exchange(gate_up_own)[early:]
     grad_qkv = returned(grad_qkv)
     gate_up_sent = jnp.stack(gate_up_rows).reshape(-1, hidden_width)
@@ -722,8 +728,8 @@
     )
     later_rows = along(grad_ext[:, :2], -1)
     qkv_own = [(qkv_keeps[k, 0].astype(f32) + qkv_other[k]).astype(bf16) for k in range(chips)]
-    both = join(later_rows, down_w, *qkv_own, *out_rows)
-    later_rows, down_w, qkv_own, out_rows = *both[:2], both[2 : 2 + chips], both[2 + chips :]
+    both = join(later_rows, down_w, *qkv_own, *out_rows[:early])
+    later_rows, down_w, qkv_own, out_rows[:early] = *both[:2], both[2 : 2 + chips], both[2 + chips :]
     grad_normed = grad_normed + grad_ext[:, 2:] + padded(later_rows, group - 2, 0)
     residual = inputs.astype(f32)
     scale_own = scale_ext[:, 2:]

time: 707 us -> 695 us (0.983)
  waiting for transfers between devices: 276 us -> 298 us
  local copies, waits for them, and re-layouts: 103 us -> 87.9 us
  starting transfers between devices: 130 us -> 115 us
    ppermute x2 -> x3, waiting for transfers between devices: 3.14 us -> 22 us  [diagonal(): lax.ppermute(value, 'fsdp', [(i, i ^ (2 if i & 1 else 4)) for i in range(...]
    all_gather x1 -> x0, waiting for transfers between devices: 15.8 us -> none  [local(): grad_all = lax.all_gather(grad_out, 'fsdp', axis_index_groups=columns)]
    ppermute x30, starting transfers between devices: 86.8 us -> 71.8 us  [rotate(): lax.ppermute(value, 'ctx', [(i, (i + steps) % count) for i in range(count)])]
    unnamed x250 -> x266, local copies, waits for them, and re-layouts: 87.4 us -> 73.5 us
    ppermute x42 -> x44, waiting for transfers between devices: 84.8 us -> 96.4 us  [across(): return lax.ppermute(value, 'fsdp', [(i, i ^ mask) for i in range(count)])]
    ppermute x42 -> x44, starting transfers between devices: 36.6 us -> 35.5 us  [across(): return lax.ppermute(value, 'fsdp', [(i, i ^ mask) for i in range(count)])]
  transfers between devices with their start and end apart: 81 -> 83, of which waited for: 32 -> 33; matrix products, arithmetic and copies ran while one was open for 8% -> 8% of each run, Pallas kernels for 14% -> 15%
where the time goes in v3:
time: 695 us; the launch traced here: 689 us
  waiting for transfers between devices  298 us (43%)
  Pallas kernels  131 us (19%)
  starting transfers between devices  115 us (17%)
  local copies, waits for them, and re-layouts  87.9 us (13%)
  other arithmetic  41.6 us (6%)
  between operations  15.7 us (2%)
    ppermute x30, waiting for transfers between devices, rotate(): lax.ppermute(value, 'ctx', [(i, (i + steps) % count) for i in range(count)])  161 us
    ppermute x44, waiting for transfers between devices, across(): return lax.ppermute(value, 'fsdp', [(i, i ^ mask) for i in range(count)])  96.4 us
    unnamed x266, local copies, waits for them, and re-layouts  73.5 us
    ppermute x30, starting transfers between devices, rotate(): lax.ppermute(value, 'ctx', [(i, (i + steps) % count) for i in range(count)])  71.8 us
    pallas_call x11, Pallas kernels, kernel_call(): pl.pallas_call(kernel, out_shape=list(outs), in_specs=specs, out_specs=[w...  64.9 us
    pallas_call x4, Pallas kernels, weight_grad(): pl.pallas_call(functools.partial(weight_grad_kernel, blocks, groups, part...  37.4 us
    ppermute x44, starting transfers between devices, across(): return lax.ppermute(value, 'fsdp', [(i, i ^ mask) for i in range(count)])  35.5 us
    pallas_call x2, Pallas kernels, block_call(): pl.pallas_call(kernel, out_shape=[out] * count, grid=(batch,), in_specs=[...  23.7 us
  transfers between devices with their start and end apart: 83, of which 33 were waited for; matrix products, arithmetic and copies ran while one was open for 8% of the time, Pallas kernels for 15%

profile of v3, /device:TPU:0, one launch (start us, length us, event | category | flops | bytes accessed | tf_op | source)
XLA Modules:
  0.0 689.1 jit_solution(12193023302486665461)
XLA Ops:
  30.7 8.0 %collective-permute-done.1 = bf16[2,8,224]{2,1,0:T(8,128)(2,1)S(1)} collective-permute-done((bf16[2,8,224]{2,1,0:T(8,128)(2,1)S(1)}, bf16[2,8,224]{2,1,0:T(8,128)(2,1)S(1)}, u32[]{:S(2)}, u32[]{:S(2)}) %collective-permute-start.1) | collective-permute-done | bytes 7200 | tf_op jit(solution)/shard_map/ppermute | solution.py:50
  44.9 11.9 %collective-permute-done.2 = bf16[4,8,224]{2,1,0:T(8,128)(2,1)S(1)} collective-permute-done((bf16[4,8,224]{2,1,0:T(8,128)(2,1)S(1)}, bf16[4,8,224]{2,1,0:T(8,128)(2,1)S(1)}, u32[]{:S(2)}, u32[]{:S(2)}) %collective-permute-start.2) | collective-permute-done | bytes 14368 | tf_op jit(solution)/shard_map/ppermute | solution.py:50
  86.0 12.8 %collective-permute-done.12 = bf16[256,576]{1,0:T(8,128)(2,1)S(1)} collective-permute-done((bf16[256,576]{1,0:T(8,128)(2,1)S(1)}, bf16[256,576]{1,0:T(8,128)(2,1)S(1)}, u32[]{:S(2)}, u32[]{:S(2)}) %collective-permute-start.12) | collective-permute-done | bytes 294944 | tf_op jit(solution)/shard_map/ppermute | solution.py:45
  100.4 8.0 %collective-permute-done.13 = bf16[256,576]{1,0:T(8,128)(2,1)S(1)} collective-permute-done((bf16[256,576]{1,0:T(8,128)(2,1)S(1)}, bf16[256,576]{1,0:T(8,128)(2,1)S(1)}, u32[]{:S(2)}, u32[]{:S(2)}) %collective-permute-start.13) | collective-permute-done | bytes 294944 | tf_op jit(solution)/shard_map/ppermute | solution.py:45
  119.6 16.0 %collective-permute-done.16.rest_2_ = bf16[2,224,1216]{2,1,0:T(8,128)(2,1)} collective-permute-done((bf16[2,224,1216]{2,1,0:T(8,128)(2,1)S(1)}, bf16[2,224,1216]{2,1,0:T(8,128)(2,1)}, u32[]{:S(2)}, u32[]{:S(2)}) %collective-permute-start.16) | collective-permute-done | bytes 1089568 | tf_op jit(solution)/shard_map/ppermute | solution.py:50
  144.0 8.9 %collective-permute-done.21.rest_7_.rest_0_ = bf16[256,1792]{1,0:T(8,128)(2,1)S(1)} collective-permute-done((bf16[256,1792]{1,0:T(8,128)(2,1)S(1)}, bf16[256,1792]{1,0:T(8,128)(2,1)S(1)}, u32[]{:S(2)}, u32[]{:S(2)}) %collective-permute-start.21) | collective-permute-done | bytes 917536 | tf_op jit(solution)/shard_map/ppermute | solution.py:55
  167.8 13.9 %collective-permute-done.26.rest_6_ = bf16[2,224,1216]{2,1,0:T(8,128)(2,1)} collective-permute-done((bf16[2,224,1216]{2,1,0:T(8,128)(2,1)}, bf16[2,224,1216]{2,1,0:T(8,128)(2,1)}, u32[]{:S(2)}, u32[]{:S(2)}) %collective-permute-start.26) | collective-permute-done | bytes 1089568 | tf_op jit(solution)/shard_map/ppermute | solution.py:50
  190.2 14.3 %collective-permute-done.27.rest_1_ = bf16[256,1792]{1,0:T(8,128)(2,1)S(1)} collective-permute-done((bf16[256,1792]{1,0:T(8,128)(2,1)S(1)}, bf16[256,1792]{1,0:T(8,128)(2,1)S(1)}, u32[]{:S(2)}, u32[]{:S(2)}) %collective-permute-start.27) | collective-permute-done | bytes 917536 | tf_op jit(solution)/shard_map/ppermute | solution.py:50
  206.3 13.1 %collective-permute-done.30.rest_3_ = bf16[256,1792]{1,0:T(8,128)(2,1)S(1)} collective-permute-done((bf16[256,1792]{1,0:T(8,128)(2,1)S(1)}, bf16[256,1792]{1,0:T(8,128)(2,1)S(1)}, u32[]{:S(2)}, u32[]{:S(2)}) %collective-permute-start.30) | collective-permute-done | bytes 917536 | tf_op jit(solution)/shard_map/ppermute | solution.py:55
  219.3 10.4 %shard_map.225 = (bf16[256,1216]{1,0:T(8,128)(2,1)S(1)}, bf16[256,1216]{1,0:T(8,128)(2,1)S(1)}, bf16[256,1216]{1,0:T(8,128)(2,1)S(1)}, bf16[256,1216]{1,0:T(8,12...) custom-call(s32[2]{0:T(128)S(1)} %pad_add_fusion.2.ids.place_ref, ...), custom_call_target="tpu_custom_call" | custom-call | tf_op jit(solution)/shard_map/pallas_call | solution.py:94
  232.5 16.1 %shard_map.226 = (bf16[1,1,608,1792]{3,2,1,0:T(8,128)(2,1)S(1)}, bf16[1,1,608,1792]{3,2,1,0:T(8,128)(2,1)}) custom-call(s32[2]{0:T(128)S(1)} %pad_add_fusion.2.ids.place_ref, bf16[256,1216]{1,0:T(8,128)(2,1)S(1)} %get-tuple-element.433.rest_0_, bf16[256,1216]{1,0:T(8,128)(2,1)S(1)} %get-tuple-element.434.rest_1_, ...), custom_call_target="tpu_custom_call" | custom-call | tf_op jit(solution)/shard_map/pallas_call | solution.py:353
  274.6 9.6 %shard_map.228 = (bf16[256,1216]{1,0:T(8,128)(2,1)S(1)}, bf16[256,1216]{1,0:T(8,128)(2,1)S(1)}, bf16[256,1792]{1,0:T(8,128)(2,1)}, bf16[256,1216]{1,0:T(8,128)(2...) custom-call(s32[2]{0:T(128)S(1)} %pad_add_fusion.2.ids.place_ref, ...), custom_call_target="tpu_custom_call" | custom-call | tf_op jit(solution)/shard_map/pallas_call | solution.py:94
  293.1 13.1 %shard_map.230 = (bf16[4,2,224,1216]{3,2,1,0:T(8,128)(2,1)S(1)}, bf16[4,2,224,1216]{3,2,1,0:T(8,128)(2,1)S(1)}) custom-call(s32[2]{0:T(128)S(1)} %pad_add_fusion.2.ids.place_ref, bf16[256,1792]{1,0:T(8,128)(2,1)S(1)} %copy-done.37, bf16[256,1792]{1,0:T(8,128)(2,1)S(1)} %copy-done.14, bf16[256,1792]{1,0:T(8,128)(2,1)S(1)} %copy-done.16, ...), custom_call_target="tpu_custom_call" | custom-call | tf_op jit(solution)/shard_map/pallas_call | solution.py:353
  339.3 10.8 %collective-permute-done.38 = bf16[256,448]{1,0:T(8,128)(2,1)S(1)} collective-permute-done((bf16[256,448]{1,0:T(8,128)(2,1)S(1)}, bf16[256,448]{1,0:T(8,128)(2,1)S(1)}, u32[]{:S(2)}, u32[]{:S(2)}) %collective-permute-start.38) | collective-permute-done | bytes 229408 | tf_op jit(solution)/shard_map/ppermute | solution.py:45
  359.8 16.1 %shard_map.233 = (bf16[2,128,576]{2,1,0:T(8,128)(2,1)S(1)}, bf16[2,128,576]{2,1,0:T(8,128)(2,1)S(1)}, bf16[2,128,576]{2,1,0:T(8,128)(2,1)S(1)}, bf16[2,128,576]{2,1,0:T(8,128)(2,1)S(1)}) custom-call(s32[2]{0:T(128)S(1)} %pad_add_fusion.2.ids.place_ref, bf16[2,128,576]{2,1,0:T(8,128)(2,1)S(1)} %bitcast.207, bf16[2,128,576]{2,1,0:T(8,128)(2,1)S(1)} %bitcast.209, ...), custom_call_target="tpu_custom_call" | custom-call | tf_op jit(solution)/shard_map/pallas_call | solution.py:461
  387.3 22.0 %collective-permute-done.43 = bf16[2,224,1216]{2,1,0:T(8,128)(2,1)S(1)} collective-permute-done((bf16[2,224,1216]{2,1,0:T(8,128)(2,1)S(1)}, bf16[2,224,1216]{2,1,0:T(8,128)(2,1)S(1)}, u32[]{:S(2)}, u32[]{:S(2)}) %collective-permute-start.43) | collective-permute-done | bytes 1089568 | tf_op jit(solution)/shard_map/ppermute | solution.py:50
  478.7 9.6 %collective-permute-done.58 = bf16[56,1792]{1,0:T(8,128)(2,1)S(1)} collective-permute-done((bf16[56,1792]{1,0:T(8,128)(2,1)S(1)}, bf16[56,1792]{1,0:T(8,128)(2,1)S(1)}, u32[]{:S(2)}, u32[]{:S(2)}) %collective-permute-start.58) | collective-permute-done | bytes 200736 | tf_op jit(solution)/shard_map/ppermute | solution.py:45
  494.0 9.1 %collective-permute-done.59 = bf16[56,1792]{1,0:T(8,128)(2,1)S(1)} collective-permute-done((bf16[56,1792]{1,0:T(8,128)(2,1)S(1)}, bf16[56,1792]{1,0:T(8,128)(2,1)S(1)}, u32[]{:S(2)}, u32[]{:S(2)}) %collective-permute-start.59) | collective-permute-done | bytes 200736 | tf_op jit(solution)/shard_map/ppermute | solution.py:45
  503.2 9.8 %collective-permute-done.60 = bf16[56,1792]{1,0:T(8,128)(2,1)S(1)} collective-permute-done((bf16[56,1792]{1,0:T(8,128)(2,1)S(1)}, bf16[56,1792]{1,0:T(8,128)(2,1)S(1)}, u32[]{:S(2)}, u32[]{:S(2)}) %collective-permute-start.60) | collective-permute-done | bytes 200736 | tf_op jit(solution)/shard_map/ppermute | solution.py:45
  512.9 12.1 %reduce-scatter.5.cloned.1.call-done = bf16[448,1216]{1,0:T(8,128)(2,1)} async-done(((bf16[1792,1216]{1,0:T(8,128)(2,1)}), bf16[448,1216]{1,0:T(8,128)(2,1)}) %reduce-scatter.5.cloned.1.call-update) | async-done | bytes 1089552 | tf_op jit(solution)/shard_map/reduce_scatter | solution.py:694
  549.4 14.3 %collective-permute-start.69 = (bf16[56,1792]{1,0:T(8,128)(2,1)S(1)}, bf16[56,1792]{1,0:T(8,128)(2,1)S(1)}, u32[]{:S(2)}, u32[]{:S(2)}) collective-permute-start(bf16[56,1792]{1,0:T(8,128)(2,1)S(1)} %add_convert_fusion.7), channel_id=1, source_target_pairs={{0,8},{8,16},{16,24},{24,0},{1,9},{9,17},{17,25},{25,1},{2,10},{10... | collective-permute-start | bytes 602120 | tf_op jit(solution)/shard_map/ppermute | solution.py:45
  563.7 28.3 %collective-permute-done.65 = bf16[56,2304]{1,0:T(8,128)(2,1)S(1)} collective-permute-done((bf16[56,2304]{1,0:T(8,128)(2,1)S(1)}, bf16[56,2304]{1,0:T(8,128)(2,1)S(1)}, u32[]{:S(2)}, u32[]{:S(2)}) %collective-permute-start.65) | collective-permute-done | bytes 258080 | tf_op jit(solution)/shard_map/ppermute | solution.py:45
  593.1 30.3 %collective-permute-done.68 = bf16[56,1792]{1,0:T(8,128)(2,1)S(1)} collective-permute-done((bf16[56,1792]{1,0:T(8,128)(2,1)S(1)}, bf16[56,1792]{1,0:T(8,128)(2,1)S(1)}, u32[]{:S(2)}, u32[]{:S(2)}) %collective-permute-start.68) | collective-permute-done | bytes 200736 | tf_op jit(solution)/shard_map/ppermute | solution.py:45
  642.9 25.1 %collective-permute-done.77 = bf16[56,2304]{1,0:T(8,128)(2,1)S(1)} collective-permute-done((bf16[56,2304]{1,0:T(8,128)(2,1)S(1)}, bf16[56,2304]{1,0:T(8,128)(2,1)S(1)}, u32[]{:S(2)}, u32[]{:S(2)}) %collective-permute-start.77) | collective-permute-done | bytes 258080 | tf_op jit(solution)/shard_map/ppermute | solution.py:45
  (530 shorter events, 330.0 us)
Async XLA Ops:
  7.2 148.1 %all-gather.3.cloned.1.call-start = ((), (), s32[]{:S(2)}) async-start(), calls=%async_computation.2 | async-start | bytes 7225344 | tf_op jit(solution)/shard_map/all_gather | solution.py:551
  17.0 41.0 %collective-permute-start.7 = (bf16[224,2304]{1,0:T(8,128)(2,1)}, bf16[224,2304]{1,0:T(8,128)(2,1)}, u32[]{:S(2)}, u32[]{:S(2)}) collective-permute-start(bf16[224,2304]{1,0:T(8,128)(2,1)} %constant_dynamic-update-slice_fusion.rest_0_.rest_4_), channel_id=1, source_target_pairs={{0,1},{1,0},{2,3},{3,2},{4,5},{5,4},{6,7},{7,6},{8,9},{9,8},{10,11... | collective-permute-start | bytes 3096584 | tf_op jit(solution)/shard_map/ppermute | solution.py:50
  62.2 250.1 %reduce-scatter.3.cloned.1.call-start = ((), (), s32[]{:S(2)}) async-start(), calls=%async_computation.3 | async-start | bytes 2723840 | tf_op jit(solution)/shard_map/reduce_scatter | solution.py:640
  62.2 46.2 %collective-permute-start.14 = (bf16[256,1792]{1,0:T(8,128)(2,1)S(1)}, bf16[256,1792]{1,0:T(8,128)(2,1)S(1)}, u32[]{:S(2)}, u32[]{:S(2)}) collective-permute-start(bf16[256,1792]{1,0:T(8,128)(2,1)S(1)} %fusion.14.rest_4_.rest_0_.rest_5_), channel_id=1, source_target_pairs={{0,2},{1,3},{2,0},{3,1},{4,6},{5,7},{6,4},{7,5},{8,10},{9,11},{10,... | collective-permute-start | bytes 2752520 | tf_op jit(solution)/shard_map/ppermute | solution.py:50
  62.7 45.7 %collective-permute-start.15 = (bf16[256,1792]{1,0:T(8,128)(2,1)S(1)}, bf16[256,1792]{1,0:T(8,128)(2,1)S(1)}, u32[]{:S(2)}, u32[]{:S(2)}) collective-permute-start(bf16[256,1792]{1,0:T(8,128)(2,1)S(1)} %fusion.14.rest_4_.rest_0_.rest_5_), channel_id=1, source_target_pairs={{0,4},{1,5},{2,6},{3,7},{4,0},{5,1},{6,2},{7,3},{8,12},{9,13},{10,... | collective-permute-start | bytes 2752520 | tf_op jit(solution)/shard_map/ppermute | solution.py:50
  80.7 54.8 %collective-permute-start.16 = (bf16[2,224,1216]{2,1,0:T(8,128)(2,1)S(1)}, bf16[2,224,1216]{2,1,0:T(8,128)(2,1)}, u32[]{:S(2)}, u32[]{:S(2)}) collective-permute-start(bf16[2,224,1216]{2,1,0:T(8,128)(2,1)S(1)} %get-tuple-element.502), channel_id=1, source_target_pairs={{0,2},{1,3},{2,0},{3,1},{4,6},{5,7},{6,4},{7,5},{8,10},{9,11},{10,... | collective-permute-start | bytes 3268616 | tf_op jit(solution)/shard_map/ppermute | solution.py:50
  85.9 49.7 %collective-permute-start.17 = (bf16[2,224,1216]{2,1,0:T(8,128)(2,1)S(1)}, bf16[2,224,1216]{2,1,0:T(8,128)(2,1)}, u32[]{:S(2)}, u32[]{:S(2)}) collective-permute-start(bf16[2,224,1216]{2,1,0:T(8,128)(2,1)S(1)} %get-tuple-element.501), channel_id=1, source_target_pairs={{0,4},{1,5},{2,6},{3,7},{4,0},{5,1},{6,2},{7,3},{8,12},{9,13},{10,... | collective-permute-start | bytes 3268616 | tf_op jit(solution)/shard_map/ppermute | solution.py:50
  139.3 42.4 %collective-permute-start.22 = (bf16[608,1792]{1,0:T(8,128)(2,1)}, bf16[608,1792]{1,0:T(8,128)(2,1)}, u32[]{:S(2)}, u32[]{:S(2)}) collective-permute-start(bf16[608,1792]{1,0:T(8,128)(2,1)} %rest_8_), channel_id=1, source_target_pairs={{0,1},{1,0},{2,3},{3,2},{4,5},{5,4},{6,7},{7,6},{8,9},{9,8},{10,11... | collective-permute-start | bytes 6537224 | tf_op jit(solution)/shard_map/ppermute | solution.py:50
  260.3 264.7 %reduce-scatter.5.cloned.1.call-start = ((), (), s32[]{:S(2)}) async-start(), calls=%async_computation.4 | async-start | bytes 5734400 | tf_op jit(solution)/shard_map/reduce_scatter | solution.py:694
  380.7 31.0 %collective-permute-start.44 = (bf16[4,224,1792]{2,1,0:T(8,128)(2,1)S(1)}, bf16[4,224,1792]{2,1,0:T(8,128)(2,1)S(1)}, u32[]{:S(2)}, u32[]{:S(2)}) collective-permute-start(bf16[4,224,1792]{2,1,0:T(8,128)(2,1)S(1)} %bitcast.226), channel_id=1, source_target_pairs={{0,1},{1,0},{2,3},{3,2},{4,5},{5,4},{6,7},{7,6},{8,9},{9,8},{10,11... | collective-permute-start | bytes 9633800 | tf_op jit(solution)/shard_map/ppermute | solution.py:50
  383.2 30.7 %collective-permute-start.45 = (bf16[2,128,576]{2,1,0:T(8,128)(2,1)S(1)}, bf16[2,128,576]{2,1,0:T(8,128)(2,1)S(1)}, u32[]{:S(2)}, u32[]{:S(2)}) collective-permute-start(bf16[2,128,576]{2,1,0:T(8,128)(2,1)S(1)} %get-tuple-element.387), channel_id=1, source_target_pairs={{0,24},{8,0},{16,8},{24,16},{1,25},{9,1},{17,9},{25,17},{2,26},{10... | collective-permute-start | bytes 884744 | tf_op jit(solution)/shard_map/ppermute | solution.py:45
  416.7 258.5 %all-gather.5.cloned.1.call-start = ((), (), s32[]{:S(2)}) async-start(), calls=%async_computation.5 | async-start | bytes 5734400 | tf_op jit(solution)/shard_map/all_gather | solution.py:754
  437.0 33.2 %collective-permute-start.53 = (bf16[152,1792]{1,0:T(8,128)(2,1)}, bf16[152,1792]{1,0:T(8,128)(2,1)}, u32[]{:S(2)}, u32[]{:S(2)}) collective-permute-start(bf16[152,1792]{1,0:T(8,128)(2,1)} %reduce-scatter.3.cloned.1.call-done), channel_id=1, source_target_pairs={{0,8},{8,16},{16,24},{24,0},{1,9},{9,17},{17,25},{25,1},{2,10},{10... | collective-permute-start | bytes 1634312 | tf_op jit(solution)/shard_map/ppermute | solution.py:45
  459.6 53.4 %collective-permute-start.54 = (bf16[224,2304]{1,0:T(8,128)(2,1)}, bf16[224,2304]{1,0:T(8,128)(2,1)}, u32[]{:S(2)}, u32[]{:S(2)}) collective-permute-start(bf16[224,2304]{1,0:T(8,128)(2,1)} %get-tuple-element.416), channel_id=1, source_target_pairs={{0,2},{1,3},{2,0},{3,1},{4,6},{5,7},{6,4},{7,5},{8,10},{9,11},{10,... | collective-permute-start | bytes 3096584 | tf_op jit(solution)/shard_map/ppermute | solution.py:50
  460.8 52.1 %collective-permute-start.55 = (bf16[224,2304]{1,0:T(8,128)(2,1)}, bf16[224,2304]{1,0:T(8,128)(2,1)}, u32[]{:S(2)}, u32[]{:S(2)}) collective-permute-start(bf16[224,2304]{1,0:T(8,128)(2,1)} %get-tuple-element.417), channel_id=1, source_target_pairs={{0,4},{1,5},{2,6},{3,7},{4,0},{5,1},{6,2},{7,3},{8,12},{9,13},{10,... | collective-permute-start | bytes 3096584 | tf_op jit(solution)/shard_map/ppermute | solution.py:50
  467.3 45.6 %collective-permute-start.56 = (bf16[224,2304]{1,0:T(8,128)(2,1)}, bf16[224,2304]{1,0:T(8,128)(2,1)}, u32[]{:S(2)}, u32[]{:S(2)}) collective-permute-start(bf16[224,2304]{1,0:T(8,128)(2,1)} %get-tuple-element.418), channel_id=1, source_target_pairs={{0,6},{1,7},{2,4},{3,5},{4,2},{5,3},{6,0},{7,1},{8,14},{9,15},{10,... | collective-permute-start | bytes 3096584 | tf_op jit(solution)/shard_map/ppermute | solution.py:50
  534.1 57.9 %collective-permute-start.65 = (bf16[56,2304]{1,0:T(8,128)(2,1)S(1)}, bf16[56,2304]{1,0:T(8,128)(2,1)S(1)}, u32[]{:S(2)}, u32[]{:S(2)}) collective-permute-start(bf16[56,2304]{1,0:T(8,128)(2,1)S(1)} %get-tuple-element.511), channel_id=1, source_target_pairs={{0,16},{8,24},{16,0},{24,8},{1,17},{9,25},{17,1},{25,9},{2,18},{10... | collective-permute-start | bytes 774152 | tf_op jit(solution)/shard_map/ppermute | solution.py:45
  544.6 47.4 %collective-permute-start.64 = (bf16[56,2304]{1,0:T(8,128)(2,1)S(1)}, bf16[56,2304]{1,0:T(8,128)(2,1)S(1)}, u32[]{:S(2)}, u32[]{:S(2)}) collective-permute-start(bf16[56,2304]{1,0:T(8,128)(2,1)S(1)} %get-tuple-element.509), channel_id=1, source_target_pairs={{0,8},{8,16},{16,24},{24,0},{1,9},{9,17},{17,25},{25,1},{2,10},{10... | collective-permute-start | bytes 774152 | tf_op jit(solution)/shard_map/ppermute | solution.py:45
  544.8 48.4 %collective-permute-start.67 = (bf16[56,1792]{1,0:T(8,128)(2,1)S(1)}, bf16[56,1792]{1,0:T(8,128)(2,1)S(1)}, u32[]{:S(2)}, u32[]{:S(2)}) collective-permute-start(bf16[56,1792]{1,0:T(8,128)(2,1)S(1)} %add_convert_fusion.7), channel_id=1, source_target_pairs={{0,24},{8,0},{16,8},{24,16},{1,25},{9,1},{17,9},{25,17},{2,26},{10... | collective-permute-start | bytes 602120 | tf_op jit(solution)/shard_map/ppermute | solution.py:45
  548.6 74.8 %collective-permute-start.68 = (bf16[56,1792]{1,0:T(8,128)(2,1)S(1)}, bf16[56,1792]{1,0:T(8,128)(2,1)S(1)}, u32[]{:S(2)}, u32[]{:S(2)}) collective-permute-start(bf16[56,1792]{1,0:T(8,128)(2,1)S(1)} %add_convert_fusion.7), channel_id=1, source_target_pairs={{0,16},{8,24},{16,0},{24,8},{1,17},{9,25},{17,1},{25,9},{2,18},{10... | collective-permute-start | bytes 602120 | tf_op jit(solution)/shard_map/ppermute | solution.py:45
  549.4 74.0 %collective-permute-start.69 = (bf16[56,1792]{1,0:T(8,128)(2,1)S(1)}, bf16[56,1792]{1,0:T(8,128)(2,1)S(1)}, u32[]{:S(2)}, u32[]{:S(2)}) collective-permute-start(bf16[56,1792]{1,0:T(8,128)(2,1)S(1)} %add_convert_fusion.7), channel_id=1, source_target_pairs={{0,8},{8,16},{16,24},{24,0},{1,9},{9,17},{17,25},{25,1},{2,10},{10... | collective-permute-start | bytes 602120 | tf_op jit(solution)/shard_map/ppermute | solution.py:45
  627.9 40.1 %collective-permute-start.77 = (bf16[56,2304]{1,0:T(8,128)(2,1)S(1)}, bf16[56,2304]{1,0:T(8,128)(2,1)S(1)}, u32[]{:S(2)}, u32[]{:S(2)}) collective-permute-start(bf16[56,2304]{1,0:T(8,128)(2,1)S(1)} %fusion.25), channel_id=1, source_target_pairs={{0,16},{8,24},{16,0},{24,8},{1,17},{9,25},{17,1},{25,9},{2,18},{10... | collective-permute-start | bytes 774152 | tf_op jit(solution)/shard_map/ppermute | solution.py:45
  637.0 31.0 %collective-permute-start.78 = (bf16[56,2304]{1,0:T(8,128)(2,1)S(1)}, bf16[56,2304]{1,0:T(8,128)(2,1)S(1)}, u32[]{:S(2)}, u32[]{:S(2)}) collective-permute-start(bf16[56,2304]{1,0:T(8,128)(2,1)S(1)} %fusion.25), channel_id=1, source_target_pairs={{0,8},{8,16},{16,24},{24,0},{1,9},{9,17},{17,25},{25,1},{2,10},{10... | collective-permute-start | bytes 774152 | tf_op jit(solution)/shard_map/ppermute | solution.py:45
  638.2 32.1 %collective-permute-start.72 = (bf16[256,1792]{1,0:T(8,128)(2,1)S(1)}, bf16[256,1792]{1,0:T(8,128)(2,1)S(1)}, u32[]{:S(2)}, u32[]{:S(2)}) collective-permute-start(bf16[256,1792]{1,0:T(8,128)(2,1)S(1)} %get-tuple-element.440), channel_id=1, source_target_pairs={{0,6},{1,7},{2,4},{3,5},{4,2},{5,3},{6,0},{7,1},{8,14},{9,15},{10,... | collective-permute-start | bytes 2752520 | tf_op jit(solution)/shard_map/ppermute | solution.py:50
  (191 other events, 2622.3 us)
Sparse Core Ops, SparseCore 0:
  62.3 72.5 all-gather.2
  260.4 43.7 reduce-scatter.2
  416.9 108.1 reduce-scatter.4
  539.6 135.6 all-gather.4

commit v4 on v3

--- a/solution.py
+++ b/solution.py
@@ -86,7 +86,7 @@
     return buffer
 
 
-def kernel_call(kernel, ids, arrays, outs, scratch=(), anywhere=(), vmem=32):
+def kernel_call(kernel, ids, arrays, outs, scratch=(), anywhere=(), vmem=24):
     whole = pl.BlockSpec(memory_space=pltpu.VMEM)
     specs = [pl.BlockSpec(memory_space=pltpu.SMEM)]
     anyplace = pl.BlockSpec(memory_space=pl.ANY)
@@ -358,7 +358,7 @@
         + [pl.BlockSpec(memory_space=pltpu.VMEM)] * len(arrays),
         out_specs=[block] * 2,
         scratch_shapes=[pltpu.VMEM((rows, chunks * tokens), bf16)],
-        compiler_params=pltpu.CompilerParams(vmem_limit_bytes=32 * 1024 * 1024),
+        compiler_params=pltpu.CompilerParams(vmem_limit_bytes=24 * 1024 * 1024),
         cost_estimate=FREE,
     )(ids, *arrays)
 
@@ -612,7 +612,7 @@
         ids,
         [*normed_all, gate_w, up_w],
         [unit] * 3 * chips,
-        vmem=32,
+        vmem=28,
     )
     hidden_all, to_gate, to_up = fed[:chips], fed[chips : 2 * chips], fed[2 * chips :]
 
@@ -624,7 +624,7 @@
             + [gate_w, up_w, down_w],
             [unit, unit, shape_of((rows, width), bf16)] * len(at),
             scratch=[vmem((rows * len(at), hidden_width), bf16)] * 2,
-            vmem=32,
+            vmem=24,
         )
         return [list(outs[3 * i : 3 * i + 3]) for i in range(len(at))]
 
@@ -688,8 +688,8 @@
     gate_up_rows += chip_exchange(gate_up_own)[early:]
     grad_qkv = returned(grad_qkv)
     gate_up_sent = jnp.stack(gate_up_rows).reshape(-1, hidden_width)
-    both = join(gate_up_sent, down_part, *out_own, *grad_qkv)
-    gate_up_sent, down_part, out_own, grad_qkv = *both[:2], both[2 : 2 + chips], both[2 + chips :]
+    both = join(down_part, *out_own, *grad_qkv)
+    down_part, out_own, grad_qkv = both[0], both[1 : 1 + chips], both[1 + chips :]
 
     gate_up_part = lax.psum_scatter(gate_up_sent, "ctx", scatter_dimension=0, tiled=True)
     down_parts += [rotate(down_part, -step) for step in range(max(2, count - 1), count)]

time: 695 us -> 688 us (0.990)
    unnamed x266 -> x260, local copies, waits for them, and re-layouts: 73.5 us -> 70.6 us
where the time goes in v4:
time: 688 us; the launch traced here: 683 us
  waiting for transfers between devices  292 us (42%)
  Pallas kernels  132 us (19%)
  starting transfers between devices  114 us (17%)
  local copies, waits for them, and re-layouts  84.9 us (12%)
  other arithmetic  44.2 us (6%)
  between operations  15.6 us (2%)
    ppermute x30, waiting for transfers between devices, rotate(): lax.ppermute(value, 'ctx', [(i, (i + steps) % count) for i in range(count)])  157 us
    ppermute x44, waiting for transfers between devices, across(): return lax.ppermute(value, 'fsdp', [(i, i ^ mask) for i in range(count)])  103 us
    ppermute x30, starting transfers between devices, rotate(): lax.ppermute(value, 'ctx', [(i, (i + steps) % count) for i in range(count)])  71.2 us
    unnamed x260, local copies, waits for them, and re-layouts  70.6 us
    pallas_call x11, Pallas kernels, kernel_call(): pl.pallas_call(kernel, out_shape=list(outs), in_specs=specs, out_specs=[w...  64.5 us
    pallas_call x4, Pallas kernels, weight_grad(): pl.pallas_call(functools.partial(weight_grad_kernel, blocks, groups, part...  37.8 us
    ppermute x44, starting transfers between devices, across(): return lax.ppermute(value, 'fsdp', [(i, i ^ mask) for i in range(count)])  35.8 us
    pallas_call x2, Pallas kernels, block_call(): pl.pallas_call(kernel, out_shape=[out] * count, grid=(batch,), in_specs=[...  24.5 us
  transfers between devices with their start and end apart: 83, of which 33 were waited for; matrix products, arithmetic and copies ran while one was open for 8% of the time, Pallas kernels for 15%

profile of v4, /device:TPU:0, one launch (start us, length us, event | category | flops | bytes accessed | tf_op | source)
XLA Modules:
  0.0 682.9 jit_solution(12121490276308782467)
XLA Ops:
  30.7 8.0 %collective-permute-done.1 = bf16[2,8,224]{2,1,0:T(8,128)(2,1)S(1)} collective-permute-done((bf16[2,8,224]{2,1,0:T(8,128)(2,1)S(1)}, bf16[2,8,224]{2,1,0:T(8,128)(2,1)S(1)}, u32[]{:S(2)}, u32[]{:S(2)}) %collective-permute-start.1) | collective-permute-done | bytes 7200 | tf_op jit(solution)/shard_map/ppermute | solution.py:50
  44.9 11.9 %collective-permute-done.2 = bf16[4,8,224]{2,1,0:T(8,128)(2,1)S(1)} collective-permute-done((bf16[4,8,224]{2,1,0:T(8,128)(2,1)S(1)}, bf16[4,8,224]{2,1,0:T(8,128)(2,1)S(1)}, u32[]{:S(2)}, u32[]{:S(2)}) %collective-permute-start.2) | collective-permute-done | bytes 14368 | tf_op jit(solution)/shard_map/ppermute | solution.py:50
  86.1 12.8 %collective-permute-done.12 = bf16[256,576]{1,0:T(8,128)(2,1)S(1)} collective-permute-done((bf16[256,576]{1,0:T(8,128)(2,1)S(1)}, bf16[256,576]{1,0:T(8,128)(2,1)S(1)}, u32[]{:S(2)}, u32[]{:S(2)}) %collective-permute-start.12) | collective-permute-done | bytes 294944 | tf_op jit(solution)/shard_map/ppermute | solution.py:45
  100.4 8.0 %collective-permute-done.13 = bf16[256,576]{1,0:T(8,128)(2,1)S(1)} collective-permute-done((bf16[256,576]{1,0:T(8,128)(2,1)S(1)}, bf16[256,576]{1,0:T(8,128)(2,1)S(1)}, u32[]{:S(2)}, u32[]{:S(2)}) %collective-permute-start.13) | collective-permute-done | bytes 294944 | tf_op jit(solution)/shard_map/ppermute | solution.py:45
  108.5 7.6 %shard_map.222 = (bf16[2,128,448]{2,1,0:T(8,128)(2,1)S(1)}, bf16[2,128,448]{2,1,0:T(8,128)(2,1)S(1)}, bf16[2,128,448]{2,1,0:T(8,128)(2,1)S(1)}, bf16[2,128,448]{2,1,0:T(8,128)(2,1)S(1)}) custom-call(s32[2]{0:T(128)S(1)} %pad_add_fusion.2.ids.place_ref, bf16[2,128,576]{2,1,0:T(8,128)(2,1)S(1)} %bitcast.206, bf16[2,128,576]{2,1,0:T(8,128)(2,1)S(1)} %bitcast.208, ...), custom_call_target="tpu_custom_call" | custom-call | tf_op jit(solution)/shard_map/pallas_call | solution.py:461
  119.6 16.0 %collective-permute-done.16.rest_2_ = bf16[2,224,1216]{2,1,0:T(8,128)(2,1)} collective-permute-done((bf16[2,224,1216]{2,1,0:T(8,128)(2,1)S(1)}, bf16[2,224,1216]{2,1,0:T(8,128)(2,1)}, u32[]{:S(2)}, u32[]{:S(2)}) %collective-permute-start.16) | collective-permute-done | bytes 1089568 | tf_op jit(solution)/shard_map/ppermute | solution.py:50
  145.3 8.8 %collective-permute-done.21.rest_7_.rest_0_ = bf16[256,1792]{1,0:T(8,128)(2,1)S(1)} collective-permute-done((bf16[256,1792]{1,0:T(8,128)(2,1)S(1)}, bf16[256,1792]{1,0:T(8,128)(2,1)S(1)}, u32[]{:S(2)}, u32[]{:S(2)}) %collective-permute-start.21) | collective-permute-done | bytes 917536 | tf_op jit(solution)/shard_map/ppermute | solution.py:55
  169.2 14.0 %collective-permute-done.26.rest_6_ = bf16[2,224,1216]{2,1,0:T(8,128)(2,1)} collective-permute-done((bf16[2,224,1216]{2,1,0:T(8,128)(2,1)}, bf16[2,224,1216]{2,1,0:T(8,128)(2,1)}, u32[]{:S(2)}, u32[]{:S(2)}) %collective-permute-start.26) | collective-permute-done | bytes 1089568 | tf_op jit(solution)/shard_map/ppermute | solution.py:50
  191.6 14.3 %collective-permute-done.27.rest_1_ = bf16[256,1792]{1,0:T(8,128)(2,1)S(1)} collective-permute-done((bf16[256,1792]{1,0:T(8,128)(2,1)S(1)}, bf16[256,1792]{1,0:T(8,128)(2,1)S(1)}, u32[]{:S(2)}, u32[]{:S(2)}) %collective-permute-start.27) | collective-permute-done | bytes 917536 | tf_op jit(solution)/shard_map/ppermute | solution.py:50
  207.7 13.1 %collective-permute-done.30.rest_3_ = bf16[256,1792]{1,0:T(8,128)(2,1)S(1)} collective-permute-done((bf16[256,1792]{1,0:T(8,128)(2,1)S(1)}, bf16[256,1792]{1,0:T(8,128)(2,1)S(1)}, u32[]{:S(2)}, u32[]{:S(2)}) %collective-permute-start.30) | collective-permute-done | bytes 917536 | tf_op jit(solution)/shard_map/ppermute | solution.py:55
  220.7 10.4 %shard_map.225 = (bf16[256,1216]{1,0:T(8,128)(2,1)S(1)}, bf16[256,1216]{1,0:T(8,128)(2,1)S(1)}, bf16[256,1216]{1,0:T(8,128)(2,1)S(1)}, bf16[256,1216]{1,0:T(8,12...) custom-call(s32[2]{0:T(128)S(1)} %pad_add_fusion.2.ids.place_ref, ...), custom_call_target="tpu_custom_call" | custom-call | tf_op jit(solution)/shard_map/pallas_call | solution.py:94
  233.0 15.4 %shard_map.226 = (bf16[1,1,608,1792]{3,2,1,0:T(8,128)(2,1)S(1)}, bf16[1,1,608,1792]{3,2,1,0:T(8,128)(2,1)S(1)}) custom-call(s32[2]{0:T(128)S(1)} %pad_add_fusion.2.ids.place_ref, bf16[256,1216]{1,0:T(8,128)(2,1)S(1)} %get-tuple-element.431.rest_0_, bf16[256,1216]{1,0:T(8,128)(2,1)S(1)} %get-tuple-element.432.rest_1_, ...), custom_call_target="tpu_custom_call" | custom-call | tf_op jit(solution)/shard_map/pallas_call | solution.py:353
  272.3 8.7 %shard_map.228 = (bf16[256,1216]{1,0:T(8,128)(2,1)S(1)}, bf16[256,1216]{1,0:T(8,128)(2,1)S(1)}, bf16[256,1792]{1,0:T(8,128)(2,1)S(1)}, bf16[256,1216]{1,0:T(8,12...) custom-call(s32[2]{0:T(128)S(1)} %pad_add_fusion.2.ids.place_ref, ...), custom_call_target="tpu_custom_call" | custom-call | tf_op jit(solution)/shard_map/pallas_call | solution.py:94
  290.0 13.1 %shard_map.230 = (bf16[4,2,224,1216]{3,2,1,0:T(8,128)(2,1)S(1)}, bf16[4,2,224,1216]{3,2,1,0:T(8,128)(2,1)S(1)}) custom-call(s32[2]{0:T(128)S(1)} %pad_add_fusion.2.ids.place_ref, bf16[256,1792]{1,0:T(8,128)(2,1)S(1)} %copy-done.36, bf16[256,1792]{1,0:T(8,128)(2,1)S(1)} %copy-done.13, bf16[256,1792]{1,0:T(8,128)(2,1)S(1)} %copy-done.15, ...), custom_call_target="tpu_custom_call" | custom-call | tf_op jit(solution)/shard_map/pallas_call | solution.py:353
  336.0 10.8 %collective-permute-done.38 = bf16[256,448]{1,0:T(8,128)(2,1)S(1)} collective-permute-done((bf16[256,448]{1,0:T(8,128)(2,1)S(1)}, bf16[256,448]{1,0:T(8,128)(2,1)S(1)}, u32[]{:S(2)}, u32[]{:S(2)}) %collective-permute-start.38) | collective-permute-done | bytes 229408 | tf_op jit(solution)/shard_map/ppermute | solution.py:45
  359.8 16.9 %shard_map.233 = (bf16[2,128,576]{2,1,0:T(8,128)(2,1)S(1)}, bf16[2,128,576]{2,1,0:T(8,128)(2,1)}, bf16[2,128,576]{2,1,0:T(8,128)(2,1)}, bf16[2,128,576]{2,1,0:T(8,128)(2,1)}) custom-call(s32[2]{0:T(128)S(1)} %pad_add_fusion.2.ids.place_ref, bf16[2,128,576]{2,1,0:T(8,128)(2,1)S(1)} %bitcast.207, bf16[2,128,576]{2,1,0:T(8,128)(2,1)S(1)} %bitcast.209, ...), custom_call_target="tpu_custom_call" | custom-call | tf_op jit(solution)/shard_map/pallas_call | solution.py:461
  384.0 22.8 %collective-permute-done.43 = bf16[2,224,1216]{2,1,0:T(8,128)(2,1)S(1)} collective-permute-done((bf16[2,224,1216]{2,1,0:T(8,128)(2,1)S(1)}, bf16[2,224,1216]{2,1,0:T(8,128)(2,1)S(1)}, u32[]{:S(2)}, u32[]{:S(2)}) %collective-permute-start.43) | collective-permute-done | bytes 1089568 | tf_op jit(solution)/shard_map/ppermute | solution.py:50
  477.9 9.6 %collective-permute-done.58 = bf16[56,1792]{1,0:T(8,128)(2,1)S(1)} collective-permute-done((bf16[56,1792]{1,0:T(8,128)(2,1)S(1)}, bf16[56,1792]{1,0:T(8,128)(2,1)S(1)}, u32[]{:S(2)}, u32[]{:S(2)}) %collective-permute-start.58) | collective-permute-done | bytes 200736 | tf_op jit(solution)/shard_map/ppermute | solution.py:45
  493.3 9.1 %collective-permute-done.59 = bf16[56,1792]{1,0:T(8,128)(2,1)S(1)} collective-permute-done((bf16[56,1792]{1,0:T(8,128)(2,1)S(1)}, bf16[56,1792]{1,0:T(8,128)(2,1)S(1)}, u32[]{:S(2)}, u32[]{:S(2)}) %collective-permute-start.59) | collective-permute-done | bytes 200736 | tf_op jit(solution)/shard_map/ppermute | solution.py:45
  502.4 9.8 %collective-permute-done.60 = bf16[56,1792]{1,0:T(8,128)(2,1)S(1)} collective-permute-done((bf16[56,1792]{1,0:T(8,128)(2,1)S(1)}, bf16[56,1792]{1,0:T(8,128)(2,1)S(1)}, u32[]{:S(2)}, u32[]{:S(2)}) %collective-permute-start.60) | collective-permute-done | bytes 200736 | tf_op jit(solution)/shard_map/ppermute | solution.py:45
  542.5 14.3 %collective-permute-start.69 = (bf16[56,1792]{1,0:T(8,128)(2,1)S(1)}, bf16[56,1792]{1,0:T(8,128)(2,1)S(1)}, u32[]{:S(2)}, u32[]{:S(2)}) collective-permute-start(bf16[56,1792]{1,0:T(8,128)(2,1)S(1)} %add_convert_fusion.7), channel_id=1, source_target_pairs={{0,8},{8,16},{16,24},{24,0},{1,9},{9,17},{17,25},{25,1},{2,10},{10... | collective-permute-start | bytes 602120 | tf_op jit(solution)/shard_map/ppermute | solution.py:45
  556.8 28.3 %collective-permute-done.65 = bf16[56,2304]{1,0:T(8,128)(2,1)S(1)} collective-permute-done((bf16[56,2304]{1,0:T(8,128)(2,1)S(1)}, bf16[56,2304]{1,0:T(8,128)(2,1)S(1)}, u32[]{:S(2)}, u32[]{:S(2)}) %collective-permute-start.65) | collective-permute-done | bytes 258080 | tf_op jit(solution)/shard_map/ppermute | solution.py:45
  586.2 29.6 %collective-permute-done.68 = bf16[56,1792]{1,0:T(8,128)(2,1)S(1)} collective-permute-done((bf16[56,1792]{1,0:T(8,128)(2,1)S(1)}, bf16[56,1792]{1,0:T(8,128)(2,1)S(1)}, u32[]{:S(2)}, u32[]{:S(2)}) %collective-permute-start.68) | collective-permute-done | bytes 200736 | tf_op jit(solution)/shard_map/ppermute | solution.py:45
  635.2 26.3 %collective-permute-done.77 = bf16[56,2304]{1,0:T(8,128)(2,1)S(1)} collective-permute-done((bf16[56,2304]{1,0:T(8,128)(2,1)S(1)}, bf16[56,2304]{1,0:T(8,128)(2,1)S(1)}, u32[]{:S(2)}, u32[]{:S(2)}) %collective-permute-start.77) | collective-permute-done | bytes 258080 | tf_op jit(solution)/shard_map/ppermute | solution.py:45
  (524 shorter events, 327.7 us)
Async XLA Ops:
  7.2 149.4 %all-gather.3.cloned.1.call-start = ((), (), s32[]{:S(2)}) async-start(), calls=%async_computation.2 | async-start | bytes 7225344 | tf_op jit(solution)/shard_map/all_gather | solution.py:551
  17.0 41.0 %collective-permute-start.7 = (bf16[224,2304]{1,0:T(8,128)(2,1)}, bf16[224,2304]{1,0:T(8,128)(2,1)}, u32[]{:S(2)}, u32[]{:S(2)}) collective-permute-start(bf16[224,2304]{1,0:T(8,128)(2,1)} %constant_dynamic-update-slice_fusion.rest_0_.rest_4_), channel_id=1, source_target_pairs={{0,1},{1,0},{2,3},{3,2},{4,5},{5,4},{6,7},{7,6},{8,9},{9,8},{10,11... | collective-permute-start | bytes 3096584 | tf_op jit(solution)/shard_map/ppermute | solution.py:50
  62.2 247.0 %reduce-scatter.3.cloned.1.call-start = ((), (), s32[]{:S(2)}) async-start(), calls=%async_computation.3 | async-start | bytes 2723840 | tf_op jit(solution)/shard_map/reduce_scatter | solution.py:640
  62.3 46.2 %collective-permute-start.14 = (bf16[256,1792]{1,0:T(8,128)(2,1)S(1)}, bf16[256,1792]{1,0:T(8,128)(2,1)S(1)}, u32[]{:S(2)}, u32[]{:S(2)}) collective-permute-start(bf16[256,1792]{1,0:T(8,128)(2,1)S(1)} %fusion.14.rest_4_.rest_0_.rest_5_), channel_id=1, source_target_pairs={{0,2},{1,3},{2,0},{3,1},{4,6},{5,7},{6,4},{7,5},{8,10},{9,11},{10,... | collective-permute-start | bytes 2752520 | tf_op jit(solution)/shard_map/ppermute | solution.py:50
  62.8 45.7 %collective-permute-start.15 = (bf16[256,1792]{1,0:T(8,128)(2,1)S(1)}, bf16[256,1792]{1,0:T(8,128)(2,1)S(1)}, u32[]{:S(2)}, u32[]{:S(2)}) collective-permute-start(bf16[256,1792]{1,0:T(8,128)(2,1)S(1)} %fusion.14.rest_4_.rest_0_.rest_5_), channel_id=1, source_target_pairs={{0,4},{1,5},{2,6},{3,7},{4,0},{5,1},{6,2},{7,3},{8,12},{9,13},{10,... | collective-permute-start | bytes 2752520 | tf_op jit(solution)/shard_map/ppermute | solution.py:50
  80.8 54.8 %collective-permute-start.16 = (bf16[2,224,1216]{2,1,0:T(8,128)(2,1)S(1)}, bf16[2,224,1216]{2,1,0:T(8,128)(2,1)}, u32[]{:S(2)}, u32[]{:S(2)}) collective-permute-start(bf16[2,224,1216]{2,1,0:T(8,128)(2,1)S(1)} %get-tuple-element.500), channel_id=1, source_target_pairs={{0,2},{1,3},{2,0},{3,1},{4,6},{5,7},{6,4},{7,5},{8,10},{9,11},{10,... | collective-permute-start | bytes 3268616 | tf_op jit(solution)/shard_map/ppermute | solution.py:50
  86.0 49.7 %collective-permute-start.17 = (bf16[2,224,1216]{2,1,0:T(8,128)(2,1)S(1)}, bf16[2,224,1216]{2,1,0:T(8,128)(2,1)}, u32[]{:S(2)}, u32[]{:S(2)}) collective-permute-start(bf16[2,224,1216]{2,1,0:T(8,128)(2,1)S(1)} %get-tuple-element.499), channel_id=1, source_target_pairs={{0,4},{1,5},{2,6},{3,7},{4,0},{5,1},{6,2},{7,3},{8,12},{9,13},{10,... | collective-permute-start | bytes 3268616 | tf_op jit(solution)/shard_map/ppermute | solution.py:50
  140.8 42.4 %collective-permute-start.22 = (bf16[608,1792]{1,0:T(8,128)(2,1)}, bf16[608,1792]{1,0:T(8,128)(2,1)}, u32[]{:S(2)}, u32[]{:S(2)}) collective-permute-start(bf16[608,1792]{1,0:T(8,128)(2,1)} %rest_8_), channel_id=1, source_target_pairs={{0,1},{1,0},{2,3},{3,2},{4,5},{5,4},{6,7},{7,6},{8,9},{9,8},{10,11... | collective-permute-start | bytes 6537224 | tf_op jit(solution)/shard_map/ppermute | solution.py:50
  257.9 260.3 %reduce-scatter.5.cloned.1.call-start = ((), (), s32[]{:S(2)}) async-start(), calls=%async_computation.4 | async-start | bytes 5734400 | tf_op jit(solution)/shard_map/reduce_scatter | solution.py:694
  379.8 34.2 %collective-permute-start.45 = (bf16[2,128,576]{2,1,0:T(8,128)(2,1)}, bf16[2,128,576]{2,1,0:T(8,128)(2,1)S(1)}, u32[]{:S(2)}, u32[]{:S(2)}) collective-permute-start(bf16[2,128,576]{2,1,0:T(8,128)(2,1)} %get-tuple-element.386), channel_id=1, source_target_pairs={{0,24},{8,0},{16,8},{24,16},{1,25},{9,1},{17,9},{25,17},{2,26},{10... | collective-permute-start | bytes 884744 | tf_op jit(solution)/shard_map/ppermute | solution.py:45
  409.2 259.8 %all-gather.5.cloned.1.call-start = ((), (), s32[]{:S(2)}) async-start(), calls=%async_computation.5 | async-start | bytes 5734400 | tf_op jit(solution)/shard_map/all_gather | solution.py:754
  435.6 33.7 %collective-permute-start.53 = (bf16[152,1792]{1,0:T(8,128)(2,1)}, bf16[152,1792]{1,0:T(8,128)(2,1)}, u32[]{:S(2)}, u32[]{:S(2)}) collective-permute-start(bf16[152,1792]{1,0:T(8,128)(2,1)} %reduce-scatter.3.cloned.1.call-done), channel_id=1, source_target_pairs={{0,8},{8,16},{16,24},{24,0},{1,9},{9,17},{17,25},{25,1},{2,10},{10... | collective-permute-start | bytes 1634312 | tf_op jit(solution)/shard_map/ppermute | solution.py:45
  459.0 53.2 %collective-permute-start.54 = (bf16[224,2304]{1,0:T(8,128)(2,1)}, bf16[224,2304]{1,0:T(8,128)(2,1)}, u32[]{:S(2)}, u32[]{:S(2)}) collective-permute-start(bf16[224,2304]{1,0:T(8,128)(2,1)} %get-tuple-element.414), channel_id=1, source_target_pairs={{0,2},{1,3},{2,0},{3,1},{4,6},{5,7},{6,4},{7,5},{8,10},{9,11},{10,... | collective-permute-start | bytes 3096584 | tf_op jit(solution)/shard_map/ppermute | solution.py:50
  460.3 51.9 %collective-permute-start.55 = (bf16[224,2304]{1,0:T(8,128)(2,1)}, bf16[224,2304]{1,0:T(8,128)(2,1)}, u32[]{:S(2)}, u32[]{:S(2)}) collective-permute-start(bf16[224,2304]{1,0:T(8,128)(2,1)} %get-tuple-element.415), channel_id=1, source_target_pairs={{0,4},{1,5},{2,6},{3,7},{4,0},{5,1},{6,2},{7,3},{8,12},{9,13},{10,... | collective-permute-start | bytes 3096584 | tf_op jit(solution)/shard_map/ppermute | solution.py:50
  465.7 46.5 %collective-permute-start.56 = (bf16[224,2304]{1,0:T(8,128)(2,1)}, bf16[224,2304]{1,0:T(8,128)(2,1)}, u32[]{:S(2)}, u32[]{:S(2)}) collective-permute-start(bf16[224,2304]{1,0:T(8,128)(2,1)} %get-tuple-element.416), channel_id=1, source_target_pairs={{0,6},{1,7},{2,4},{3,5},{4,2},{5,3},{6,0},{7,1},{8,14},{9,15},{10,... | collective-permute-start | bytes 3096584 | tf_op jit(solution)/shard_map/ppermute | solution.py:50
  527.6 57.4 %collective-permute-start.65 = (bf16[56,2304]{1,0:T(8,128)(2,1)S(1)}, bf16[56,2304]{1,0:T(8,128)(2,1)S(1)}, u32[]{:S(2)}, u32[]{:S(2)}) collective-permute-start(bf16[56,2304]{1,0:T(8,128)(2,1)S(1)} %get-tuple-element.509), channel_id=1, source_target_pairs={{0,16},{8,24},{16,0},{24,8},{1,17},{9,25},{17,1},{25,9},{2,18},{10... | collective-permute-start | bytes 774152 | tf_op jit(solution)/shard_map/ppermute | solution.py:45
  537.7 47.4 %collective-permute-start.64 = (bf16[56,2304]{1,0:T(8,128)(2,1)S(1)}, bf16[56,2304]{1,0:T(8,128)(2,1)S(1)}, u32[]{:S(2)}, u32[]{:S(2)}) collective-permute-start(bf16[56,2304]{1,0:T(8,128)(2,1)S(1)} %get-tuple-element.507), channel_id=1, source_target_pairs={{0,8},{8,16},{16,24},{24,0},{1,9},{9,17},{17,25},{25,1},{2,10},{10... | collective-permute-start | bytes 774152 | tf_op jit(solution)/shard_map/ppermute | solution.py:45
  537.8 48.4 %collective-permute-start.67 = (bf16[56,1792]{1,0:T(8,128)(2,1)S(1)}, bf16[56,1792]{1,0:T(8,128)(2,1)S(1)}, u32[]{:S(2)}, u32[]{:S(2)}) collective-permute-start(bf16[56,1792]{1,0:T(8,128)(2,1)S(1)} %add_convert_fusion.7), channel_id=1, source_target_pairs={{0,24},{8,0},{16,8},{24,16},{1,25},{9,1},{17,9},{25,17},{2,26},{10... | collective-permute-start | bytes 602120 | tf_op jit(solution)/shard_map/ppermute | solution.py:45
  541.7 74.1 %collective-permute-start.68 = (bf16[56,1792]{1,0:T(8,128)(2,1)S(1)}, bf16[56,1792]{1,0:T(8,128)(2,1)S(1)}, u32[]{:S(2)}, u32[]{:S(2)}) collective-permute-start(bf16[56,1792]{1,0:T(8,128)(2,1)S(1)} %add_convert_fusion.7), channel_id=1, source_target_pairs={{0,16},{8,24},{16,0},{24,8},{1,17},{9,25},{17,1},{25,9},{2,18},{10... | collective-permute-start | bytes 602120 | tf_op jit(solution)/shard_map/ppermute | solution.py:45
  542.5 73.3 %collective-permute-start.69 = (bf16[56,1792]{1,0:T(8,128)(2,1)S(1)}, bf16[56,1792]{1,0:T(8,128)(2,1)S(1)}, u32[]{:S(2)}, u32[]{:S(2)}) collective-permute-start(bf16[56,1792]{1,0:T(8,128)(2,1)S(1)} %add_convert_fusion.7), channel_id=1, source_target_pairs={{0,8},{8,16},{16,24},{24,0},{1,9},{9,17},{17,25},{25,1},{2,10},{10... | collective-permute-start | bytes 602120 | tf_op jit(solution)/shard_map/ppermute | solution.py:45
  620.2 41.3 %collective-permute-start.77 = (bf16[56,2304]{1,0:T(8,128)(2,1)S(1)}, bf16[56,2304]{1,0:T(8,128)(2,1)S(1)}, u32[]{:S(2)}, u32[]{:S(2)}) collective-permute-start(bf16[56,2304]{1,0:T(8,128)(2,1)S(1)} %fusion.25), channel_id=1, source_target_pairs={{0,16},{8,24},{16,0},{24,8},{1,17},{9,25},{17,1},{25,9},{2,18},{10... | collective-permute-start | bytes 774152 | tf_op jit(solution)/shard_map/ppermute | solution.py:45
  630.5 33.3 %collective-permute-start.72 = (bf16[256,1792]{1,0:T(8,128)(2,1)S(1)}, bf16[256,1792]{1,0:T(8,128)(2,1)S(1)}, u32[]{:S(2)}, u32[]{:S(2)}) collective-permute-start(bf16[256,1792]{1,0:T(8,128)(2,1)S(1)} %get-tuple-element.438), channel_id=1, source_target_pairs={{0,6},{1,7},{2,4},{3,5},{4,2},{5,3},{6,0},{7,1},{8,14},{9,15},{10,... | collective-permute-start | bytes 2752520 | tf_op jit(solution)/shard_map/ppermute | solution.py:50
  632.9 34.3 %collective-permute-start.71 = (bf16[256,1792]{1,0:T(8,128)(2,1)S(1)}, bf16[256,1792]{1,0:T(8,128)(2,1)S(1)}, u32[]{:S(2)}, u32[]{:S(2)}) collective-permute-start(bf16[256,1792]{1,0:T(8,128)(2,1)S(1)} %get-tuple-element.437), channel_id=1, source_target_pairs={{0,4},{1,5},{2,6},{3,7},{4,0},{5,1},{6,2},{7,3},{8,12},{9,13},{10,... | collective-permute-start | bytes 2752520 | tf_op jit(solution)/shard_map/ppermute | solution.py:50
  634.6 32.8 %collective-permute-start.70 = (bf16[256,1792]{1,0:T(8,128)(2,1)S(1)}, bf16[256,1792]{1,0:T(8,128)(2,1)S(1)}, u32[]{:S(2)}, u32[]{:S(2)}) collective-permute-start(bf16[256,1792]{1,0:T(8,128)(2,1)S(1)} %get-tuple-element.436), channel_id=1, source_target_pairs={{0,2},{1,3},{2,0},{3,1},{4,6},{5,7},{6,4},{7,5},{8,10},{9,11},{10,... | collective-permute-start | bytes 2752520 | tf_op jit(solution)/shard_map/ppermute | solution.py:50
  (188 other events, 2619.9 us)
Sparse Core Ops, SparseCore 0:
  62.3 72.5 all-gather.2
  258.0 43.1 reduce-scatter.2
  409.4 108.7 reduce-scatter.4
  532.7 135.6 all-gather.4
